TPU v7x, 32 devices: a whole 2x2x4 slice. The times are simulated.
32 devices in a mesh: req: 8 (over z, y), seq: 4 (over x, core).
Axes of the slice: x: 2, y: 2, z: 4, core: 2. Of those that a mesh axis runs over, the one named last changes fastest.
Arguments:
- tokens: bfloat16 [8, 2048, 2560], P('req', 'seq'), may hold values from -6 to 6
- mix_weight: bfloat16 [2560, 2816], P(('req', 'seq')), may hold values from -0.125 to 0.125
- step_weight: bfloat16 [2560, 40], P(('req', 'seq')), may hold values from -0.125 to 0.125
- conv_weight: float32 [4, 2816], replicated, may hold values from -3 to 3
- conv_bias: float32 [2816], replicated, may hold values from -3 to 3
- step_bias: float32 [40], replicated, may hold values from -5 to -3
- decay_rate: float32 [40], replicated, may hold values from 0.0009765625 to 1
- skip_gain: float32 [40], replicated, may hold values from 0.5 to 2
- norm_gain: float32 [2560], replicated, may hold values from 0.1 to 1.9
- prompt_len: int32 [8], replicated, may hold values from 512 to 2048, as said below
- prompt_start: int32 [8], replicated, may hold values from 0 to 1536, as said below
- deal: int32 [8], replicated, may hold values from 0 to 7, as said below
Outputs:
- result: bfloat16 [8, 2048, 2560], P('req', 'seq')
- final_state: float32 [8, 40, 64, 128], P('req', 'seq')
Inputs may be any that keep to these rules, and one draw needn't show every extreme that they name: `prompt_len`: one prompt has exactly 2048 positions and one exactly a quarter of 2048. prompt_start plus prompt_len is at most 2048 for every request. `deal`: a permutation of the requests; some slot s holds request (s + 4) modulo 8.
All inputs are finite; a program needn't handle non-finite values.
Results may differ from a plain program's by a relative error of at most 0.0035.
Values may be sent and summed in bfloat16 or wider, within the bound.
No kernel may reach another device: no remote copies, remote signals or barrier semaphores. Data moves between devices by JAX's collectives and lax.ppermute only.
A program may use at most 128 MiB of HBM per device.

v0:
```python
import jax
import jax.numpy as jnp
from jax import lax
from jax.sharding import PartitionSpec as P

GROUP = 256


EPS = 1e-05


def passed_along(block, axis, distance):
    devices = range(lax.axis_size(axis))
    route = [(i - distance, i) for i in devices if i - distance in devices]
    return lax.ppermute(block, axis, route)


def carried_in(part, axis, combine, identity):
    place = lax.axis_index(axis)
    gathered = jax.tree.map(lambda a: lax.all_gather(a, axis), part)
    state = jax.tree.map(lambda a, e: jnp.zeros_like(a) + jnp.asarray(e, a.dtype), part, identity)

    def one(step, state):
        return combine(
            state, jax.tree.map(lambda a: lax.dynamic_index_in_dim(a, step, 0, False), gathered)
        )

    return lax.fori_loop(0, place, one, state)


def broadcast(x, axis, root):
    mine = lax.axis_index(axis) == root
    return lax.psum(jnp.where(mine, x, jnp.zeros_like(x)), axis)


def on_device(
    tokens,
    mix_weight,
    step_weight,
    conv_weight,
    conv_bias,
    step_bias,
    decay_rate,
    skip_gain,
    norm_gain,
    prompt_len,
    prompt_start,
    deal,
):
    seq_count = lax.axis_size("seq")
    seq_index = lax.axis_index("seq")
    req_index = lax.axis_index("req")
    rows = tokens[0]
    span = rows.shape[0]
    total_reqs = deal.shape[0]
    slots = jnp.arange(total_reqs, dtype=jnp.int32)
    request = jnp.sum(jnp.where(slots == req_index, deal, 0))
    length = jnp.sum(jnp.where(slots == request, prompt_len, 0))
    start = jnp.sum(jnp.where(slots == request, prompt_start, 0))
    place = seq_index * span + jnp.arange(span, dtype=jnp.int32)
    valid = ((place >= start) & (place < start + length)).astype(jnp.float32)
    whole_mix, whole_step = (
        lax.all_gather(mix_weight, ("req", "seq"), axis=0, tiled=True),
        lax.all_gather(step_weight, ("req", "seq"), axis=0, tiled=True),
    )
    mixed = jnp.dot(rows, whole_mix, preferred_element_type=jnp.float32)
    raw_step = jnp.dot(rows, whole_step, preferred_element_type=jnp.float32)
    mixed = (mixed * valid[:, None]).astype(jnp.bfloat16)
    taps = conv_weight.shape[0]
    edge = passed_along(mixed[span - (taps - 1) :], "seq", 1)
    padded = jnp.concatenate([edge, mixed], axis=0)
    conv_sum = jnp.zeros(mixed.shape, jnp.float32) + conv_bias[None, :]
    for offset in range(taps):
        conv_sum = conv_sum + conv_weight[offset][None, :] * padded[offset : offset + span].astype(
            jnp.float32
        )
    convolved = jax.nn.silu(conv_sum).astype(jnp.bfloat16)
    heads = decay_rate.shape[0]
    inner = norm_gain.shape[0]
    head_dim = inner // heads
    nstate = (mixed.shape[1] - inner) // 2
    blocks = span // GROUP
    inputs = convolved[:, :inner].reshape(span, heads, head_dim)
    mixed_b = convolved[:, inner : inner + nstate]
    mixed_c = convolved[:, inner + nstate :]
    step_size = jax.nn.softplus(raw_step + step_bias[None, :]) * valid[:, None]
    pieces = (
        inputs.reshape(blocks, GROUP, heads, head_dim),
        mixed_b.reshape(blocks, GROUP, nstate),
        mixed_c.reshape(blocks, GROUP, nstate),
        step_size.reshape(blocks, GROUP, heads),
    )

    def local_group(block):
        part_in, part_b, part_c, part_step = block
        cum_decay = jnp.cumsum(-part_step * decay_rate[None, :], axis=0)
        places = jnp.arange(GROUP, dtype=jnp.int32)
        causal = places[:, None] >= places[None, :]
        spread = cum_decay[:, None, :] - cum_decay[None, :, :]
        spread = jnp.where(causal[:, :, None], spread, -1e30)
        scores = jnp.einsum("qn,kn->qk", part_c, part_b, preferred_element_type=jnp.float32)
        mixing = (jnp.exp(spread) * scores[:, :, None] * part_step[None, :, :]).astype(jnp.bfloat16)
        inner_out = jnp.einsum("qkh,khp->qhp", mixing, part_in, preferred_element_type=jnp.float32)
        to_end = jnp.exp(cum_decay[-1][None, :] - cum_decay) * part_step
        scaled = (to_end[:, :, None] * part_in.astype(jnp.float32)).astype(jnp.bfloat16)
        local = jnp.einsum("khp,kn->hpn", scaled, part_b, preferred_element_type=jnp.float32)
        return (inner_out, cum_decay, local)

    inner_out, cum_decay, group_state = lax.map(local_group, pieces)
    totals = cum_decay[:, -1, :]

    def advance(carry, item):
        group_total, group_local = item
        return (jnp.exp(group_total)[:, None, None] * carry + group_local, carry)

    dev_state, entry_zero = lax.scan(
        advance, jnp.zeros((heads, head_dim, nstate), jnp.float32), (totals, group_state)
    )
    before = jnp.cumsum(totals, axis=0) - totals
    dev_decay = jnp.exp(jnp.sum(totals, axis=0))

    def chain(earlier, later):
        return (earlier[0] * later[0], later[0][:, None, None] * earlier[1] + later[1])

    incoming_decay, incoming = carried_in(
        (dev_decay, dev_state), "seq", chain, (jnp.ones_like(dev_decay), jnp.zeros_like(dev_state))
    )
    entry = entry_zero + jnp.exp(before)[:, :, None, None] * incoming[None]
    carried = jnp.einsum(
        "cqn,chpn->cqhp", pieces[2].astype(jnp.float32), entry, precision=lax.Precision.HIGHEST
    )
    carried = carried * jnp.exp(cum_decay)[:, :, :, None]
    outputs = (inner_out + carried).reshape(span, heads, head_dim) + skip_gain[
        None, :, None
    ] * inputs.astype(jnp.float32)
    flat = outputs.reshape(span, inner)
    factor = lax.rsqrt(jnp.mean(flat * flat, axis=1, keepdims=True) + EPS)
    result = (flat * factor * norm_gain[None, :] * valid[:, None]).astype(jnp.bfloat16)[None]
    share = heads // seq_count
    leaving = dev_decay[:, None, None] * incoming + dev_state
    last_state = broadcast(leaving, "seq", seq_count - 1)
    own_state = lax.dynamic_slice_in_dim(last_state, seq_index * share, share, 0)[None]
    wanted = jnp.sum(jnp.where(deal == req_index, slots, 0))
    piece = lax.all_gather(own_state, "req", axis=0, tiled=True)
    count = piece.shape[0]
    chosen = jnp.arange(count, dtype=jnp.int32) == wanted
    final_state = jnp.zeros_like(own_state) + jnp.sum(
        jnp.where(chosen[:, None, None, None], piece, 0.0), axis=0, keepdims=True
    )
    return (result, final_state)


def solution(mesh):
    return jax.shard_map(
        on_device,
        mesh=mesh,
        in_specs=(
            P("req", "seq", None),
            P(("req", "seq"), None),
            P(("req", "seq"), None),
            P(),
            P(),
            P(),
            P(),
            P(),
            P(),
            P(),
            P(),
            P(),
        ),
        out_specs=(P("req", "seq", None), P("req", "seq", None, None)),
        check_vma=False,
    )
```

profile of v0, /device:TPU:0, one launch (start us, length us, event | category | flops | bytes accessed | tf_op | source)
XLA Modules:
  0.0 340.6 jit_solution(9646272335498083431)
XLA Ops:
  8.0 45.1 %all-gather.3 = bf16[32,80,40]{1,2,0:T(8,128)(2,1)S(1)} all-gather(bf16[1,80,40]{1,2,0:T(8,128)(2,1)} %bitcast.158), channel_id=1, replica_groups=mesh['req'=8,'seq'=4] {'req','seq'}, dimensions={0}, use_global_device_ids=true | all-gather | bytes 211200 | tf_op jit(solution)/shard_map/all_gather | solution.py:64
  55.0 1.9 fusion.51
  56.9 2.0 fusion.52
  62.4 56.1 %all-gather.8.cloned.1.call-done = bf16[2560,2816]{1,0:T(8,128)(2,1)} async-done(((bf16[80,2816]{1,0:T(8,128)(2,1)}), bf16[2560,2816]{1,0:T(8,128)(2,1)}) %all-gather.8.cloned.1.call-update) | async-done | bytes 14417936 | tf_op jit(solution)/shard_map/all_gather | solution.py:63
  118.6 11.5 %multiply_convert_fusion.6 = bf16[512,2816]{1,0:T(8,128)(2,1)S(1)} fusion(bf16[2560,2816]{1,0:T(8,128)(2,1)} %all-gather.8.cloned.1.call-done, f32[512]{0:T(512)S(1)} %fusion.50, bf16[1,512,2560]{2,1,0:T(8,128)(2,1)S(1)} %copy-done), kind=kOutput, calls=%fused_computation.48 | convolution fusion | flops 7384858624 | bytes 19924992 | tf_op jit(solution)/shard_map/dot_general | solution.py:66
  131.6 2.2 collective-permute-start
  134.6 7.9 %multiply_convert_fusion.5 = bf16[512,2816]{1,0:T(8,128)(2,1)S(1)} fusion(bf16[512,2816]{1,0:T(8,128)(2,1)} %copy-done.7, bf16[3,2816]{1,0:T(4,128)(2,1)S(1)} %collective-permute-done, f32[2816]{0:T(1024)S(1)} %get-tuple-element.187, f32[2816]{0:T(1024)S(1)} %get-tuple-element.188, f32[2816]{0:T(1024)S(1)} %get-tuple-element.186, ...), kind=kLoop, calls=%fused_computation.47 | loop fusion | flops 37486592 | bytes 5840384 | tf_op jit(solution)/shard_map/convert_element_type | solution.py:77
  145.8 7.5 %reshape.122 = bf16[2,256,40,64]{3,2,1,0:T(8,128)(2,1)} reshape(bf16[512,2560]{1,0:T(8,128)(2,1)} %slice.64) | data formatting | bytes 5242880 | tf_op jit(solution)/shard_map/reshape;reshape | solution.py:88
  153.4 6.4 %copy.43 = bf16[2,256,40,64]{1,3,2,0:T(8,128)(2,1)} copy(bf16[2,256,40,64]{3,2,1,0:T(8,128)(2,1)} %reshape.122) | data formatting | bytes 5242880 | tf_op jit(solution)/shard_map/while | solution.py:109
  161.6 17.0 %while.39 = (s32[]{:T(128)}, f32[2,256,40,64]{1,3,2,0:T(8,128)}, f32[2,256,40]{1,2,0:T(8,128)S(1)}, f32[2,40,64,128]{3,2,1,0:T(8,128)}, bf16[2,256,40,64]{1,3,2,...) while((s32[]{:T(128)}, f32[2,256,40,64]{1,3,2,0:T(8,128)}, ...), condition=%wide.region_6.7_spmd, body=%wide.region_3.6_spmd.sunk | while | flops 536604800 | bytes 18677688 | solution.py:109
  162.8 5.3 %bitcast_dynamic-update-slice_fusion.4 = f32[2,256,40,64]{1,3,2,0:T(8,128)} fusion(f32[2,256,40,64]{1,3,2,0:T(8,128)} %get-tuple-element.363, s32[]{:T(128)} %get-tuple-element.362, f32[256,40]{0,1:T(8,128)S(1)} %bitcast.156, f32[256,256]{1,0:T(8,128)S(1)} %fusion.74, f32[256,40]{0,1:T(8,128)S(1)} %bitcast_bitcast_fusion.3, ...), kind=kOutput, calls=%fused_computation.15.clone.1 | convolution fusion | flops 348651520 | bytes 4383744 | tf_op jit(solution)/shard_map/while/body/eval_jaxpr/qkh,khp->qhp/dot_general | solution.py:103
  171.3 5.3 %bitcast_dynamic-update-slice_fusion.4 = f32[2,256,40,64]{1,3,2,0:T(8,128)} fusion(f32[2,256,40,64]{1,3,2,0:T(8,128)} %get-tuple-element.363, s32[]{:T(128)} %get-tuple-element.362, f32[256,40]{0,1:T(8,128)S(1)} %bitcast.156, f32[256,256]{1,0:T(8,128)S(1)} %fusion.74, f32[256,40]{0,1:T(8,128)S(1)} %bitcast_bitcast_fusion.3, ...), kind=kOutput, calls=%fused_computation.15.clone.1 | convolution fusion | flops 348651520 | bytes 4383744 | tf_op jit(solution)/shard_map/while/body/eval_jaxpr/qkh,khp->qhp/dot_general | solution.py:103
  178.8 1.9 broadcast.58
  180.7 5.6 %while.41 = (s32[]{:T(128)}, f32[40,64,128]{2,1,0:T(8,128)S(1)}, f32[2,40,64,128]{3,2,1,0:T(8,128)}, f32[2,40]{1,0:T(2,128)S(1)}, f32[2,40,64,128]{3,2,1,0:T(8,128)}, /*index=5*/s32[]{:T(128)}, s32[]{:T(128)}) while((s32[]{:T(128)}, f32[40,64,128]{2,1,0:T(8,128)S(1)}, f32[2,40,64,128]{3,2,1,0:T(8,128)}, f32[2,40]{1,0:T(2,128)S(1)}, ...), condition=%wide.region_8.9_spmd.clone, body=%wide.region_7.8_spmd.clone.sunk | while | flops 1310723 | bytes 6554688 | solution.py:116
  188.8 6.9 %all-reduce = f32[160]{0:T(256)S(1)} all-reduce(f32[160]{0:T(256)S(1)} %get-tuple-element.232), channel_id=2, replica_groups=mesh['req'=8,'seq'=4] {'seq'}, use_global_device_ids=true, to_apply=%add | all-reduce | flops 160 | bytes 1280
  195.8 32.4 %all-gather.10.cloned.1.call-done = f32[160,64,128]{2,1,0:T(8,128)} async-done(((f32[40,64,128]{2,1,0:T(8,128)}), f32[160,64,128]{2,1,0:T(8,128)}) %all-gather.10.cloned.1.call-update) | async-done | bytes 5242896 | tf_op jit(solution)/shard_map/all_gather | solution.py:20
  231.0 42.8 %all-reduce.3.cloned.1.call-done = f32[40,64,128]{2,1,0:T(8,128)} async-done(((f32[40,64,128]{2,1,0:T(8,128)}), f32[40,64,128]{2,1,0:T(8,128)}) %all-reduce.3.cloned.1.call-update) | async-done | bytes 1310736 | tf_op jit(solution)/shard_map/psum | solution.py:33
  276.5 8.1 %multiply_add_fusion.1 = f32[2,256,40,64]{1,3,2,0:T(8,128)} fusion(f32[2,256,40,64]{1,3,2,0:T(8,128)} %get-tuple-element.123, f32[2,256,40]{1,2,0:T(8,128)S(1)} %exp.56, bf16[2,256,128,1]{2,1,3,0:T(8,128)(2,1)S(1)} %bitcast.154, f32[2,40,64,128]{3,2,1,0:T(8,128)} %get-tuple-element.126, f32[40,64,128]{2,1,0:T(8,128)S(1)} %get-tuple-element.128, ...), kind=kOutput, calls=%fused_computation.52 | convolution fusion | flops 2017198080 | bytes 14631232 | tf_op jit(solution)/shard_map/cqn,chpn->cqhp/dot_general | solution.py:129
  284.6 8.7 %copy.50 = f32[2,256,40,64]{3,2,1,0:T(8,128)} copy(f32[2,256,40,64]{1,3,2,0:T(8,128)} %multiply_add_fusion.1) | data formatting | bytes 10485760 | tf_op jit(solution)/shard_map/reshape | solution.py:133
  293.3 9.6 %reshape.123 = f32[512,2560]{1,0:T(8,128)} reshape(f32[2,256,40,64]{3,2,1,0:T(8,128)} %copy.50) | data formatting | bytes 10485760 | tf_op jit(solution)/shard_map/reshape | solution.py:133
  302.9 4.7 %multiply_reduce_fusion = f32[512]{0:T(512)S(1)} fusion(f32[512,2560]{1,0:T(8,128)} %reshape.123, f32[2560]{0:T(1024)S(1)} %mul.218, bf16[512,2816]{1,0:T(8,128)(2,1)} %copy-done.5), kind=kLoop, calls=%fused_computation.50 | loop fusion | flops 6553088 | bytes 7876608 | tf_op jit(solution)/shard_map/reduce_sum | solution.py:137
  308.0 4.6 %fusion.30 = bf16[1,512,2560]{2,1,0:T(8,128)(2,1)} fusion(f32[512,2560]{1,0:T(8,128)S(1)} %copy-done.4, f32[512]{0:T(512)S(1)} %fusion.50, f32[2560]{0:T(1024)S(1)} %copy-done.11, f32[512]{0:T(512)S(1)} %add_rsqrt_fusion, f32[2560]{0:T(1024)S(1)} %mul.218, bf16[512,2816]{1,0:T(8,128)(2,1)} %copy-done.5), kind=kLoop, calls=%fused_computation.58 | loop fusion | flops 9175040 | bytes 10510336 | tf_op jit(solution)/shard_map/broadcast_in_dim | solution.py:138
  312.7 18.5 %all-gather.12.cloned.1.call-done = f32[80,64,128]{2,1,0:T(8,128)} async-done(((f32[10,64,128]{2,1,0:T(8,128)}), f32[80,64,128]{2,1,0:T(8,128)}) %all-gather.12.cloned.1.call-update) | async-done | bytes 2621456 | tf_op jit(solution)/shard_map/all_gather | solution.py:144
  331.2 2.8 select_reduce_fusion
  (103 shorter events, 32.1 us)
Async XLA Ops:
  7.2 53.7 %copy-start = (bf16[1,512,2560]{2,1,0:T(8,128)(2,1)S(1)}, bf16[1,512,2560]{2,1,0:T(8,128)(2,1)}, u32[]{:S(2)}) copy-start(bf16[1,512,2560]{2,1,0:T(8,128)(2,1)} %param.18) | copy-start | bytes 7864324
  7.2 111.4 %all-gather.8.cloned.1.call-start = ((), (), s32[]{:S(2)}) async-start(), calls=%async_computation | async-start | bytes 14868480 | tf_op jit(solution)/shard_map/all_gather | solution.py:63
  7.9 220.3 %all-gather.10.cloned.1.call-start = ((), (), s32[]{:S(2)}) async-start(), calls=%async_computation.2 | async-start | bytes 6553600 | tf_op jit(solution)/shard_map/all_gather | solution.py:20
  62.4 71.4 %copy-start.8 = (f32[4,2816]{1,0:T(4,128)S(1)}, f32[4,2816]{1,0:T(4,128)}, u32[]{:S(2)}) copy-start(f32[4,2816]{1,0:T(4,128)} %param.21) | copy-start | bytes 135172
  62.4 72.2 %copy-start.10 = (f32[2816]{0:T(1024)S(1)}, f32[2816]{0:T(1024)}, u32[]{:S(2)}) copy-start(f32[2816]{0:T(1024)} %param.22) | copy-start | bytes 33796
  130.1 1.5 copy-start.7
  131.6 3.0 collective-permute-start
  142.5 1.6 copy-start.5
  153.4 8.2 %copy-start.9 = (f32[40]{0:T(128)S(1)}, f32[40]{0:T(128)}, u32[]{:S(2)}) copy-start(f32[40]{0:T(128)} %param.24) | copy-start | bytes 484
  162.8 5.6 %copy-start.6 = (bf16[2,256,40,64]{1,3,2,0:T(8,128)(2,1)S(1)}, bf16[2,256,40,64]{1,3,2,0:T(8,128)(2,1)}, u32[]{:S(2)}) copy-start(bf16[2,256,40,64]{1,3,2,0:T(8,128)(2,1)} %get-tuple-element.377) | copy-start | bytes 7864324 | tf_op jit(solution)/shard_map/while
  171.3 5.6 %copy-start.6 = (bf16[2,256,40,64]{1,3,2,0:T(8,128)(2,1)S(1)}, bf16[2,256,40,64]{1,3,2,0:T(8,128)(2,1)}, u32[]{:S(2)}) copy-start(bf16[2,256,40,64]{1,3,2,0:T(8,128)(2,1)} %get-tuple-element.377) | copy-start | bytes 7864324 | tf_op jit(solution)/shard_map/while
  180.7 6.7 %copy-start.13 = (u32[32]{0:T(128)S(1)}, u32[32]{0:T(128)}, u32[]{:S(2)}) copy-start(u32[32]{0:T(128)} %constant.93) | copy-start | bytes 388
  186.3 1.1 copy-start.2
  187.4 86.5 %all-reduce.3.cloned.1.call-start = ((), (), s32[]{:S(2)}) async-start(), calls=%async_computation.1 | async-start | bytes 2621440 | tf_op jit(solution)/shard_map/psum | solution.py:33
  228.4 1.3 copy-start.3
  229.7 45.9 %copy-start.12 = (f32[40]{0:T(128)S(1)}, f32[40]{0:T(128)}, u32[]{:S(2)}) copy-start(f32[40]{0:T(128)} %param.25) | copy-start | bytes 484
  231.0 100.2 %all-gather.12.cloned.1.call-start = ((), (), s32[]{:S(2)}) async-start(), calls=%async_computation.3 | async-start | bytes 2949120 | tf_op jit(solution)/shard_map/all_gather | solution.py:144
  302.9 5.1 %copy-start.4 = (f32[512,2560]{1,0:T(8,128)S(1)}, f32[512,2560]{1,0:T(8,128)}, u32[]{:S(2)}) copy-start(f32[512,2560]{1,0:T(8,128)} %reshape.123) | copy-start | bytes 15728644
  302.9 5.1 %copy-start.11 = (f32[2560]{0:T(1024)S(1)}, f32[2560]{0:T(1024)}, u32[]{:S(2)}) copy-start(f32[2560]{0:T(1024)} %param.26) | copy-start | bytes 30724
  308.0 26.0 %copy-start.1 = (bf16[1,512,2560]{2,1,0:T(8,128)(2,1)S(1)}, bf16[1,512,2560]{2,1,0:T(8,128)(2,1)}, u32[]{:S(2)}) copy-start(bf16[1,512,2560]{2,1,0:T(8,128)(2,1)} %param.18) | copy-start | bytes 7864324
Sparse Core Ops, SparseCore 0:
  10.8 107.6 all-gather.7
  187.5 40.6 all-gather.9
  231.2 42.6 all-reduce.2
  276.5 54.6 all-gather.11
where the time goes:
time: 342 us; the launch traced here: 341 us
  waiting for transfers between devices  151 us (44%)
  blocking collectives  52 us (15%)
  local copies, waits for them, and re-layouts  47.6 us (14%)
  other arithmetic  35.7 us (10%)
  matrix products  35.4 us (10%)
  between operations  15.9 us (5%)
    all_gather x1, waiting for transfers between devices, on_device(): lax.all_gather(mix_weight, ('req', 'seq'), axis=0, tiled=True)  56.1 us
    all_gather x1, blocking collectives, on_device(): lax.all_gather(step_weight, ('req', 'seq'), axis=0, tiled=True)  45.1 us
    psum x1, waiting for transfers between devices, broadcast(): return lax.psum(jnp.where(mine, x, jnp.zeros_like(x)), axis)  42.8 us
    all_gather x1, waiting for transfers between devices, carried_in(): gathered = jax.tree.map(lambda a: lax.all_gather(a, axis), part)  32.4 us
    all_gather x1, waiting for transfers between devices, on_device(): piece = lax.all_gather(own_state, 'req', axis=0, tiled=True)  18.5 us
    reshape x2, local copies, waits for them, and re-layouts, on_device(): (inner_out + carried).reshape(span, heads, head_dim)  18.3 us
    dot_general x1, matrix products, on_device(): mixed = jnp.dot(rows, whole_mix, preferred_element_type=jnp.float32)  11.5 us
    dot_general x2, matrix products, local_group(): jnp.einsum('qkh,khp->qhp', mixing, part_in, preferred_element_type=jnp.fl...  10.6 us
  transfers between devices with their start and end apart: 5, of which 5 were waited for; matrix products, arithmetic and copies ran while one was open for 13% of the time, Pallas kernels for 0%

commit v1 on v0

--- a/solution.py
+++ b/solution.py
@@ -1,12 +1,601 @@
+import functools
+
 import jax
 import jax.numpy as jnp
 from jax import lax
+from jax.experimental import pallas as pl
+from jax.experimental.pallas import tpu as pltpu
 from jax.sharding import PartitionSpec as P
 
 GROUP = 256
-
-
 EPS = 1e-05
+LOG2E = 1.4426950408889634
+LANES = 128
+HALO = 16
+F32 = jnp.float32
+BF16 = jnp.bfloat16
+AXES = ("req", "seq")
+
+
+def dot(a, b):
+    return jnp.dot(a, b, preferred_element_type=F32)
+
+
+def params(vmem_mib, side=False):
+    return pltpu.CompilerParams(
+        dimension_semantics=("arbitrary",), vmem_limit_bytes=vmem_mib * 1024 * 1024
+    )
+
+
+def valid_rows(first, rows, start, end):
+    place = first + lax.broadcasted_iota(jnp.int32, (rows, LANES), 0)
+    return jnp.where((place >= start) & (place < end), 1.0, 0.0).astype(F32)
+
+
+def place_weights(ints, low, high, whole, sems):
+    half = low.shape[0] // 160
+    copies = []
+    for p in range(2 * half):
+        source = low if p < half else high
+        row = pl.multiple_of(ints[8 + p] * 160, 160)
+        copies.append(
+            pltpu.make_async_copy(
+                source.at[pl.ds((p % half) * 160, 160), :],
+                whole.at[pl.ds(row, 160), :],
+                sems.at[p],
+            )
+        )
+    for copy in copies:
+        copy.start()
+    for copy in copies:
+        copy.wait()
+
+
+def fetch_tokens(ints, step, own, other, tokens):
+    mine = (step // 2) == ints[3]
+
+    @pl.when(mine)
+    def _():
+        tokens[...] = own[...]
+
+    @pl.when(jnp.logical_not(mine))
+    def _():
+        tokens[...] = other[...]
+
+
+def convolve(ints, step, acc_of, halo_of, spans, taps, padded):
+    start, end, first = ints[0], ints[1], ints[2]
+
+    @pl.when(step == 0)
+    def _():
+        edge = halo_of()
+        ok = valid_rows(first - HALO, HALO, start, end)
+        for at, lane in enumerate(spans):
+            rounded = (edge[:, lane * LANES : (lane + 1) * LANES] * ok).astype(BF16).astype(F32)
+            padded[at, 0:8, :] = rounded[HALO - 8 :, :]
+
+    acc = acc_of()
+    ok = valid_rows(first + step * GROUP, GROUP, start, end)
+    out = []
+    for at, lane in enumerate(spans):
+        rounded = (acc[:, lane * LANES : (lane + 1) * LANES] * ok).astype(BF16).astype(F32)
+        padded[at, 8 : 8 + GROUP, :] = rounded
+        total = taps[4:5, at * LANES : (at + 1) * LANES]
+        for k in range(4):
+            total = total + taps[k : k + 1, at * LANES : (at + 1) * LANES] * padded[
+                at, 5 + k : 5 + k + GROUP, :
+            ]
+        half = 0.5 * total
+        out.append((half + half * jnp.tanh(half)).astype(BF16))
+        padded[at, 0:8, :] = padded[at, GROUP : GROUP + 8, :]
+    return acc, ok, out
+
+
+def first_kernel(
+    ints, own, other, halo, low, high, taps, rates,
+    bc_out, x_out, cq_out, kq_out, kt_out, ca_out, tot_out,
+    whole, tokens, padded, before, sems,
+):
+    step = pl.program_id(0)
+
+    @pl.when(step == 0)
+    def _():
+        place_weights(ints, low, high, whole, sems)
+        before[...] = jnp.zeros_like(before)
+
+    fetch_tokens(ints, step, own, other, tokens)
+    acc, ok, out = convolve(
+        ints,
+        step,
+        lambda: dot(tokens[...], whole[...]),
+        lambda: dot(halo[...], whole[...]),
+        (0, 2, 3),
+        taps,
+        padded,
+    )
+    bc_out[...] = out[0]
+    x_out[:, 0:LANES] = out[1]
+    x_out[:, LANES : 2 * LANES] = out[2]
+    raw = acc[:, LANES : 2 * LANES] + rates[0:1, :]
+    size = (jnp.maximum(raw, 0.0) + jnp.log1p(jnp.exp(-jnp.abs(raw)))) * ok
+    decay = size * rates[1:2, :]
+    high_part = decay.astype(BF16)
+    rest = decay - high_part.astype(F32)
+    mid_part = rest.astype(BF16)
+    low_part = (rest - mid_part.astype(F32)).astype(BF16)
+    row = lax.broadcasted_iota(jnp.int32, (GROUP, GROUP), 0)
+    col = lax.broadcasted_iota(jnp.int32, (GROUP, GROUP), 1)
+    below = jnp.where(row >= col, 1.0, 0.0).astype(BF16)
+    cum = dot(below, high_part) + dot(below, mid_part) + dot(below, low_part)
+    from_key = jnp.log2(size) - cum
+    cq_out[...] = cum
+    kq_out[...] = from_key
+    kt_out[0] = from_key.T[0:32, :]
+    ca_out[...] = cum + before[0:1, :]
+    before[...] = before[...] + jnp.broadcast_to(cum[GROUP - 1 : GROUP, :], before.shape)
+    tot_out[...] = before[...]
+
+
+def column(a, head):
+    return jnp.broadcast_to(a[:, head : head + 1], (a.shape[0], LANES))
+
+
+def split(a):
+    upper = a.astype(BF16)
+    return upper, (a - upper.astype(F32)).astype(BF16)
+
+
+def scan_kernel(
+    heads, extra, ints, own, other, halo, low, high, taps, x_ref, b_ref, c_ref, cq_ref, kq_ref,
+    kt_ref, tot_ref, skip_ref, y_out, s_out, whole, tokens, padded, state, sems,
+):
+    step = pl.program_id(0)
+    pairs = len(heads)
+
+    @pl.when(step == 0)
+    def _():
+        place_weights(ints, low, high, whole, sems)
+        state[...] = jnp.zeros_like(state)
+
+    fetch_tokens(ints, step, own, other, tokens)
+    _, _, out = convolve(
+        ints,
+        step,
+        lambda: dot(tokens[...], whole[...]),
+        lambda: dot(halo[...], whole[...]),
+        tuple(range(pairs - extra)),
+        taps,
+        padded,
+    )
+    xs = [x_ref[:, i * LANES : (i + 1) * LANES] for i in range(extra)] + out
+    b, c = b_ref[...], c_ref[...]
+    scores = lax.dot_general(c, b, (((1,), (1,)), ((), ())), preferred_element_type=F32)
+    half = GROUP // 2
+    row = lax.broadcasted_iota(jnp.int32, (half, half), 0)
+    col = lax.broadcasted_iota(jnp.int32, (half, half), 1)
+    causal = row >= col
+    left = lax.broadcasted_iota(jnp.int32, (GROUP, LANES), 1) < LANES // 2
+    cq, kq, kt = cq_ref[...], kq_ref[...], kt_ref[0]
+    upper, lower = split(state[...])
+    carried = dot(jnp.concatenate([c, c], axis=1), jnp.concatenate([upper, lower], axis=0))
+    zero = jnp.zeros((GROUP, LANES), BF16)
+    scaled, ends = [], []
+    for i, head in enumerate(heads):
+        x = xs[i]
+        top, bottom, spread = [], [], []
+        for h in (head, head + 1):
+            q = column(cq, h)
+            spread.append(q)
+            k0 = jnp.broadcast_to(kt[h : h + 1, 0:half], (half, half))
+            k1 = jnp.broadcast_to(kt[h : h + 1, half:], (half, half))
+            m00 = jnp.where(causal, jnp.exp2(q[0:half] + k0) * scores[0:half, 0:half], 0.0)
+            m10 = jnp.exp2(q[half:] + k0) * scores[half:, 0:half]
+            m11 = jnp.where(causal, jnp.exp2(q[half:] + k1) * scores[half:, half:], 0.0)
+            top.append(m00.astype(BF16))
+            bottom.append(m10.astype(BF16))
+            bottom.append(m11.astype(BF16))
+        x0, x1 = jnp.where(left, x, zero), jnp.where(left, zero, x)
+        y_top = dot(jnp.concatenate(top, axis=1), jnp.concatenate([x0[0:half], x1[0:half]], axis=0))
+        y_bottom = dot(jnp.concatenate(bottom, axis=1), jnp.concatenate([x0, x1], axis=0))
+        q = jnp.where(left, spread[0], spread[1])
+        lanes = slice(i * LANES, (i + 1) * LANES)
+        xf = x.astype(F32)
+        rest = jnp.exp2(q) * carried[:, lanes] + skip_ref[0:1, lanes] * xf
+        y_out[0:half, lanes] = y_top + rest[0:half]
+        y_out[half:, lanes] = y_bottom + rest[half:]
+        k = jnp.where(left, column(kq, head), column(kq, head + 1))
+        end = q[GROUP - 1 : GROUP, :]
+        scaled.append((jnp.exp2(k + end) * xf).astype(BF16))
+        ends.append(jnp.exp2(end))
+    local = lax.dot_general(
+        b, jnp.concatenate(scaled, axis=1), (((0,), (0,)), ((), ())), preferred_element_type=F32
+    )
+    new = jnp.concatenate(ends, axis=1) * state[...] + local
+    state[...] = new
+
+    @pl.when(step == pl.num_programs(0) - 1)
+    def _():
+        s_out[0:LANES, :] = new
+        whole_row = lax.broadcasted_iota(jnp.int32, (8, LANES), 1) < LANES // 2
+        for i, head in enumerate(heads):
+            t = tot_ref[...]
+            s_out[LANES : LANES + 8, i * LANES : (i + 1) * LANES] = jnp.where(
+                whole_row, column(t, head), column(t, head + 1)
+            )
+
+
+def join_kernel(heads, halves, ints, y_ref, c_ref, ca_ref, s_ref, r_ref, send_out, keep_out, fin_out):
+    step = pl.program_id(0)
+    later = ints[4] > 0
+    left = lax.broadcasted_iota(jnp.int32, (GROUP, LANES), 1) < LANES // 2
+    c, ca = c_ref[...], ca_ref[...]
+    entering = r_ref[0:LANES, :] * jnp.where(later, 1.0, 0.0)
+    upper, lower = split(entering)
+    carried = dot(jnp.concatenate([c, c], axis=1), jnp.concatenate([upper, lower], axis=0))
+    ys = []
+    for i, head in enumerate(heads):
+        lanes = slice(i * LANES, (i + 1) * LANES)
+        q = jnp.where(left, column(ca, head), column(ca, head + 1))
+        ys.append(y_ref[:, lanes] + jnp.exp2(q) * carried[:, lanes])
+
+    @pl.when(step < 2)
+    def _():
+        for i in range(len(heads)):
+            send_out[:, i * LANES : (i + 1) * LANES] = ys[i]
+
+    @pl.when(step >= 2)
+    def _():
+        for i in range(len(heads)):
+            keep_out[:, i * LANES : (i + 1) * LANES] = ys[i]
+
+    @pl.when(step == 0)
+    def _():
+        for i, (early, late) in enumerate(halves):
+            a = slice(early * LANES, (early + 1) * LANES)
+            b = slice(late * LANES, (late + 1) * LANES)
+            at_first = jnp.exp2(r_ref[LANES : LANES + 1, a]) * s_ref[0:LANES, a] + r_ref[0:LANES, a]
+            at_last = jnp.exp2(s_ref[LANES : LANES + 1, b]) * r_ref[0:LANES, b] + s_ref[0:LANES, b]
+            both = jnp.where(later, at_last, at_first)
+            fin_out[i * LANES : (i + 1) * LANES, :] = both.T.astype(fin_out.dtype)
+
+
+def norm_kernel(places, ints, gain_ref, ka_ref, kb_ref, ra_ref, rb_ref, out_ref):
+    step = pl.program_id(0)
+    core = ints[3]
+    rows = out_ref.shape[0]
+    first = ints[2] + core * (2 * GROUP) + step * rows
+    ok = valid_rows(first, rows, ints[0], ints[1])
+    blocks = []
+    for who, refs in ((core, (ka_ref, kb_ref)), (1 - core, (ra_ref, rb_ref))):
+        for ref, wheres in zip(refs, places, strict=True):
+            for i, where in enumerate(wheres):
+                at = pl.multiple_of((where + 5 * who) * LANES, LANES)
+                blocks.append((at, ref, i))
+    total = jnp.zeros((rows, LANES), F32)
+    for _, ref, i in blocks:
+        v = ref[:, i * LANES : (i + 1) * LANES]
+        total = total + v * v
+    mean = jnp.sum(total, axis=1, keepdims=True) * (1.0 / out_ref.shape[1])
+    factor = lax.rsqrt(mean + EPS) * ok
+    for at, ref, i in blocks:
+        v = ref[:, i * LANES : (i + 1) * LANES]
+        out_ref[:, pl.ds(at, LANES)] = (v * factor * gain_ref[0:1, pl.ds(at, LANES)]).astype(BF16)
+
+
+def swapped(x, masks):
+    count = lax.axis_size("req") * lax.axis_size("seq")
+    return lax.ppermute(x, AXES, [(i, i ^ masks[i % 2]) for i in range(count)])
+
+
+def spec(shape, index):
+    return pl.BlockSpec(shape, index)
+
+
+def fixed(shape):
+    return pl.BlockSpec(shape, lambda i, ints: (0,) * len(shape))
+
+
+def by_step(shape):
+    return pl.BlockSpec(shape, lambda i, ints: (i,) + (0,) * (len(shape) - 1))
+
+
+ANY = pl.BlockSpec(memory_space=pl.ANY)
+
+
+def on_device(
+    tokens, mix_weight, step_weight, conv_weight, conv_bias, step_bias, decay_rate, skip_gain,
+    norm_gain, prompt_len, prompt_start, deal,
+):
+    seq_index = lax.axis_index("seq")
+    req_index = lax.axis_index("req")
+    core, along = seq_index % 2, seq_index // 2
+    rows = tokens[0]
+    span, depth = rows.shape
+    inner = norm_gain.shape[0]
+    heads = decay_rate.shape[0]
+    head_dim = inner // heads
+    nstate = (mix_weight.shape[1] - inner) // 2
+    share = heads // 4
+    quarter = inner // 4
+    slots = jnp.arange(deal.shape[0], dtype=jnp.int32)
+    request = jnp.sum(jnp.where(slots == req_index, deal, 0))
+    length = jnp.sum(jnp.where(slots == request, prompt_len, 0))
+    start = jnp.sum(jnp.where(slots == request, prompt_start, 0))
+    chip = req_index * 2 + along
+
+    def mine_of(a, b, who):
+        bc = lax.dynamic_slice_in_dim(a, inner + nstate * who, nstate, 1)
+        early = lax.dynamic_slice_in_dim(a, quarter * who, quarter, 1)
+        late = lax.dynamic_slice_in_dim(a, 2 * quarter + quarter * who, quarter, 1)
+        parts = [bc]
+        if b is not None:
+            parts += [steps_of(b, who)]
+        for lo, hi in ((0, 1), (1, 3), (3, 5)):
+            parts += [early[:, lo * LANES : hi * LANES], late[:, lo * LANES : hi * LANES]]
+        return jnp.concatenate(parts, axis=1)
+
+    def steps_of(b, who):
+        one = lax.dynamic_slice_in_dim(b, share * who, share, 1)
+        two = lax.dynamic_slice_in_dim(b, 2 * share + share * who, share, 1)
+        return jnp.concatenate(
+            [one, two, jnp.zeros((b.shape[0], LANES - 2 * share), b.dtype)], axis=1
+        )
+
+    kept = mine_of(mix_weight, step_weight, core)
+    given = mine_of(mix_weight, step_weight, 1 - core)
+    got = swapped(given, (1, 1))
+    weights = jnp.where(
+        core == 0, jnp.concatenate([kept, got], axis=0), jnp.concatenate([got, kept], axis=0)
+    )
+    other = swapped(rows, (1, 1))
+    last_rows = jnp.where(core == 1, rows[span - HALO :], other[span - HALO :])
+    count = lax.axis_size("req") * lax.axis_size("seq")
+    halo = lax.ppermute(
+        last_rows, AXES, [(i, i + 2) for i in range(count) if (i // 2) % 2 == 0]
+    )
+
+    masks = ((16, 16), (8, 8), (2, 4), (4, 2))
+    order = []
+    for p in range(16):
+        rel = [0, 0]
+        for s, mask in enumerate(masks):
+            if (p >> s) & 1:
+                rel = [rel[0] ^ (mask[0] // 2), rel[1] ^ (mask[1] // 2)]
+        order.append(jnp.bitwise_xor(chip, jnp.where(core == 0, rel[0], rel[1])))
+
+    def gathered(block):
+        for mask in masks[:-1]:
+            block = jnp.concatenate([block, swapped(block, mask)], axis=0)
+        return block, swapped(block, masks[-1])
+
+    width = weights.shape[1] // 3
+    chunks = [gathered(weights[:, i * width : (i + 1) * width]) for i in range(3)]
+
+    taps = mine_of(
+        jnp.concatenate([conv_weight, conv_bias[None], jnp.zeros_like(conv_weight[:3])], axis=0),
+        None,
+        core,
+    )
+    rates = jnp.concatenate(
+        [
+            steps_of(step_bias[None], core),
+            steps_of(decay_rate[None] * (-LOG2E), core),
+            jnp.zeros((6, LANES), F32),
+        ],
+        axis=0,
+    )
+    skip_all = mine_of(
+        jnp.concatenate([jnp.repeat(skip_gain, head_dim), jnp.zeros((2 * nstate,), F32)])[None],
+        None,
+        core,
+    )
+    skip = jnp.broadcast_to(skip_all[:, LANES:], (8, inner // 2))
+    ints = jnp.stack(
+        [start, start + length, along * 2 * span, core, along]
+        + [jnp.zeros_like(core)] * 3
+        + order
+    ).astype(jnp.int32)
+
+    chip_rows = 2 * span
+    steps = chip_rows // GROUP
+    per = span // GROUP
+
+    def clamp(v):
+        return jnp.clip(v, 0, per - 1)
+
+    own_spec = pl.BlockSpec((GROUP, depth), lambda i, ints: (clamp(i - per * ints[3]), 0))
+    other_spec = pl.BlockSpec(
+        (GROUP, depth), lambda i, ints: (clamp(i - per * (1 - ints[3])), 0)
+    )
+    halo_spec = fixed((HALO, depth))
+
+    def scratch(spans):
+        return [
+            pltpu.VMEM((depth, width), BF16),
+            pltpu.VMEM((GROUP, depth), BF16),
+            pltpu.VMEM((spans, GROUP + 8, LANES), F32),
+        ]
+
+    bc, x0, cq, kq, kt, ca, tot = pl.pallas_call(
+        first_kernel,
+        grid_spec=pltpu.PrefetchScalarGridSpec(
+            num_scalar_prefetch=1,
+            grid=(steps,),
+            in_specs=[
+                own_spec, other_spec, halo_spec, ANY, ANY, fixed((8, 3 * LANES)), fixed((8, LANES)),
+            ],
+            out_specs=[
+                by_step((GROUP, LANES)),
+                by_step((GROUP, 2 * LANES)),
+                by_step((GROUP, LANES)),
+                by_step((GROUP, LANES)),
+                by_step((1, 32, GROUP)),
+                by_step((GROUP, LANES)),
+                fixed((8, LANES)),
+            ],
+            scratch_shapes=scratch(3)
+            + [pltpu.VMEM((8, LANES), F32), pltpu.SemaphoreType.DMA((16,))],
+        ),
+        out_shape=[
+            jax.ShapeDtypeStruct((chip_rows, LANES), BF16),
+            jax.ShapeDtypeStruct((chip_rows, 2 * LANES), BF16),
+            jax.ShapeDtypeStruct((chip_rows, LANES), F32),
+            jax.ShapeDtypeStruct((chip_rows, LANES), F32),
+            jax.ShapeDtypeStruct((steps, 32, GROUP), F32),
+            jax.ShapeDtypeStruct((chip_rows, LANES), F32),
+            jax.ShapeDtypeStruct((8, LANES), F32),
+        ],
+        compiler_params=params(40),
+        cost_estimate=pl.CostEstimate(
+            flops=2 * chip_rows * depth * width, bytes_accessed=9000000, transcendentals=500000
+        ),
+        name="first",
+    )(ints, rows, other, halo, *chunks[0], taps[:, : 3 * LANES], rates)
+
+    bc_other = swapped(bc, (1, 1))
+    b = jnp.where(core == 0, bc, bc_other)
+    c = jnp.where(core == 0, bc_other, bc)
+
+    def pair_heads(lo, hi):
+        return [2 * i for i in range(lo, hi)] + [share + 2 * i for i in range(lo, hi)]
+
+    batches = (
+        (pair_heads(0, 1) + pair_heads(1, 3), 2, ((0, 1), (2, 4), (3, 5)), 3 * LANES, 0),
+        (pair_heads(3, 5), 0, ((0, 2), (1, 3)), 7 * LANES, 6 * LANES),
+    )
+
+    def scanned(batch, chunk):
+        firsts, extra, _, tap_at, skip_at = batch
+        pairs = len(firsts)
+        new = pairs - extra
+        return pl.pallas_call(
+            functools.partial(scan_kernel, firsts, extra),
+            grid_spec=pltpu.PrefetchScalarGridSpec(
+                num_scalar_prefetch=1,
+                grid=(steps,),
+                in_specs=[
+                    own_spec, other_spec, halo_spec, ANY, ANY, fixed((8, new * LANES)),
+                    by_step((GROUP, 2 * LANES)), by_step((GROUP, LANES)), by_step((GROUP, LANES)),
+                    by_step((GROUP, LANES)), by_step((GROUP, LANES)), by_step((1, 32, GROUP)),
+                    fixed((8, LANES)), fixed((8, pairs * LANES)),
+                ],
+                out_specs=[
+                    by_step((GROUP, pairs * LANES)),
+                    fixed((LANES + 8, pairs * LANES)),
+                ],
+                scratch_shapes=scratch(new)
+                + [pltpu.VMEM((LANES, pairs * LANES), F32), pltpu.SemaphoreType.DMA((16,))],
+            ),
+            out_shape=[
+                jax.ShapeDtypeStruct((chip_rows, pairs * LANES), F32),
+                jax.ShapeDtypeStruct((LANES + 8, pairs * LANES), F32),
+            ],
+            compiler_params=params(48),
+            cost_estimate=pl.CostEstimate(
+                flops=2 * chip_rows * depth * width + pairs * 600000000,
+                bytes_accessed=12000000,
+                transcendentals=pairs * 400000,
+            ),
+            name="scan",
+        )(
+            ints, rows, other, halo, *chunk, taps[:, tap_at : tap_at + new * LANES],
+            x0, b, c, cq, kq, kt, tot, skip[:, skip_at : skip_at + pairs * LANES],
+        )
+
+    def turned(i, ints):
+        return (i + 2 * (1 - ints[3])) % 4, 0
+
+    def joined(batch, y, s, r):
+        firsts, _, halves, _, _ = batch
+        pairs = len(firsts)
+        half_rows = chip_rows // 2
+        return pl.pallas_call(
+            functools.partial(join_kernel, firsts, halves),
+            grid_spec=pltpu.PrefetchScalarGridSpec(
+                num_scalar_prefetch=1,
+                grid=(steps,),
+                in_specs=[
+                    pl.BlockSpec((GROUP, pairs * LANES), turned),
+                    pl.BlockSpec((GROUP, LANES), turned),
+                    pl.BlockSpec((GROUP, LANES), turned),
+                    fixed((LANES + 8, pairs * LANES)),
+                    fixed((LANES + 8, pairs * LANES)),
+                ],
+                out_specs=[
+                    pl.BlockSpec((GROUP, pairs * LANES), lambda i, ints: (jnp.minimum(i, 1), 0)),
+                    pl.BlockSpec((GROUP, pairs * LANES), lambda i, ints: (jnp.maximum(i - 2, 0), 0)),
+                    fixed((len(halves) * LANES, nstate)),
+                ],
+            ),
+            out_shape=[
+                jax.ShapeDtypeStruct((half_rows, pairs * LANES), F32),
+                jax.ShapeDtypeStruct((half_rows, pairs * LANES), F32),
+                jax.ShapeDtypeStruct((len(halves) * LANES, nstate), BF16),
+            ],
+            compiler_params=params(32),
+            cost_estimate=pl.CostEstimate(
+                flops=4 * chip_rows * LANES * pairs * LANES,
+                bytes_accessed=chip_rows * pairs * LANES * 8,
+                transcendentals=chip_rows * pairs * LANES,
+            ),
+            name="join",
+        )(ints, y, c, ca, s, r)
+
+    wanted = jnp.sum(jnp.where(deal == req_index, slots, 0))
+    partner_wanted = jnp.sum(jnp.where(deal == (req_index ^ 1), slots, 0))
+
+    def delivered(block):
+        one = swapped(block, (16, 16))
+        pair = jnp.stack([block, one])
+        two = swapped(pair, (8, 8))
+        cand = jnp.concatenate([pair, two], axis=0)
+
+        def pick(row):
+            rel = row ^ req_index
+            at = (rel >> 2) + 2 * ((rel >> 1) & 1)
+            return lax.dynamic_index_in_dim(cand, at, 0, False), rel & 1
+
+        sent, _ = pick(partner_wanted)
+        three = swapped(sent, (4, 4))
+        here, odd = pick(wanted)
+        return jnp.where(odd == 1, three, here).astype(F32)
+
+    kept_y, got_y, finals = [], [], []
+    for batch, chunk in zip(batches, chunks[1:], strict=True):
+        y, s = scanned(batch, chunk)
+        r = swapped(s, (2, 2))
+        send, keep, fin = joined(batch, y, s, r)
+        got_y.append(swapped(send, (1, 1)))
+        kept_y.append(keep)
+        finals.append(delivered(fin))
+
+    final_state = jnp.concatenate(finals, axis=0).reshape(1, share, head_dim, nstate)
+    places = (
+        [0, 10, 1, 2, 11, 12],
+        [3, 4, 13, 14],
+    )
+    result = pl.pallas_call(
+        functools.partial(norm_kernel, places),
+        grid_spec=pltpu.PrefetchScalarGridSpec(
+            num_scalar_prefetch=1,
+            grid=(span // GROUP,),
+            in_specs=[
+                fixed((1, inner)),
+                by_step((GROUP, 6 * LANES)),
+                by_step((GROUP, 4 * LANES)),
+                by_step((GROUP, 6 * LANES)),
+                by_step((GROUP, 4 * LANES)),
+            ],
+            out_specs=by_step((GROUP, inner)),
+        ),
+        out_shape=jax.ShapeDtypeStruct((span, inner), BF16),
+        compiler_params=params(32),
+        cost_estimate=pl.CostEstimate(
+            flops=6 * span * inner, bytes_accessed=6 * span * inner, transcendentals=span
+        ),
+        name="norm",
+    )(ints, norm_gain[None], *kept_y, *got_y)
+    return (result[None], final_state)
 
 
 def passed_along(block, axis, distance):
@@ -33,7 +622,7 @@
     return lax.psum(jnp.where(mine, x, jnp.zeros_like(x)), axis)
 
 
-def on_device(
+def on_device_general(
     tokens,
     mix_weight,
     step_weight,
@@ -151,23 +740,16 @@
 
 
 def solution(mesh):
+    fits = mesh.shape["req"] == 8 and mesh.shape["seq"] == 4
     return jax.shard_map(
-        on_device,
+        on_device if fits else on_device_general,
         mesh=mesh,
         in_specs=(
             P("req", "seq", None),
             P(("req", "seq"), None),
             P(("req", "seq"), None),
-            P(),
-            P(),
-            P(),
-            P(),
-            P(),
-            P(),
-            P(),
-            P(),
-            P(),
-        ),
+        )
+        + (P(),) * 9,
         out_specs=(P("req", "seq", None), P("req", "seq", None, None)),
         check_vma=False,
     )

time: 342 us -> 176 us (0.51)
  waiting for transfers between devices: 151 us -> 55 us
  Pallas kernels: 0 us -> 52.5 us
  blocking collectives: 52 us -> 0 us
  starting transfers between devices: 2.32 us -> 49 us
  local copies, waits for them, and re-layouts: 47.6 us -> 6.67 us
  matrix products: 35.4 us -> 0 us
  other arithmetic: 35.7 us -> 8.55 us
  between operations: 15.9 us -> 3.63 us
    all_gather x3 -> x0, waiting for transfers between devices: 107 us -> none  [the longest x1 56.1 us: on_device(): lax.all_gather(mix_weight, ('req', 'seq'), axis=0, tiled=True)]
    ppermute x1 -> x26, waiting for transfers between devices: 0.6 us -> 55 us  [the longest x25 55 us: swapped(): return lax.ppermute(x, AXES, [(i, i ^ masks[i % 2]) for i in range(count)])]
    pallas_call x0 -> x6, Pallas kernels: none -> 52.5 us  [the longest x2 30.6 us: scanned(): pl.pallas_call(functools.partial(scan_kernel, firsts, extra), grid_spec=p...]
    ppermute x1 -> x26, starting transfers between devices: 2.16 us -> 49 us  [the longest x25 44.5 us: swapped(): return lax.ppermute(x, AXES, [(i, i ^ masks[i % 2]) for i in range(count)])]
    all_gather x1 -> x0, blocking collectives: 45.1 us -> none  [on_device(): lax.all_gather(step_weight, ('req', 'seq'), axis=0, tiled=True)]
    psum x1 -> x0, waiting for transfers between devices: 42.8 us -> none  [broadcast(): return lax.psum(jnp.where(mine, x, jnp.zeros_like(x)), axis)]
    dot_general x9 -> x0, matrix products: 35.4 us -> none  [the longest x1 11.5 us: on_device(): mixed = jnp.dot(rows, whole_mix, preferred_element_type=jnp.float32)]
    reshape x3 -> x1, local copies, waits for them, and re-layouts: 18.4 us -> 0.07 us  [on_device(): jnp.repeat(skip_gain, head_dim)]
  transfers between devices with their start and end apart: 5 -> 26, of which waited for: 5 -> 14; matrix products, arithmetic and copies ran while one was open for 13% -> 6% of each run, Pallas kernels for 0% -> 28%
where the time goes in v1:
time: 176 us; the launch traced here: 175 us
  waiting for transfers between devices  55 us (31%)
  Pallas kernels  52.5 us (30%)
  starting transfers between devices  49 us (28%)
  other arithmetic  8.55 us (5%)
  local copies, waits for them, and re-layouts  6.67 us (4%)
  between operations  3.63 us (2%)
    ppermute x25, waiting for transfers between devices, swapped(): return lax.ppermute(x, AXES, [(i, i ^ masks[i % 2]) for i in range(count)])  55 us
    ppermute x25, starting transfers between devices, swapped(): return lax.ppermute(x, AXES, [(i, i ^ masks[i % 2]) for i in range(count)])  44.5 us
    pallas_call x2, Pallas kernels, scanned(): pl.pallas_call(functools.partial(scan_kernel, firsts, extra), grid_spec=p...  30.6 us
    pallas_call x1, Pallas kernels, on_device(): pl.pallas_call(first_kernel, grid_spec=pltpu.PrefetchScalarGridSpec(num_s...  12.3 us
    pallas_call x2, Pallas kernels, joined(): pl.pallas_call(functools.partial(join_kernel, firsts, halves), grid_spec=...  6.72 us
    ppermute x1, starting transfers between devices, on_device(): lax.ppermute(last_rows, AXES, [(i, i + 2) for i in range(count) if i // 2...  4.47 us
  transfers between devices with their start and end apart: 26, of which 14 were waited for; matrix products, arithmetic and copies ran while one was open for 6% of the time, Pallas kernels for 28%

profile of v1, /device:TPU:0, one launch (start us, length us, event | category | flops | bytes accessed | tf_op | source)
XLA Modules:
  0.0 175.3 jit_solution(17320907382740429313)
XLA Ops:
  5.5 4.0 %collective-permute-start.7 = (bf16[160,512]{1,0:T(8,128)(2,1)S(1)}, bf16[160,512]{1,0:T(8,128)(2,1)S(1)}, u32[]{:S(2)}, u32[]{:S(2)}) collective-permute-start(bf16[160,512]{1,0:T(8,128)(2,1)S(1)} %get-tuple-element.42), channel_id=1, source_target_pairs={{0,16},{1,17},{2,18},{3,19},{4,20},{5,21},{6,22},{7,23},{8,24},{9,... | collective-permute-start | bytes 491528 | tf_op jit(solution)/shard_map/ppermute | solution.py:287
  9.6 11.9 %collective-permute-done.7 = bf16[160,512]{1,0:T(8,128)(2,1)S(1)} collective-permute-done((bf16[160,512]{1,0:T(8,128)(2,1)S(1)}, bf16[160,512]{1,0:T(8,128)(2,1)S(1)}, u32[]{:S(2)}, u32[]{:S(2)}) %collective-permute-start.7) | collective-permute-done | bytes 163872 | tf_op jit(solution)/shard_map/ppermute | solution.py:287
  22.1 2.6 %collective-permute-done.3 = bf16[160,512]{1,0:T(8,128)(2,1)S(1)} collective-permute-done((bf16[160,512]{1,0:T(8,128)(2,1)S(1)}, bf16[160,512]{1,0:T(8,128)(2,1)S(1)}, u32[]{:S(2)}, u32[]{:S(2)}) %collective-permute-start.3) | collective-permute-done | bytes 163872 | tf_op jit(solution)/shard_map/ppermute | solution.py:287
  25.4 6.9 %collective-permute-done.8 = bf16[320,512]{1,0:T(8,128)(2,1)S(1)} collective-permute-done((bf16[320,512]{1,0:T(8,128)(2,1)S(1)}, bf16[320,512]{1,0:T(8,128)(2,1)S(1)}, u32[]{:S(2)}, u32[]{:S(2)}) %collective-permute-start.8) | collective-permute-done | bytes 327712 | tf_op jit(solution)/shard_map/ppermute | solution.py:287
  36.3 4.5 %collective-permute-done.4 = bf16[320,512]{1,0:T(8,128)(2,1)S(1)} collective-permute-done((bf16[320,512]{1,0:T(8,128)(2,1)S(1)}, bf16[320,512]{1,0:T(8,128)(2,1)S(1)}, u32[]{:S(2)}, u32[]{:S(2)}) %collective-permute-start.4) | collective-permute-done | bytes 327712 | tf_op jit(solution)/shard_map/ppermute | solution.py:287
  41.7 2.5 %collective-permute-start.5 = (bf16[640,512]{1,0:T(8,128)(2,1)}, bf16[640,512]{1,0:T(8,128)(2,1)S(1)}, u32[]{:S(2)}, u32[]{:S(2)}) collective-permute-start(bf16[640,512]{1,0:T(8,128)(2,1)} %pad_maximum_fusion.3), channel_id=1, source_target_pairs={{0,2},{1,5},{2,0},{3,7},{4,6},{5,1},{6,4},{7,3},{8,10},{9,13},{10,... | collective-permute-start | bytes 1966088 | tf_op jit(solution)/shard_map/ppermute | solution.py:287
  50.4 2.9 %collective-permute-done.14 = bf16[320,512]{1,0:T(8,128)(2,1)S(1)} collective-permute-done((bf16[320,512]{1,0:T(8,128)(2,1)}, bf16[320,512]{1,0:T(8,128)(2,1)S(1)}, u32[]{:S(2)}, u32[]{:S(2)}) %collective-permute-start.14) | collective-permute-done | bytes 327712 | tf_op jit(solution)/shard_map/ppermute | solution.py:287
  53.3 2.3 %collective-permute-start.15 = (bf16[640,512]{1,0:T(8,128)(2,1)S(1)}, bf16[640,512]{1,0:T(8,128)(2,1)S(1)}, u32[]{:S(2)}, u32[]{:S(2)}) collective-permute-start(bf16[640,512]{1,0:T(8,128)(2,1)S(1)} %pad_maximum_fusion.5), channel_id=1, source_target_pairs={{0,2},{1,5},{2,0},{3,7},{4,6},{5,1},{6,4},{7,3},{8,10},{9,13},{10,... | collective-permute-start | bytes 1966088 | tf_op jit(solution)/shard_map/ppermute | solution.py:287
  58.2 4.5 %collective-permute-start.1 = (bf16[16,2560]{1,0:T(8,128)(2,1)S(1)}, bf16[16,2560]{1,0:T(8,128)(2,1)S(1)}, u32[]{:S(2)}, u32[]{:S(2)}) collective-permute-start(bf16[16,2560]{1,0:T(8,128)(2,1)S(1)} %slice_select_fusion), channel_id=1, source_target_pairs={{0,2},{1,3},{4,6},{5,7},{8,10},{9,11},{12,14},{13,15},{16,18},{17,... | collective-permute-start | bytes 245768 | tf_op jit(solution)/shard_map/ppermute | solution.py:353
  62.7 8.6 %collective-permute-done.15 = bf16[640,512]{1,0:T(8,128)(2,1)S(1)} collective-permute-done((bf16[640,512]{1,0:T(8,128)(2,1)S(1)}, bf16[640,512]{1,0:T(8,128)(2,1)S(1)}, u32[]{:S(2)}, u32[]{:S(2)}) %collective-permute-start.15) | collective-permute-done | bytes 655392 | tf_op jit(solution)/shard_map/ppermute | solution.py:287
  73.9 12.3 %first.1 = (bf16[1024,128]{1,0:T(8,128)(2,1)S(1)}, bf16[1024,256]{1,0:T(8,128)(2,1)S(1)}, f32[1024,128]{1,0:T(8,128)S(1)}, f32[1024,128]{1,0:T(8,128)S(1)}, f32[...) custom-call(s32[24]{0:T(128)S(1)} %stack.105.ints, bf16[512,2560]{1,0:T(8,128)(2,1)S(1)} %bitcast.55, ...), custom_call_target="tpu_custom_call" | custom-call | flops 2684354560 | bytes 9000000 | tf_op jit(solution)/shard_map/first/pallas_call | solution.py:419
  86.1 15.7 %collective-permute-start.11 = (bf16[1024,128]{1,0:T(8,128)(2,1)S(1)}, bf16[1024,128]{1,0:T(8,128)(2,1)S(1)}, u32[]{:S(2)}, u32[]{:S(2)}) collective-permute-start(bf16[1024,128]{1,0:T(8,128)(2,1)S(1)} %get-tuple-element.20), channel_id=1, source_target_pairs={{0,1},{1,0},{2,3},{3,2},{4,5},{5,4},{6,7},{7,6},{8,9},{9,8},{10,11... | collective-permute-start | bytes 786440 | tf_op jit(solution)/shard_map/ppermute | solution.py:287
  103.1 15.7 %scan.2 = (f32[1024,768]{1,0:T(8,128)}, f32[136,768]{1,0:T(8,128)S(1)}) custom-call(s32[24]{0:T(128)S(1)} %stack.105.ints, bf16[512,2560]{1,0:T(8,128)(2,1)} %bitcast.53, bf16[512,2560]{1,0:T(8,128)(2,1)} %collective-permute-done.other, bf16[16,2560]{1,0:T(8,128)(2,1)S(1)} %collective-permute-done.1.halo, bf16[1280,512]{1,0:T(8,128)(2,1)S(1)} %pad_maximum_fusion.low, ...), custom_call_target="tpu_custom_call" | custom-call | flops 6284354560 | bytes 12000000 | tf_op jit(solution)/shard_map/scan/pallas_call | solution.py:471
  118.8 2.6 %collective-permute-start.12 = (f32[136,768]{1,0:T(8,128)S(1)}, f32[136,768]{1,0:T(8,128)S(1)}, u32[]{:S(2)}, u32[]{:S(2)}) collective-permute-start(f32[136,768]{1,0:T(8,128)S(1)} %get-tuple-element.27.s_ref), channel_id=1, source_target_pairs={{0,2},{1,3},{2,0},{3,1},{4,6},{5,7},{6,4},{7,5},{8,10},{9,11},{10,... | collective-permute-start | bytes 1253384 | tf_op jit(solution)/shard_map/ppermute | solution.py:287
  121.4 14.9 %scan.3 = (f32[1024,512]{1,0:T(8,128)}, f32[136,512]{1,0:T(8,128)S(1)}) custom-call(s32[24]{0:T(128)S(1)} %stack.105.ints, bf16[512,2560]{1,0:T(8,128)(2,1)} %bitcast.54, bf16[512,2560]{1,0:T(8,128)(2,1)} %collective-permute-done.other, bf16[16,2560]{1,0:T(8,128)(2,1)S(1)} %collective-permute-done.1.halo, bf16[1280,512]{1,0:T(8,128)(2,1)S(1)} %pad_maximum_fusion.2.low, ...), custom_call_target="tpu_custom_call" | custom-call | flops 5084354560 | bytes 12000000 | tf_op jit(solution)/shard_map/scan/pallas_call | solution.py:471
  136.4 4.3 %join.2 = (f32[512,768]{1,0:T(8,128)}, f32[512,768]{1,0:T(8,128)S(1)}, bf16[384,128]{1,0:T(8,128)(2,1)S(1)}) custom-call(s32[24]{0:T(128)S(1)} %stack.105.ints, f32[1024,768]{1,0:T(8,128)S(1)} %copy-done, bf16[1024,128]{1,0:T(8,128)(2,1)S(1)} %get-tuple-element.39.c_ref, f32[1024,128]{1,0:T(8,128)S(1)} %get-tuple-element.26.ca_ref, ...), custom_call_target="tpu_custom_call" | custom-call | flops 402653184 | bytes 6291456 | tf_op jit(solution)/shard_map/join/pallas_call | solution.py:512
  140.7 4.2 %collective-permute-done.17.r_ref = f32[136,512]{1,0:T(8,128)S(1)} collective-permute-done((f32[136,512]{1,0:T(8,128)S(1)}, f32[136,512]{1,0:T(8,128)S(1)}, u32[]{:S(2)}, u32[]{:S(2)}) %collective-permute-start.17) | collective-permute-done | bytes 278560 | tf_op jit(solution)/shard_map/ppermute | solution.py:287
  145.0 2.4 %join.3 = (f32[512,512]{1,0:T(8,128)S(1)}, f32[512,512]{1,0:T(8,128)S(1)}, bf16[256,128]{1,0:T(8,128)(2,1)S(1)}) custom-call(s32[24]{0:T(128)S(1)} %stack.105.ints, f32[1024,512]{1,0:T(8,128)S(1)} %copy-done.1, bf16[1024,128]{1,0:T(8,128)(2,1)S(1)} %get-tuple-element.39.c_ref, f32[1024,128]{1,0:T(8,128)S(1)} %get-tuple-element.26.ca_ref, ...), custom_call_target="tpu_custom_call" | custom-call | flops 268435456 | bytes 4194304 | tf_op jit(solution)/shard_map/join/pallas_call | solution.py:512
  150.3 2.1 %collective-permute-start.20 = (bf16[384,128]{1,0:T(8,128)(2,1)S(1)}, bf16[384,128]{1,0:T(8,128)(2,1)S(1)}, u32[]{:S(2)}, u32[]{:S(2)}) collective-permute-start(bf16[384,128]{1,0:T(8,128)(2,1)S(1)} %get-tuple-element.34), channel_id=1, source_target_pairs={{0,16},{1,17},{2,18},{3,19},{4,20},{5,21},{6,22},{7,23},{8,24},{9,... | collective-permute-start | bytes 294920 | tf_op jit(solution)/shard_map/ppermute | solution.py:287
  152.3 4.5 %collective-permute-done.23 = bf16[256,128]{1,0:T(8,128)(2,1)S(1)} collective-permute-done((bf16[256,128]{1,0:T(8,128)(2,1)S(1)}, bf16[256,128]{1,0:T(8,128)(2,1)S(1)}, u32[]{:S(2)}, u32[]{:S(2)}) %collective-permute-start.23) | collective-permute-done | bytes 65568 | tf_op jit(solution)/shard_map/ppermute | solution.py:287
  158.9 2.1 %collective-permute-start.21 = (bf16[2,384,128]{2,1,0:T(8,128)(2,1)S(1)}, bf16[2,384,128]{2,1,0:T(8,128)(2,1)S(1)}, u32[]{:S(2)}, u32[]{:S(2)}) collective-permute-start(bf16[2,384,128]{2,1,0:T(8,128)(2,1)S(1)} %pad_maximum_fusion.11), channel_id=1, source_target_pairs={{0,8},{1,9},{2,10},{3,11},{4,12},{5,13},{6,14},{7,15},{8,0},{9,1},... | collective-permute-start | bytes 589832 | tf_op jit(solution)/shard_map/ppermute | solution.py:287
  161.0 2.1 %collective-permute-done.24 = bf16[2,256,128]{2,1,0:T(8,128)(2,1)} collective-permute-done((bf16[2,256,128]{2,1,0:T(8,128)(2,1)}, bf16[2,256,128]{2,1,0:T(8,128)(2,1)}, u32[]{:S(2)}, u32[]{:S(2)}) %collective-permute-start.24) | collective-permute-done | bytes 131104 | tf_op jit(solution)/shard_map/ppermute | solution.py:287
  168.7 2.9 %collective-permute-done.22 = bf16[384,128]{1,0:T(8,128)(2,1)S(1)} collective-permute-done((bf16[384,128]{1,0:T(8,128)(2,1)S(1)}, bf16[384,128]{1,0:T(8,128)(2,1)S(1)}, u32[]{:S(2)}, u32[]{:S(2)}) %collective-permute-start.22) | collective-permute-done | bytes 98336 | tf_op jit(solution)/shard_map/ppermute | solution.py:287
  172.4 2.9 %norm.1 = bf16[512,2560]{1,0:T(8,128)(2,1)} custom-call(s32[24]{0:T(128)S(1)} %stack.105.ints, f32[1,2560]{1,0:T(1,128)S(1)} %broadcast_in_dim.38.gain_ref, f32[512,768]{1,0:T(8,128)S(1)} %get-tuple-element.28.ka_ref, f32[512,512]{1,0:T(8,128)S(1)} %copy-done.3, f32[512,768]{1,0:T(8,128)S(1)} %collective-permute-done.18.ra_ref, ...), custom_call_target="tpu_custom_call" | custom-call | flops 7864320 | bytes 7864320 | tf_op jit(solution)/shard_map/norm/pallas_call | solution.py:577
  (129 shorter events, 32.5 us)
Async XLA Ops:
  4.2 53.1 %collective-permute-start = (bf16[512,2560]{1,0:T(8,128)(2,1)}, bf16[512,2560]{1,0:T(8,128)(2,1)}, u32[]{:S(2)}, u32[]{:S(2)}) collective-permute-start(bf16[512,2560]{1,0:T(8,128)(2,1)} %bitcast.52), channel_id=1, source_target_pairs={{0,1},{1,0},{2,3},{3,2},{4,5},{5,4},{6,7},{7,6},{8,9},{9,8},{10,11... | collective-permute-start | bytes 7864328 | tf_op jit(solution)/shard_map/ppermute | solution.py:287
  5.5 16.0 %collective-permute-start.7 = (bf16[160,512]{1,0:T(8,128)(2,1)S(1)}, bf16[160,512]{1,0:T(8,128)(2,1)S(1)}, u32[]{:S(2)}, u32[]{:S(2)}) collective-permute-start(bf16[160,512]{1,0:T(8,128)(2,1)S(1)} %get-tuple-element.42), channel_id=1, source_target_pairs={{0,16},{1,17},{2,18},{3,19},{4,20},{5,21},{6,22},{7,23},{8,24},{9,... | collective-permute-start | bytes 491528 | tf_op jit(solution)/shard_map/ppermute | solution.py:287
  9.5 15.1 %collective-permute-start.3 = (bf16[160,512]{1,0:T(8,128)(2,1)S(1)}, bf16[160,512]{1,0:T(8,128)(2,1)S(1)}, u32[]{:S(2)}, u32[]{:S(2)}) collective-permute-start(bf16[160,512]{1,0:T(8,128)(2,1)S(1)} %get-tuple-element.43), channel_id=1, source_target_pairs={{0,16},{1,17},{2,18},{3,19},{4,20},{5,21},{6,22},{7,23},{8,24},{9,... | collective-permute-start | bytes 491528 | tf_op jit(solution)/shard_map/ppermute | solution.py:287
  21.6 10.7 %collective-permute-start.8 = (bf16[320,512]{1,0:T(8,128)(2,1)S(1)}, bf16[320,512]{1,0:T(8,128)(2,1)S(1)}, u32[]{:S(2)}, u32[]{:S(2)}) collective-permute-start(bf16[320,512]{1,0:T(8,128)(2,1)S(1)} %pad_maximum_fusion.8), channel_id=1, source_target_pairs={{0,8},{1,9},{2,10},{3,11},{4,12},{5,13},{6,14},{7,15},{8,0},{9,1},... | collective-permute-start | bytes 983048 | tf_op jit(solution)/shard_map/ppermute | solution.py:287
  24.7 16.1 %collective-permute-start.4 = (bf16[320,512]{1,0:T(8,128)(2,1)S(1)}, bf16[320,512]{1,0:T(8,128)(2,1)S(1)}, u32[]{:S(2)}, u32[]{:S(2)}) collective-permute-start(bf16[320,512]{1,0:T(8,128)(2,1)S(1)} %pad_maximum_fusion.7), channel_id=1, source_target_pairs={{0,8},{1,9},{2,10},{3,11},{4,12},{5,13},{6,14},{7,15},{8,0},{9,1},... | collective-permute-start | bytes 983048 | tf_op jit(solution)/shard_map/ppermute | solution.py:287
  33.2 15.9 %collective-permute-start.9 = (bf16[640,512]{1,0:T(8,128)(2,1)}, bf16[640,512]{1,0:T(8,128)(2,1)S(1)}, u32[]{:S(2)}, u32[]{:S(2)}) collective-permute-start(bf16[640,512]{1,0:T(8,128)(2,1)} %pad_maximum_fusion.4), channel_id=1, source_target_pairs={{0,2},{1,5},{2,0},{3,7},{4,6},{5,1},{6,4},{7,3},{8,10},{9,13},{10,... | collective-permute-start | bytes 1966088 | tf_op jit(solution)/shard_map/ppermute | solution.py:287
  35.1 9.8 %collective-permute-start.13 = (bf16[160,512]{1,0:T(8,128)(2,1)S(1)}, bf16[160,512]{1,0:T(8,128)(2,1)S(1)}, u32[]{:S(2)}, u32[]{:S(2)}) collective-permute-start(bf16[160,512]{1,0:T(8,128)(2,1)S(1)} %get-tuple-element.41), channel_id=1, source_target_pairs={{0,16},{1,17},{2,18},{3,19},{4,20},{5,21},{6,22},{7,23},{8,24},{9,... | collective-permute-start | bytes 491528 | tf_op jit(solution)/shard_map/ppermute | solution.py:287
  41.7 13.9 %collective-permute-start.5 = (bf16[640,512]{1,0:T(8,128)(2,1)}, bf16[640,512]{1,0:T(8,128)(2,1)S(1)}, u32[]{:S(2)}, u32[]{:S(2)}) collective-permute-start(bf16[640,512]{1,0:T(8,128)(2,1)} %pad_maximum_fusion.3), channel_id=1, source_target_pairs={{0,2},{1,5},{2,0},{3,7},{4,6},{5,1},{6,4},{7,3},{8,10},{9,13},{10,... | collective-permute-start | bytes 1966088 | tf_op jit(solution)/shard_map/ppermute | solution.py:287
  45.7 7.6 %collective-permute-start.14 = (bf16[320,512]{1,0:T(8,128)(2,1)}, bf16[320,512]{1,0:T(8,128)(2,1)S(1)}, u32[]{:S(2)}, u32[]{:S(2)}) collective-permute-start(bf16[320,512]{1,0:T(8,128)(2,1)} %pad_maximum_fusion.9), channel_id=1, source_target_pairs={{0,8},{1,9},{2,10},{3,11},{4,12},{5,13},{6,14},{7,15},{8,0},{9,1},... | collective-permute-start | bytes 983048 | tf_op jit(solution)/shard_map/ppermute | solution.py:287
  49.2 24.7 %collective-permute-start.10 = (bf16[1280,512]{1,0:T(8,128)(2,1)S(1)}, bf16[1280,512]{1,0:T(8,128)(2,1)S(1)}, u32[]{:S(2)}, u32[]{:S(2)}) collective-permute-start(bf16[1280,512]{1,0:T(8,128)(2,1)S(1)} %pad_maximum_fusion.1.low), channel_id=1, source_target_pairs={{0,4},{1,3},{2,6},{3,1},{4,0},{5,7},{6,2},{7,5},{8,12},{9,11},{10,... | collective-permute-start | bytes 3932168 | tf_op jit(solution)/shard_map/ppermute | solution.py:287
  53.3 18.0 %collective-permute-start.15 = (bf16[640,512]{1,0:T(8,128)(2,1)S(1)}, bf16[640,512]{1,0:T(8,128)(2,1)S(1)}, u32[]{:S(2)}, u32[]{:S(2)}) collective-permute-start(bf16[640,512]{1,0:T(8,128)(2,1)S(1)} %pad_maximum_fusion.5), channel_id=1, source_target_pairs={{0,2},{1,5},{2,0},{3,7},{4,6},{5,1},{6,4},{7,3},{8,10},{9,13},{10,... | collective-permute-start | bytes 1966088 | tf_op jit(solution)/shard_map/ppermute | solution.py:287
  55.7 47.4 %collective-permute-start.6 = (bf16[1280,512]{1,0:T(8,128)(2,1)S(1)}, bf16[1280,512]{1,0:T(8,128)(2,1)S(1)}, u32[]{:S(2)}, u32[]{:S(2)}) collective-permute-start(bf16[1280,512]{1,0:T(8,128)(2,1)S(1)} %pad_maximum_fusion.low), channel_id=1, source_target_pairs={{0,4},{1,3},{2,6},{3,1},{4,0},{5,7},{6,2},{7,5},{8,12},{9,11},{10,... | collective-permute-start | bytes 3932168 | tf_op jit(solution)/shard_map/ppermute | solution.py:287
  58.2 15.6 %collective-permute-start.1 = (bf16[16,2560]{1,0:T(8,128)(2,1)S(1)}, bf16[16,2560]{1,0:T(8,128)(2,1)S(1)}, u32[]{:S(2)}, u32[]{:S(2)}) collective-permute-start(bf16[16,2560]{1,0:T(8,128)(2,1)S(1)} %slice_select_fusion), channel_id=1, source_target_pairs={{0,2},{1,3},{4,6},{5,7},{8,10},{9,11},{12,14},{13,15},{16,18},{17,... | collective-permute-start | bytes 245768 | tf_op jit(solution)/shard_map/ppermute | solution.py:353
  71.3 50.1 %collective-permute-start.16 = (bf16[1280,512]{1,0:T(8,128)(2,1)S(1)}, bf16[1280,512]{1,0:T(8,128)(2,1)S(1)}, u32[]{:S(2)}, u32[]{:S(2)}) collective-permute-start(bf16[1280,512]{1,0:T(8,128)(2,1)S(1)} %pad_maximum_fusion.2.low), channel_id=1, source_target_pairs={{0,4},{1,3},{2,6},{3,1},{4,0},{5,7},{6,2},{7,5},{8,12},{9,11},{10,... | collective-permute-start | bytes 3932168 | tf_op jit(solution)/shard_map/ppermute | solution.py:287
  86.1 16.9 %collective-permute-start.11 = (bf16[1024,128]{1,0:T(8,128)(2,1)S(1)}, bf16[1024,128]{1,0:T(8,128)(2,1)S(1)}, u32[]{:S(2)}, u32[]{:S(2)}) collective-permute-start(bf16[1024,128]{1,0:T(8,128)(2,1)S(1)} %get-tuple-element.20), channel_id=1, source_target_pairs={{0,1},{1,0},{2,3},{3,2},{4,5},{5,4},{6,7},{7,6},{8,9},{9,8},{10,11... | collective-permute-start | bytes 786440 | tf_op jit(solution)/shard_map/ppermute | solution.py:287
  118.8 17.6 %collective-permute-start.12 = (f32[136,768]{1,0:T(8,128)S(1)}, f32[136,768]{1,0:T(8,128)S(1)}, u32[]{:S(2)}, u32[]{:S(2)}) collective-permute-start(f32[136,768]{1,0:T(8,128)S(1)} %get-tuple-element.27.s_ref), channel_id=1, source_target_pairs={{0,2},{1,3},{2,0},{3,1},{4,6},{5,7},{6,4},{7,5},{8,10},{9,11},{10,... | collective-permute-start | bytes 1253384 | tf_op jit(solution)/shard_map/ppermute | solution.py:287
  136.3 8.7 %collective-permute-start.17 = (f32[136,512]{1,0:T(8,128)S(1)}, f32[136,512]{1,0:T(8,128)S(1)}, u32[]{:S(2)}, u32[]{:S(2)}) collective-permute-start(f32[136,512]{1,0:T(8,128)S(1)} %get-tuple-element.30.s_ref), channel_id=1, source_target_pairs={{0,2},{1,3},{2,0},{3,1},{4,6},{5,7},{6,4},{7,5},{8,10},{9,11},{10,... | collective-permute-start | bytes 835592 | tf_op jit(solution)/shard_map/ppermute | solution.py:287
  140.7 31.7 %collective-permute-start.18 = (f32[512,768]{1,0:T(8,128)}, f32[512,768]{1,0:T(8,128)S(1)}, u32[]{:S(2)}, u32[]{:S(2)}) collective-permute-start(f32[512,768]{1,0:T(8,128)} %get-tuple-element.32), channel_id=1, source_target_pairs={{0,1},{1,0},{2,3},{3,2},{4,5},{5,4},{6,7},{7,6},{8,9},{9,8},{10,11... | collective-permute-start | bytes 4718600 | tf_op jit(solution)/shard_map/ppermute | solution.py:287
  149.4 7.4 %collective-permute-start.23 = (bf16[256,128]{1,0:T(8,128)(2,1)S(1)}, bf16[256,128]{1,0:T(8,128)(2,1)S(1)}, u32[]{:S(2)}, u32[]{:S(2)}) collective-permute-start(bf16[256,128]{1,0:T(8,128)(2,1)S(1)} %get-tuple-element.35), channel_id=1, source_target_pairs={{0,16},{1,17},{2,18},{3,19},{4,20},{5,21},{6,22},{7,23},{8,24},{9,... | collective-permute-start | bytes 196616 | tf_op jit(solution)/shard_map/ppermute | solution.py:287
  150.3 8.6 %collective-permute-start.20 = (bf16[384,128]{1,0:T(8,128)(2,1)S(1)}, bf16[384,128]{1,0:T(8,128)(2,1)S(1)}, u32[]{:S(2)}, u32[]{:S(2)}) collective-permute-start(bf16[384,128]{1,0:T(8,128)(2,1)S(1)} %get-tuple-element.34), channel_id=1, source_target_pairs={{0,16},{1,17},{2,18},{3,19},{4,20},{5,21},{6,22},{7,23},{8,24},{9,... | collective-permute-start | bytes 294920 | tf_op jit(solution)/shard_map/ppermute | solution.py:287
  157.5 5.6 %collective-permute-start.24 = (bf16[2,256,128]{2,1,0:T(8,128)(2,1)}, bf16[2,256,128]{2,1,0:T(8,128)(2,1)}, u32[]{:S(2)}, u32[]{:S(2)}) collective-permute-start(bf16[2,256,128]{2,1,0:T(8,128)(2,1)} %pad_maximum_fusion.13), channel_id=1, source_target_pairs={{0,8},{1,9},{2,10},{3,11},{4,12},{5,13},{6,14},{7,15},{8,0},{9,1},... | collective-permute-start | bytes 393224 | tf_op jit(solution)/shard_map/ppermute | solution.py:287
  158.8 13.6 %collective-permute-start.19 = (f32[512,512]{1,0:T(8,128)}, f32[512,512]{1,0:T(8,128)S(1)}, u32[]{:S(2)}, u32[]{:S(2)}) collective-permute-start(f32[512,512]{1,0:T(8,128)} %copy-done.5), channel_id=1, source_target_pairs={{0,1},{1,0},{2,3},{3,2},{4,5},{5,4},{6,7},{7,6},{8,9},{9,8},{10,11... | collective-permute-start | bytes 3145736 | tf_op jit(solution)/shard_map/ppermute | solution.py:287
  158.9 8.0 %collective-permute-start.21 = (bf16[2,384,128]{2,1,0:T(8,128)(2,1)S(1)}, bf16[2,384,128]{2,1,0:T(8,128)(2,1)S(1)}, u32[]{:S(2)}, u32[]{:S(2)}) collective-permute-start(bf16[2,384,128]{2,1,0:T(8,128)(2,1)S(1)} %pad_maximum_fusion.11), channel_id=1, source_target_pairs={{0,8},{1,9},{2,10},{3,11},{4,12},{5,13},{6,14},{7,15},{8,0},{9,1},... | collective-permute-start | bytes 589832 | tf_op jit(solution)/shard_map/ppermute | solution.py:287
  166.9 4.7 %collective-permute-start.22 = (bf16[384,128]{1,0:T(8,128)(2,1)S(1)}, bf16[384,128]{1,0:T(8,128)(2,1)S(1)}, u32[]{:S(2)}, u32[]{:S(2)}) collective-permute-start(bf16[384,128]{1,0:T(8,128)(2,1)S(1)} %dynamic-slice_bitcast_fusion), channel_id=1, source_target_pairs={{0,4},{1,5},{2,6},{3,7},{4,0},{5,1},{6,2},{7,3},{8,12},{9,13},{10,... | collective-permute-start | bytes 294920 | tf_op jit(solution)/shard_map/ppermute | solution.py:287
  (17 other events, 134.4 us)

commit v2 on v0

--- a/solution.py
+++ b/solution.py
@@ -1,12 +1,517 @@
+import functools
+
 import jax
 import jax.numpy as jnp
 from jax import lax
+from jax.experimental import pallas as pl
+from jax.experimental.pallas import tpu as pltpu
 from jax.sharding import PartitionSpec as P
 
 GROUP = 256
-
-
 EPS = 1e-05
+LOG2E = 1.4426950408889634
+LANES = 128
+HALO = 16
+F32 = jnp.float32
+BF16 = jnp.bfloat16
+AXES = ("req", "seq")
+FLIPS = {"a": 16, "b": 8, "y": 4, "x": 2}
+ROUTES = (("axyb", "abxy"), ("abyx", "axby"), ("ayxb", "abyx"), ("aybx", "abxy"))
+PAIRS = ((0,), (1, 2, 3), (4, 5, 6, 7), (8, 9))
+VMEM = pl.BlockSpec(memory_space=pltpu.VMEM)
+SMEM = pl.BlockSpec(memory_space=pltpu.SMEM)
+
+
+def dot(a, b):
+    return jnp.dot(a, b, preferred_element_type=F32)
+
+
+def params(vmem_mib):
+    return pltpu.CompilerParams(vmem_limit_bytes=vmem_mib * 1024 * 1024)
+
+
+def first_head(pair, share):
+    return (pair % 2) * share + 2 * (pair // 2)
+
+
+def lanes(i):
+    return slice(i * LANES, (i + 1) * LANES)
+
+
+def valid_rows(first, rows, start, end):
+    place = first + lax.broadcasted_iota(jnp.int32, (rows, LANES), 0)
+    return jnp.where((place >= start) & (place < end), 1.0, 0.0).astype(F32)
+
+
+def column(a, head):
+    return jnp.broadcast_to(a[:, head : head + 1], (a.shape[0], LANES))
+
+
+def split(a):
+    upper = a.astype(BF16)
+    return upper, (a - upper.astype(F32)).astype(BF16)
+
+
+def project(chunk, ints, own, other, low, high, whole, padded, raw):
+    block = low.shape[0] // 8
+    for p in range(16):
+        source = low if p < 8 else high
+        row = pl.multiple_of(ints[8 + 16 * chunk + p] * block, block)
+        whole[pl.ds(row, block), :] = source[(p % 8) * block : (p % 8 + 1) * block, :]
+    start, end, first, core = ints[0], ints[1], ints[2], ints[3]
+    span = other.shape[0]
+    spans = [i for i in range(low.shape[1] // LANES) if raw is None or i != 1]
+    mine = dot(own[...], whole[...])
+    theirs = dot(other[...], whole[...])
+    at_mine = pl.multiple_of(core * span, span)
+    at_theirs = pl.multiple_of((1 - core) * span, span)
+    ok_edge = valid_rows(first - 8, 8, start, end)
+    ok_mine = valid_rows(first + at_mine, span, start, end)
+    ok_theirs = valid_rows(first + at_theirs, span, start, end)
+
+    def rounded(a, ok):
+        return (a * ok).astype(BF16).astype(F32)
+
+    for at, lane in enumerate(spans):
+        edge = mine[0:HALO, lanes(lane)][HALO - 8 :]
+        padded[at, 0:8, :] = rounded(edge, ok_edge)
+        padded[at, pl.ds(8 + at_mine, span), :] = rounded(mine[HALO:, lanes(lane)], ok_mine)
+        padded[at, pl.ds(8 + at_theirs, span), :] = rounded(theirs[:, lanes(lane)], ok_theirs)
+    if raw is not None:
+        raw[pl.ds(at_mine, span), :] = mine[HALO:, lanes(1)]
+        raw[pl.ds(at_theirs, span), :] = theirs[:, lanes(1)]
+
+
+def convolved(at, group, taps, padded):
+    total = taps[4:5, lanes(at)]
+    for k in range(4):
+        rows = padded[at, group * GROUP + 5 + k : (group + 1) * GROUP + 5 + k, :]
+        total = total + taps[k : k + 1, lanes(at)] * rows
+    half = 0.5 * total
+    return (half + half * jnp.tanh(half)).astype(BF16)
+
+
+def first_kernel(
+    ints, own, other, low, high, taps, rates,
+    bc_out, x_out, cq_out, kq_out, kt_out, ca_out, tot_out,
+    whole, padded, raw,
+):
+    project(0, ints, own, other, low, high, whole, padded, raw)
+    row = lax.broadcasted_iota(jnp.int32, (GROUP, GROUP), 0)
+    col = lax.broadcasted_iota(jnp.int32, (GROUP, GROUP), 1)
+    below = jnp.where(row >= col, 1.0, 0.0).astype(BF16)
+    before = jnp.zeros((1, LANES), F32)
+    for group in range(bc_out.shape[0] // GROUP):
+        rows = slice(group * GROUP, (group + 1) * GROUP)
+        bc_out[rows, :] = convolved(0, group, taps, padded)
+        for at in range(1, padded.shape[0]):
+            x_out[rows, lanes(at - 1)] = convolved(at, group, taps, padded)
+        ok = valid_rows(ints[2] + group * GROUP, GROUP, ints[0], ints[1])
+        step = raw[rows, :] + rates[0:1, :]
+        size = (jnp.maximum(step, 0.0) + jnp.log1p(jnp.exp(-jnp.abs(step)))) * ok
+        decay = size * rates[1:2, :]
+        high_part, rest = split(decay)
+        rest = decay - high_part.astype(F32)
+        mid_part, low_part = split(rest)
+        cum = dot(below, high_part) + dot(below, mid_part) + dot(below, low_part)
+        from_key = jnp.log2(size) - cum
+        cq_out[rows, :] = cum
+        kq_out[rows, :] = from_key
+        kt_out[group] = from_key.T[0:32, :]
+        ca_out[rows, :] = cum + before
+        before = before + cum[GROUP - 1 : GROUP, :]
+    tot_out[...] = jnp.broadcast_to(before, tot_out.shape)
+
+
+def scan_kernel(
+    chunk, heads, extra, ints, own, other, low, high, taps, x_ref, b_ref, c_ref, cq_ref, kq_ref,
+    kt_ref, tot_ref, skip_ref, y_out, s_out, send_out, whole, padded, carry,
+):
+    project(chunk, ints, own, other, low, high, whole, padded, None)
+    pairs = len(heads)
+    half = GROUP // 2
+    row = lax.broadcasted_iota(jnp.int32, (half, half), 0)
+    col = lax.broadcasted_iota(jnp.int32, (half, half), 1)
+    causal = row >= col
+    left = lax.broadcasted_iota(jnp.int32, (GROUP, LANES), 1) < LANES // 2
+    zero = jnp.zeros((GROUP, LANES), BF16)
+    for group in range(y_out.shape[0] // GROUP):
+        rows = slice(group * GROUP, (group + 1) * GROUP)
+        b, c = b_ref[rows, :], c_ref[rows, :]
+        scores = lax.dot_general(c, b, (((1,), (1,)), ((), ())), preferred_element_type=F32)
+        cq, kq, kt = cq_ref[rows, :], kq_ref[rows, :], kt_ref[group]
+        carried = None
+        if group:
+            upper, lower = split(carry[...])
+            carried = dot(jnp.concatenate([c, c], axis=1), jnp.concatenate([upper, lower], axis=0))
+        scaled, ends = [], []
+        for i, head in enumerate(heads):
+            if i < extra:
+                x = x_ref[rows, lanes(i)]
+            else:
+                x = convolved(i - extra, group, taps, padded)
+            top, bottom, spread = [], [], []
+            for h in (head, head + 1):
+                q = column(cq, h)
+                spread.append(q)
+                k0 = jnp.broadcast_to(kt[h : h + 1, 0:half], (half, half))
+                k1 = jnp.broadcast_to(kt[h : h + 1, half:], (half, half))
+                m00 = jnp.where(causal, jnp.exp2(q[0:half] + k0) * scores[0:half, 0:half], 0.0)
+                m10 = jnp.exp2(q[half:] + k0) * scores[half:, 0:half]
+                m11 = jnp.where(causal, jnp.exp2(q[half:] + k1) * scores[half:, half:], 0.0)
+                top.append(m00.astype(BF16))
+                bottom.append(m10.astype(BF16))
+                bottom.append(m11.astype(BF16))
+            x0, x1 = jnp.where(left, x, zero), jnp.where(left, zero, x)
+            y_top = dot(
+                jnp.concatenate(top, axis=1), jnp.concatenate([x0[0:half], x1[0:half]], axis=0)
+            )
+            y_bottom = dot(jnp.concatenate(bottom, axis=1), jnp.concatenate([x0, x1], axis=0))
+            q = jnp.where(left, spread[0], spread[1])
+            xf = x.astype(F32)
+            rest = skip_ref[0:1, lanes(i)] * xf
+            if group:
+                rest = rest + jnp.exp2(q) * carried[:, lanes(i)]
+            y_out[group * GROUP : group * GROUP + half, lanes(i)] = y_top + rest[0:half]
+            y_out[group * GROUP + half : (group + 1) * GROUP, lanes(i)] = y_bottom + rest[half:]
+            k = jnp.where(left, column(kq, head), column(kq, head + 1))
+            end = q[GROUP - 1 : GROUP, :]
+            scaled.append((jnp.exp2(k + end) * xf).astype(BF16))
+            ends.append(jnp.exp2(end))
+        local = lax.dot_general(
+            b, jnp.concatenate(scaled, axis=1), (((0,), (0,)), ((), ())), preferred_element_type=F32
+        )
+        if group:
+            local = jnp.concatenate(ends, axis=1) * carry[...] + local
+        carry[...] = local
+    s_out[...] = carry[...]
+    send_out[0:LANES, :] = carry[...].astype(BF16)
+    side = lax.broadcasted_iota(jnp.int32, (8, LANES), 1) < LANES // 2
+    for i, head in enumerate(heads):
+        total = jnp.where(side, column(tot_ref[...], head), column(tot_ref[...], head + 1))
+        one, rest = split(total)
+        two, three = split(total - one.astype(F32))
+        place = lax.broadcasted_iota(jnp.int32, (8, LANES), 0)
+        parts = jnp.where(place == 0, one.astype(F32), two.astype(F32))
+        parts = jnp.where(place >= 2, three.astype(F32), parts)
+        parts = jnp.where(place >= 3, 0.0, parts)
+        send_out[LANES:, lanes(i)] = jnp.concatenate([parts, jnp.zeros_like(parts)], axis=0).astype(
+            BF16
+        )
+
+
+def join_kernel(heads, sizes, halves, ints, c_ref, ca_ref, tot_ref, r_ref, *refs):
+    count = len(sizes)
+    y_refs, s_refs = refs[:count], refs[count : 2 * count]
+    send_out, keep_out, fin_out = refs[2 * count :]
+    later = ints[4] > 0
+    core = ints[3]
+    where = [(j, k) for j, size in enumerate(sizes) for k in range(size)]
+    span = send_out.shape[0]
+    left = lax.broadcasted_iota(jnp.int32, (span, LANES), 1) < LANES // 2
+    received = r_ref[0:LANES, :].astype(F32)
+    entering = (received * jnp.where(later, 1.0, 0.0)).astype(BF16)
+    for out, at in ((send_out, (1 - core) * span), (keep_out, core * span)):
+        rows = pl.ds(pl.multiple_of(at, span), span)
+        c, ca = c_ref[rows, :], ca_ref[rows, :]
+        carried = dot(c, entering)
+        for i, head in enumerate(heads):
+            j, k = where[i]
+            q = jnp.where(left, column(ca, head), column(ca, head + 1))
+            out[:, lanes(i)] = y_refs[j][rows, lanes(k)] + jnp.exp2(q) * carried[:, lanes(i)]
+    side = lax.broadcasted_iota(jnp.int32, (8, LANES), 1) < LANES // 2
+    for i, (early, late) in enumerate(halves):
+
+        def own_state(p):
+            j, k = where[p]
+            return s_refs[j][:, lanes(k)]
+
+        parts = r_ref[LANES:, lanes(early)].astype(F32)
+        their_total = parts[0:1] + parts[1:2] + parts[2:3]
+        tot = tot_ref[...]
+        my_total = jnp.where(side, column(tot, heads[late]), column(tot, heads[late] + 1))[0:1]
+        at_first = jnp.exp2(their_total) * own_state(early) + received[:, lanes(early)]
+        at_last = jnp.exp2(my_total) * received[:, lanes(late)] + own_state(late)
+        both = jnp.where(later, at_last, at_first)
+        fin_out[i * LANES : (i + 1) * LANES, :] = both.T.astype(fin_out.dtype)
+
+
+def norm_kernel(places, ints, gain_ref, ka_ref, kb_ref, ra_ref, rb_ref, out_ref):
+    step = pl.program_id(0)
+    core = ints[3]
+    rows = out_ref.shape[0]
+    first = ints[2] + (core * pl.num_programs(0) + step) * rows
+    ok = valid_rows(first, rows, ints[0], ints[1])
+    blocks = []
+    for who, refs in ((core, (ka_ref, kb_ref)), (1 - core, (ra_ref, rb_ref))):
+        for ref, wheres in zip(refs, places, strict=True):
+            for i, where in enumerate(wheres):
+                at = pl.multiple_of((where + 5 * who) * LANES, LANES)
+                blocks.append((at, ref, i))
+    total = jnp.zeros((rows, LANES), F32)
+    for _, ref, i in blocks:
+        v = ref[:, lanes(i)]
+        total = total + v * v
+    mean = jnp.sum(total, axis=1, keepdims=True) * (1.0 / out_ref.shape[1])
+    factor = lax.rsqrt(mean + EPS) * ok
+    for at, ref, i in blocks:
+        v = ref[:, lanes(i)]
+        out_ref[:, pl.ds(at, LANES)] = (v * factor * gain_ref[0:1, pl.ds(at, LANES)]).astype(BF16)
+
+
+def swapped(x, masks):
+    count = lax.axis_size("req") * lax.axis_size("seq")
+    return lax.ppermute(x, AXES, [(i, i ^ masks[i % 2]) for i in range(count)])
+
+
+def on_device(
+    tokens, mix_weight, step_weight, conv_weight, conv_bias, step_bias, decay_rate, skip_gain,
+    norm_gain, prompt_len, prompt_start, deal,
+):
+    seq_index = lax.axis_index("seq")
+    req_index = lax.axis_index("req")
+    core, along = seq_index % 2, seq_index // 2
+    rows = tokens[0]
+    span, depth = rows.shape
+    inner = norm_gain.shape[0]
+    heads = decay_rate.shape[0]
+    head_dim = inner // heads
+    nstate = (mix_weight.shape[1] - inner) // 2
+    share = heads // 4
+    quarter = inner // 4
+    chip = req_index * 2 + along
+
+    def mine_of(a, b, who):
+        bc = lax.dynamic_slice_in_dim(a, inner + nstate * who, nstate, 1)
+        early = lax.dynamic_slice_in_dim(a, quarter * who, quarter, 1)
+        late = lax.dynamic_slice_in_dim(a, 2 * quarter + quarter * who, quarter, 1)
+        parts = [bc]
+        if b is not None:
+            parts += [steps_of(b, who)]
+        for i in range(quarter // LANES):
+            parts += [early[:, lanes(i)], late[:, lanes(i)]]
+        return jnp.concatenate(parts, axis=1)
+
+    def steps_of(b, who):
+        one = lax.dynamic_slice_in_dim(b, share * who, share, 1)
+        two = lax.dynamic_slice_in_dim(b, 2 * share + share * who, share, 1)
+        return jnp.concatenate(
+            [one, two, jnp.zeros((b.shape[0], LANES - 2 * share), b.dtype)], axis=1
+        )
+
+    kept = mine_of(mix_weight, step_weight, core)
+    given = mine_of(mix_weight, step_weight, 1 - core)
+    got = swapped(given, (1, 1))
+    weights = jnp.where(
+        core == 0, jnp.concatenate([kept, got], axis=0), jnp.concatenate([got, kept], axis=0)
+    )
+
+    order = []
+
+    def gathered(block, routes):
+        masks = [(FLIPS[one], FLIPS[two]) for one, two in zip(*routes, strict=True)]
+        for p in range(2 ** len(masks)):
+            one, two = (
+                sum(mask[who] // 2 for s, mask in enumerate(masks) if (p >> s) & 1)
+                for who in range(2)
+            )
+            order.append(jnp.bitwise_xor(chip, jnp.where(core == 0, one, two)))
+        for mask in masks[:-1]:
+            block = jnp.concatenate([block, swapped(block, mask)], axis=0)
+        return block, swapped(block, masks[-1])
+
+    chunks, at = [], 0
+    for i, routes in enumerate(ROUTES):
+        width = (len(PAIRS[i]) + (2 if i == 0 else 0)) * LANES
+        chunks.append(gathered(weights[:, at : at + width], routes))
+        at += width
+
+    other = swapped(rows, (1, 1))
+    last_rows = jnp.where(core == 1, rows[span - HALO :], other[span - HALO :])
+    count = lax.axis_size("req") * lax.axis_size("seq")
+    halo = lax.ppermute(
+        last_rows, AXES, [(i, i + 2) for i in range(count) if (i // 2) % 2 == 0]
+    )
+    own = jnp.concatenate([halo, rows], axis=0)
+
+    slots = jnp.arange(deal.shape[0], dtype=jnp.int32)
+    request = jnp.sum(jnp.where(slots == req_index, deal, 0))
+    length = jnp.sum(jnp.where(slots == request, prompt_len, 0))
+    start = jnp.sum(jnp.where(slots == request, prompt_start, 0))
+    taps = mine_of(
+        jnp.concatenate([conv_weight, conv_bias[None], jnp.zeros_like(conv_weight[:3])], axis=0),
+        None,
+        core,
+    )
+    rates = jnp.concatenate(
+        [
+            steps_of(step_bias[None], core),
+            steps_of(decay_rate[None] * (-LOG2E), core),
+            jnp.zeros((6, LANES), F32),
+        ],
+        axis=0,
+    )
+    skip_all = mine_of(
+        jnp.concatenate([jnp.repeat(skip_gain, head_dim), jnp.zeros((2 * nstate,), F32)])[None],
+        None,
+        core,
+    )
+    skip = jnp.broadcast_to(skip_all[:, LANES:], (8, inner // 2))
+    ints = jnp.stack(
+        [start, start + length, along * 2 * span, core, along]
+        + [jnp.zeros_like(core)] * 3
+        + order
+    ).astype(jnp.int32)
+
+    chip_rows = 2 * span
+    groups = chip_rows // GROUP
+
+    def scratch(width, spans):
+        return [
+            pltpu.VMEM((depth, width), BF16),
+            pltpu.VMEM((spans, chip_rows + 8, LANES), F32),
+        ]
+
+    width = chunks[0][0].shape[1]
+    extra = len(PAIRS[0])
+    bc, x0, cq, kq, kt, ca, tot = pl.pallas_call(
+        first_kernel,
+        in_specs=[SMEM] + [VMEM] * 6,
+        out_specs=[VMEM] * 7,
+        scratch_shapes=scratch(width, 1 + extra) + [pltpu.VMEM((chip_rows, LANES), F32)],
+        out_shape=[
+            jax.ShapeDtypeStruct((chip_rows, LANES), BF16),
+            jax.ShapeDtypeStruct((chip_rows, extra * LANES), BF16),
+            jax.ShapeDtypeStruct((chip_rows, LANES), F32),
+            jax.ShapeDtypeStruct((chip_rows, LANES), F32),
+            jax.ShapeDtypeStruct((groups, 32, GROUP), F32),
+            jax.ShapeDtypeStruct((chip_rows, LANES), F32),
+            jax.ShapeDtypeStruct((8, LANES), F32),
+        ],
+        compiler_params=params(24),
+        cost_estimate=pl.CostEstimate(
+            flops=2 * chip_rows * depth * width, bytes_accessed=9000000, transcendentals=500000
+        ),
+        name="first",
+    )(ints, own, other, *chunks[0], taps[:, : (1 + extra) * LANES], rates)
+
+    bc_other = swapped(bc, (1, 1))
+    b = jnp.where(core == 0, bc, bc_other)
+    c = jnp.where(core == 0, bc_other, bc)
+
+    def scanned(index):
+        chunk = chunks[index]
+        more = extra if index == 1 else 0
+        held = (PAIRS[0] if more else ()) + PAIRS[index]
+        pairs = len(held)
+        new = pairs - more
+        firsts = [first_head(p, share) for p in held]
+        tap_at, skip_at = (1 + PAIRS[index][0]) * LANES, held[0] * LANES
+        width = chunk[0].shape[1]
+        return pl.pallas_call(
+            functools.partial(scan_kernel, index, firsts, more),
+            in_specs=[SMEM] + [VMEM] * 13,
+            out_specs=[VMEM] * 3,
+            scratch_shapes=scratch(width, new) + [pltpu.VMEM((LANES, pairs * LANES), F32)],
+            out_shape=[
+                jax.ShapeDtypeStruct((chip_rows, pairs * LANES), F32),
+                jax.ShapeDtypeStruct((LANES, pairs * LANES), F32),
+                jax.ShapeDtypeStruct((LANES + 16, pairs * LANES), BF16),
+            ],
+            compiler_params=params(28),
+            cost_estimate=pl.CostEstimate(
+                flops=2 * chip_rows * depth * width + pairs * 600000000,
+                bytes_accessed=12000000,
+                transcendentals=pairs * 400000,
+            ),
+            name="scan",
+        )(
+            ints, own, other, *chunk, taps[:, tap_at : tap_at + new * LANES],
+            x0, b, c, cq, kq, kt, tot, skip[:, skip_at : skip_at + pairs * LANES],
+        )
+
+    def joined(held, ys, ss, r):
+        pairs = len(held)
+        halves = [(i, i + 1) for i in range(0, pairs, 2)]
+        sizes = [y.shape[1] // LANES for y in ys]
+        return pl.pallas_call(
+            functools.partial(join_kernel, [first_head(p, share) for p in held], sizes, halves),
+            in_specs=[SMEM] + [VMEM] * (4 + 2 * len(ys)),
+            out_specs=[VMEM] * 3,
+            out_shape=[
+                jax.ShapeDtypeStruct((span, pairs * LANES), F32),
+                jax.ShapeDtypeStruct((span, pairs * LANES), F32),
+                jax.ShapeDtypeStruct((len(halves) * LANES, nstate), BF16),
+            ],
+            compiler_params=params(28),
+            cost_estimate=pl.CostEstimate(
+                flops=4 * chip_rows * LANES * pairs * LANES,
+                bytes_accessed=chip_rows * pairs * LANES * 8,
+                transcendentals=chip_rows * pairs * LANES,
+            ),
+            name="join",
+        )(ints, c, ca, tot, r, *ys, *ss)
+
+    wanted = jnp.sum(jnp.where(deal == req_index, slots, 0))
+    partner_wanted = jnp.sum(jnp.where(deal == (req_index ^ 1), slots, 0))
+
+    def delivered(block):
+        one = swapped(block, (16, 16))
+        pair = jnp.stack([block, one])
+        two = swapped(pair, (8, 8))
+
+        def pick(row):
+            rel = row ^ req_index
+            far, near = (rel >> 2) & 1, (rel >> 1) & 1
+            return jnp.where(
+                near == 1,
+                jnp.where(far == 1, two[1], two[0]),
+                jnp.where(far == 1, one, block),
+            )
+
+        three = swapped(pick(partner_wanted), (4, 4))
+        odd = (wanted ^ req_index) & 1
+        return jnp.where(odd == 1, three, pick(wanted)).astype(F32)
+
+    y1, s1, t1 = scanned(1)
+    y2, s2, t2 = scanned(2)
+    r12 = swapped(jnp.concatenate([t1, t2], axis=1), (2, 2))
+    first_pairs = PAIRS[0] + PAIRS[1] + PAIRS[2]
+    send_a, keep_a, fin_a = joined(first_pairs, (y1, y2), (s1, s2), r12)
+    got_a = swapped(send_a, (1, 1))
+    final_a = delivered(fin_a)
+    y3, s3, t3 = scanned(3)
+    r3 = swapped(t3, (2, 2))
+    send_b, keep_b, fin_b = joined(PAIRS[3], (y3,), (s3,), r3)
+    got_b = swapped(send_b, (1, 1))
+    final_b = delivered(fin_b)
+
+    final_state = jnp.concatenate([final_a, final_b], axis=0).reshape(1, share, head_dim, nstate)
+    places = [
+        [(p % 2) * (2 * quarter // LANES) + p // 2 for p in held]
+        for held in (first_pairs, PAIRS[3])
+    ]
+    block = span // 4
+    result = pl.pallas_call(
+        functools.partial(norm_kernel, places),
+        grid_spec=pltpu.PrefetchScalarGridSpec(
+            num_scalar_prefetch=1,
+            grid=(span // block,),
+            in_specs=[pl.BlockSpec((1, inner), lambda i, ints: (0, 0))]
+            + [
+                pl.BlockSpec((block, a.shape[1]), lambda i, ints: (i, 0))
+                for a in (keep_a, keep_b, got_a, got_b)
+            ],
+            out_specs=pl.BlockSpec((block, inner), lambda i, ints: (i, 0)),
+        ),
+        out_shape=jax.ShapeDtypeStruct((span, inner), BF16),
+        compiler_params=params(24),
+        cost_estimate=pl.CostEstimate(
+            flops=6 * span * inner, bytes_accessed=6 * span * inner, transcendentals=span
+        ),
+        name="norm",
+    )(ints, norm_gain[None], keep_a, keep_b, got_a, got_b)
+    return (result[None], final_state)
 
 
 def passed_along(block, axis, distance):
@@ -33,7 +538,7 @@
     return lax.psum(jnp.where(mine, x, jnp.zeros_like(x)), axis)
 
 
-def on_device(
+def on_device_general(
     tokens,
     mix_weight,
     step_weight,
@@ -151,23 +656,16 @@
 
 
 def solution(mesh):
+    fits = mesh.shape["req"] == 8 and mesh.shape["seq"] == 4
     return jax.shard_map(
-        on_device,
+        on_device if fits else on_device_general,
         mesh=mesh,
         in_specs=(
             P("req", "seq", None),
             P(("req", "seq"), None),
             P(("req", "seq"), None),
-            P(),
-            P(),
-            P(),
-            P(),
-            P(),
-            P(),
-            P(),
-            P(),
-            P(),
-        ),
+        )
+        + (P(),) * 9,
         out_specs=(P("req", "seq", None), P("req", "seq", None, None)),
         check_vma=False,
     )

time: 342 us -> 159 us (0.46)
  waiting for transfers between devices: 151 us -> 42.6 us
  blocking collectives: 52 us -> 0 us
  starting transfers between devices: 2.32 us -> 48 us
  local copies, waits for them, and re-layouts: 47.6 us -> 9.45 us
  matrix products: 35.4 us -> 0 us
  Pallas kernels: 0 us -> 32.7 us
  other arithmetic: 35.7 us -> 22 us
  between operations: 15.9 us -> 3.61 us
    all_gather x3 -> x0, waiting for transfers between devices: 107 us -> none  [the longest x1 56.1 us: on_device(): lax.all_gather(mix_weight, ('req', 'seq'), axis=0, tiled=True)]
    ppermute x1 -> x30, starting transfers between devices: 2.16 us -> 48 us  [the longest x29 44.8 us: swapped(): return lax.ppermute(x, AXES, [(i, i ^ masks[i % 2]) for i in range(count)])]
    all_gather x1 -> x0, blocking collectives: 45.1 us -> none  [on_device(): lax.all_gather(step_weight, ('req', 'seq'), axis=0, tiled=True)]
    psum x1 -> x0, waiting for transfers between devices: 42.8 us -> none  [broadcast(): return lax.psum(jnp.where(mine, x, jnp.zeros_like(x)), axis)]
    ppermute x1 -> x30, waiting for transfers between devices: 0.6 us -> 42.6 us  [the longest x29 42.6 us: swapped(): return lax.ppermute(x, AXES, [(i, i ^ masks[i % 2]) for i in range(count)])]
    dot_general x9 -> x0, matrix products: 35.4 us -> none  [the longest x1 11.5 us: on_device(): mixed = jnp.dot(rows, whole_mix, preferred_element_type=jnp.float32)]
    pallas_call x0 -> x7, Pallas kernels: none -> 32.7 us  [the longest x3 17 us: scanned(): pl.pallas_call(functools.partial(scan_kernel, index, firsts, more), in_sp...]
    reshape x3 -> x1, local copies, waits for them, and re-layouts: 18.4 us -> 0.07 us  [on_device(): jnp.repeat(skip_gain, head_dim)]
  transfers between devices with their start and end apart: 5 -> 30, of which waited for: 5 -> 14; matrix products, arithmetic and copies ran while one was open for 13% -> 17% of each run, Pallas kernels for 0% -> 18%
where the time goes in v2:
time: 159 us; the launch traced here: 158 us
  starting transfers between devices  48 us (30%)
  waiting for transfers between devices  42.6 us (27%)
  Pallas kernels  32.7 us (21%)
  other arithmetic  22 us (14%)
  local copies, waits for them, and re-layouts  9.45 us (6%)
  between operations  3.61 us (2%)
    ppermute x29, starting transfers between devices, swapped(): return lax.ppermute(x, AXES, [(i, i ^ masks[i % 2]) for i in range(count)])  44.8 us
    ppermute x29, waiting for transfers between devices, swapped(): return lax.ppermute(x, AXES, [(i, i ^ masks[i % 2]) for i in range(count)])  42.6 us
    pallas_call x3, Pallas kernels, scanned(): pl.pallas_call(functools.partial(scan_kernel, index, firsts, more), in_sp...  17 us
    concatenate x12, other arithmetic, gathered(): block = jnp.concatenate([block, swapped(block, mask)], axis=0)  12 us
    pallas_call x2, Pallas kernels, joined(): pl.pallas_call(functools.partial(join_kernel, [first_head(p, share) for p...  5.62 us
    pallas_call x1, Pallas kernels, on_device(): pl.pallas_call(first_kernel, in_specs=[SMEM] + [VMEM] * 6, out_specs=[VME...  5.12 us
    pallas_call x1, Pallas kernels, on_device(): pl.pallas_call(functools.partial(norm_kernel, places), grid_spec=pltpu.Pr...  4.95 us
    ppermute x1, starting transfers between devices, on_device(): lax.ppermute(last_rows, AXES, [(i, i + 2) for i in range(count) if i // 2...  3.27 us
  transfers between devices with their start and end apart: 30, of which 14 were waited for; matrix products, arithmetic and copies ran while one was open for 17% of the time, Pallas kernels for 18%

profile of v2, /device:TPU:0, one launch (start us, length us, event | category | flops | bytes accessed | tf_op | source)
XLA Modules:
  0.0 158.4 jit_solution(1611173807802621759)
XLA Ops:
  11.9 4.0 %collective-permute-start.3 = (bf16[160,384]{1,0:T(8,128)(2,1)}, bf16[160,384]{1,0:T(8,128)(2,1)}, u32[]{:S(2)}, u32[]{:S(2)}) collective-permute-start(bf16[160,384]{1,0:T(8,128)(2,1)} %get-tuple-element.52), channel_id=1, source_target_pairs={{0,16},{1,17},{2,18},{3,19},{4,20},{5,21},{6,22},{7,23},{8,24},{9,... | collective-permute-start | bytes 368648 | tf_op jit(solution)/shard_map/ppermute | solution.py:264
  16.1 2.9 %collective-permute-start.8 = (bf16[160,384]{1,0:T(8,128)(2,1)S(1)}, bf16[160,384]{1,0:T(8,128)(2,1)}, u32[]{:S(2)}, u32[]{:S(2)}) collective-permute-start(bf16[160,384]{1,0:T(8,128)(2,1)S(1)} %get-tuple-element.51), channel_id=1, source_target_pairs={{0,16},{1,17},{2,18},{3,19},{4,20},{5,21},{6,22},{7,23},{8,24},{9,... | collective-permute-start | bytes 368648 | tf_op jit(solution)/shard_map/ppermute | solution.py:264
  18.9 10.2 %collective-permute-done.3 = bf16[160,384]{1,0:T(8,128)(2,1)} collective-permute-done((bf16[160,384]{1,0:T(8,128)(2,1)}, bf16[160,384]{1,0:T(8,128)(2,1)}, u32[]{:S(2)}, u32[]{:S(2)}) %collective-permute-start.3) | collective-permute-done | bytes 122912 | tf_op jit(solution)/shard_map/ppermute | solution.py:264
  48.7 3.1 %collective-permute-start.17 = (bf16[160,256]{1,0:T(8,128)(2,1)S(1)}, bf16[160,256]{1,0:T(8,128)(2,1)S(1)}, u32[]{:S(2)}, u32[]{:S(2)}) collective-permute-start(bf16[160,256]{1,0:T(8,128)(2,1)S(1)} %slice.249), channel_id=1, source_target_pairs={{0,16},{1,17},{2,18},{3,19},{4,20},{5,21},{6,22},{7,23},{8,24},{9,... | collective-permute-start | bytes 245768 | tf_op jit(solution)/shard_map/ppermute | solution.py:264
  51.8 3.8 %collective-permute-done.17 = bf16[160,256]{1,0:T(8,128)(2,1)S(1)} collective-permute-done((bf16[160,256]{1,0:T(8,128)(2,1)S(1)}, bf16[160,256]{1,0:T(8,128)(2,1)S(1)}, u32[]{:S(2)}, u32[]{:S(2)}) %collective-permute-start.17) | collective-permute-done | bytes 81952 | tf_op jit(solution)/shard_map/ppermute | solution.py:264
  63.5 3.3 %collective-permute-start.1 = (bf16[16,2560]{1,0:T(8,128)(2,1)S(1)}, bf16[16,2560]{1,0:T(8,128)(2,1)S(1)}, u32[]{:S(2)}, u32[]{:S(2)}) collective-permute-start(bf16[16,2560]{1,0:T(8,128)(2,1)S(1)} %slice_select_fusion), channel_id=1, source_target_pairs={{0,2},{1,3},{4,6},{5,7},{8,10},{9,11},{12,14},{13,15},{16,18},{17,... | collective-permute-start | bytes 245768 | tf_op jit(solution)/shard_map/ppermute | solution.py:332
  66.8 4.8 %collective-permute-done.10 = bf16[640,384]{1,0:T(8,128)(2,1)S(1)} collective-permute-done((bf16[640,384]{1,0:T(8,128)(2,1)S(1)}, bf16[640,384]{1,0:T(8,128)(2,1)S(1)}, u32[]{:S(2)}, u32[]{:S(2)}) %collective-permute-start.10) | collective-permute-done | bytes 491552 | tf_op jit(solution)/shard_map/ppermute | solution.py:264
  75.0 5.1 %first.1 = (bf16[1024,128]{1,0:T(8,128)(2,1)S(1)}, bf16[1024,128]{1,0:T(8,128)(2,1)S(1)}, f32[1024,128]{1,0:T(8,128)S(1)}, f32[1024,128]{1,0:T(8,128)S(1)}, f32[...) custom-call(s32[72]{0:T(128)S(1)} %stack.189.ints, ...), custom_call_target="tpu_custom_call" | custom-call | flops 2013265920 | bytes 9000000 | tf_op jit(solution)/shard_map/first/pallas_call | solution.py:377
  80.1 4.4 %collective-permute-start.7 = (bf16[1024,128]{1,0:T(8,128)(2,1)S(1)}, bf16[1024,128]{1,0:T(8,128)(2,1)S(1)}, u32[]{:S(2)}, u32[]{:S(2)}) collective-permute-start(bf16[1024,128]{1,0:T(8,128)(2,1)S(1)} %get-tuple-element.24), channel_id=1, source_target_pairs={{0,1},{1,0},{2,3},{3,2},{4,5},{5,4},{6,7},{7,6},{8,9},{9,8},{10,11... | collective-permute-start | bytes 786440 | tf_op jit(solution)/shard_map/ppermute | solution.py:264
  84.6 2.9 %collective-permute-start.19 = (bf16[640,256]{1,0:T(8,128)(2,1)S(1)}, bf16[640,256]{1,0:T(8,128)(2,1)S(1)}, u32[]{:S(2)}, u32[]{:S(2)}) collective-permute-start(bf16[640,256]{1,0:T(8,128)(2,1)S(1)} %pad_maximum_fusion.9), channel_id=1, source_target_pairs={{0,8},{1,3},{2,10},{3,1},{4,12},{5,7},{6,14},{7,5},{8,0},{9,11},{1... | collective-permute-start | bytes 983048 | tf_op jit(solution)/shard_map/ppermute | solution.py:264
  89.0 6.6 %scan.4 = (f32[1024,512]{1,0:T(8,128)S(1)}, f32[128,512]{1,0:T(8,128)S(1)}, bf16[144,512]{1,0:T(8,128)(2,1)S(1)}) custom-call(s32[72]{0:T(128)S(1)} %stack.189.ints, bf16[528,2560]{1,0:T(8,128)(2,1)S(1)} %pad_maximum_fusion.own, bf16[512,2560]{1,0:T(8,128)(2,1)S(1)} %collective-permute-done.other, bf16[1280,512]{1,0:T(8,128)(2,1)S(1)} %pad_maximum_fusion.1.low, ...), custom_call_target="tpu_custom_call" | custom-call | flops 5084354560 | bytes 12000000 | tf_op jit(solution)/shard_map/scan/pallas_call | solution.py:411
  95.7 6.6 %scan.3 = (f32[1024,512]{1,0:T(8,128)S(1)}, f32[128,512]{1,0:T(8,128)S(1)}, bf16[144,512]{1,0:T(8,128)(2,1)S(1)}) custom-call(s32[72]{0:T(128)S(1)} %stack.189.ints, bf16[528,2560]{1,0:T(8,128)(2,1)S(1)} %pad_maximum_fusion.own, bf16[512,2560]{1,0:T(8,128)(2,1)S(1)} %collective-permute-done.other, bf16[1280,384]{1,0:T(8,128)(2,1)S(1)} %pad_maximum_fusion.3.low, ...), custom_call_target="tpu_custom_call" | custom-call | flops 4413265920 | bytes 12000000 | tf_op jit(solution)/shard_map/scan/pallas_call | solution.py:411
  104.5 4.7 %collective-permute-done.16.r_ref = bf16[144,1024]{1,0:T(8,128)(2,1)S(1)} collective-permute-done((bf16[144,1024]{1,0:T(8,128)(2,1)S(1)}, bf16[144,1024]{1,0:T(8,128)(2,1)S(1)}, u32[]{:S(2)}, u32[]{:S(2)}) %collective-permute-start.16) | collective-permute-done | bytes 294944 | tf_op jit(solution)/shard_map/ppermute | solution.py:264
  109.2 4.3 %join.2 = (f32[512,1024]{1,0:T(8,128)}, f32[512,1024]{1,0:T(8,128)S(1)}, bf16[512,128]{1,0:T(8,128)(2,1)S(1)}) custom-call(s32[72]{0:T(128)S(1)} %stack.189.ints, bf16[1024,128]{1,0:T(8,128)(2,1)S(1)} %get-tuple-element.50.c_ref, f32[1024,128]{1,0:T(8,128)S(1)} %get-tuple-element.25.ca_ref, f32[8,128]{1,0:T(8,128)S(1)} %get-tuple-element.26.tot_ref, ...), custom_call_target="tpu_custom_call" | custom-call | flops 536870912 | bytes 8388608 | tf_op jit(solution)/shard_map/join/pallas_call | solution.py:437
  113.6 2.6 %collective-permute-done.20.high = bf16[1280,256]{1,0:T(8,128)(2,1)S(1)} collective-permute-done((bf16[1280,256]{1,0:T(8,128)(2,1)S(1)}, bf16[1280,256]{1,0:T(8,128)(2,1)S(1)}, u32[]{:S(2)}, u32[]{:S(2)}) %collective-permute-start.20) | collective-permute-done | bytes 655392 | tf_op jit(solution)/shard_map/ppermute | solution.py:264
  116.3 3.8 %scan.5 = (f32[1024,256]{1,0:T(8,128)S(1)}, f32[128,256]{1,0:T(8,128)S(1)}, bf16[144,256]{1,0:T(8,128)(2,1)S(1)}) custom-call(s32[72]{0:T(128)S(1)} %stack.189.ints, bf16[528,2560]{1,0:T(8,128)(2,1)S(1)} %pad_maximum_fusion.own, bf16[512,2560]{1,0:T(8,128)(2,1)S(1)} %copy-done.1, bf16[1280,256]{1,0:T(8,128)(2,1)S(1)} %pad_maximum_fusion.5.low, ...), custom_call_target="tpu_custom_call" | custom-call | flops 2542177280 | bytes 12000000 | tf_op jit(solution)/shard_map/scan/pallas_call | solution.py:411
  121.8 2.7 %collective-permute-done.21.r_ref = bf16[144,256]{1,0:T(8,128)(2,1)S(1)} collective-permute-done((bf16[144,256]{1,0:T(8,128)(2,1)S(1)}, bf16[144,256]{1,0:T(8,128)(2,1)S(1)}, u32[]{:S(2)}, u32[]{:S(2)}) %collective-permute-start.21) | collective-permute-done | bytes 73760 | tf_op jit(solution)/shard_map/ppermute | solution.py:264
  125.8 5.6 %collective-permute-start.27 = (bf16[128,128]{1,0:T(8,128)(2,1)S(1)}, bf16[128,128]{1,0:T(8,128)(2,1)S(1)}, u32[]{:S(2)}, u32[]{:S(2)}) collective-permute-start(bf16[128,128]{1,0:T(8,128)(2,1)S(1)} %get-tuple-element.45), channel_id=1, source_target_pairs={{0,16},{1,17},{2,18},{3,19},{4,20},{5,21},{6,22},{7,23},{8,24},{9,... | collective-permute-start | bytes 98312 | tf_op jit(solution)/shard_map/ppermute | solution.py:264
  131.5 3.5 %collective-permute-done.27 = bf16[128,128]{1,0:T(8,128)(2,1)S(1)} collective-permute-done((bf16[128,128]{1,0:T(8,128)(2,1)S(1)}, bf16[128,128]{1,0:T(8,128)(2,1)S(1)}, u32[]{:S(2)}, u32[]{:S(2)}) %collective-permute-start.27) | collective-permute-done | bytes 32800 | tf_op jit(solution)/shard_map/ppermute | solution.py:264
  138.1 2.4 %collective-permute-start.25 = (bf16[2,512,128]{2,1,0:T(8,128)(2,1)}, bf16[2,512,128]{2,1,0:T(8,128)(2,1)}, u32[]{:S(2)}, u32[]{:S(2)}) collective-permute-start(bf16[2,512,128]{2,1,0:T(8,128)(2,1)} %pad_maximum_fusion.11), channel_id=1, source_target_pairs={{0,8},{1,9},{2,10},{3,11},{4,12},{5,13},{6,14},{7,15},{8,0},{9,1},... | collective-permute-start | bytes 786440 | tf_op jit(solution)/shard_map/ppermute | solution.py:264
  142.5 2.6 %collective-permute-done.25 = bf16[2,512,128]{2,1,0:T(8,128)(2,1)} collective-permute-done((bf16[2,512,128]{2,1,0:T(8,128)(2,1)}, bf16[2,512,128]{2,1,0:T(8,128)(2,1)}, u32[]{:S(2)}, u32[]{:S(2)}) %collective-permute-start.25) | collective-permute-done | bytes 262176 | tf_op jit(solution)/shard_map/ppermute | solution.py:264
  146.1 2.6 %collective-permute-start.26 = (bf16[512,128]{1,0:T(8,128)(2,1)S(1)}, bf16[512,128]{1,0:T(8,128)(2,1)S(1)}, u32[]{:S(2)}, u32[]{:S(2)}) collective-permute-start(bf16[512,128]{1,0:T(8,128)(2,1)S(1)} %bitcast_select_fusion.1), channel_id=1, source_target_pairs={{0,4},{1,5},{2,6},{3,7},{4,0},{5,1},{6,2},{7,3},{8,12},{9,13},{10,... | collective-permute-start | bytes 393224 | tf_op jit(solution)/shard_map/ppermute | solution.py:264
  148.7 2.9 %collective-permute-done.26 = bf16[512,128]{1,0:T(8,128)(2,1)S(1)} collective-permute-done((bf16[512,128]{1,0:T(8,128)(2,1)S(1)}, bf16[512,128]{1,0:T(8,128)(2,1)S(1)}, u32[]{:S(2)}, u32[]{:S(2)}) %collective-permute-start.26) | collective-permute-done | bytes 131104 | tf_op jit(solution)/shard_map/ppermute | solution.py:264
  153.4 4.9 %norm.1 = bf16[512,2560]{1,0:T(8,128)(2,1)} custom-call(s32[72]{0:T(128)S(1)} %stack.189.ints, f32[1,2560]{1,0:T(1,128)S(1)} %broadcast_in_dim.40.gain_ref, f32[512,1024]{1,0:T(8,128)S(1)} %get-tuple-element.37.ka_ref, f32[512,256]{1,0:T(8,128)S(1)} %get-tuple-element.41.kb_ref, f32[512,1024]{1,0:T(8,128)} %collective-permute-done.22.ra_ref, ...), custom_call_target="tpu_custom_call" | custom-call | flops 7864320 | bytes 7864320 | tf_op jit(solution)/shard_map/norm/pallas_call | solution.py:495
  (149 shorter events, 54.4 us)
Async XLA Ops:
  4.3 59.2 %collective-permute-start = (bf16[512,2560]{1,0:T(8,128)(2,1)}, bf16[512,2560]{1,0:T(8,128)(2,1)S(1)}, u32[]{:S(2)}, u32[]{:S(2)}) collective-permute-start(bf16[512,2560]{1,0:T(8,128)(2,1)} %bitcast.68), channel_id=1, source_target_pairs={{0,1},{1,0},{2,3},{3,2},{4,5},{5,4},{6,7},{7,6},{8,9},{9,8},{10,11... | collective-permute-start | bytes 7864328 | tf_op jit(solution)/shard_map/ppermute | solution.py:264
  11.9 17.2 %collective-permute-start.3 = (bf16[160,384]{1,0:T(8,128)(2,1)}, bf16[160,384]{1,0:T(8,128)(2,1)}, u32[]{:S(2)}, u32[]{:S(2)}) collective-permute-start(bf16[160,384]{1,0:T(8,128)(2,1)} %get-tuple-element.52), channel_id=1, source_target_pairs={{0,16},{1,17},{2,18},{3,19},{4,20},{5,21},{6,22},{7,23},{8,24},{9,... | collective-permute-start | bytes 368648 | tf_op jit(solution)/shard_map/ppermute | solution.py:264
  15.9 16.8 %collective-permute-start.12 = (bf16[160,512]{1,0:T(8,128)(2,1)S(1)}, bf16[160,512]{1,0:T(8,128)(2,1)}, u32[]{:S(2)}, u32[]{:S(2)}) collective-permute-start(bf16[160,512]{1,0:T(8,128)(2,1)S(1)} %slice.244), channel_id=1, source_target_pairs={{0,16},{1,17},{2,18},{3,19},{4,20},{5,21},{6,22},{7,23},{8,24},{9,... | collective-permute-start | bytes 491528 | tf_op jit(solution)/shard_map/ppermute | solution.py:264
  16.1 20.9 %collective-permute-start.8 = (bf16[160,384]{1,0:T(8,128)(2,1)S(1)}, bf16[160,384]{1,0:T(8,128)(2,1)}, u32[]{:S(2)}, u32[]{:S(2)}) collective-permute-start(bf16[160,384]{1,0:T(8,128)(2,1)S(1)} %get-tuple-element.51), channel_id=1, source_target_pairs={{0,16},{1,17},{2,18},{3,19},{4,20},{5,21},{6,22},{7,23},{8,24},{9,... | collective-permute-start | bytes 368648 | tf_op jit(solution)/shard_map/ppermute | solution.py:264
  30.1 8.5 %collective-permute-start.4 = (bf16[320,384]{1,0:T(8,128)(2,1)S(1)}, bf16[320,384]{1,0:T(8,128)(2,1)S(1)}, u32[]{:S(2)}, u32[]{:S(2)}) collective-permute-start(bf16[320,384]{1,0:T(8,128)(2,1)S(1)} %pad_maximum_fusion.12), channel_id=1, source_target_pairs={{0,2},{1,9},{2,0},{3,11},{4,6},{5,13},{6,4},{7,15},{8,10},{9,1},{1... | collective-permute-start | bytes 737288 | tf_op jit(solution)/shard_map/ppermute | solution.py:264
  33.6 7.1 %collective-permute-start.13 = (bf16[320,512]{1,0:T(8,128)(2,1)S(1)}, bf16[320,512]{1,0:T(8,128)(2,1)S(1)}, u32[]{:S(2)}, u32[]{:S(2)}) collective-permute-start(bf16[320,512]{1,0:T(8,128)(2,1)S(1)} %pad_maximum_fusion.8), channel_id=1, source_target_pairs={{0,4},{1,9},{2,6},{3,11},{4,0},{5,13},{6,2},{7,15},{8,12},{9,1},{1... | collective-permute-start | bytes 983048 | tf_op jit(solution)/shard_map/ppermute | solution.py:264
  38.6 17.3 %collective-permute-start.9 = (bf16[320,384]{1,0:T(8,128)(2,1)}, bf16[320,384]{1,0:T(8,128)(2,1)}, u32[]{:S(2)}, u32[]{:S(2)}) collective-permute-start(bf16[320,384]{1,0:T(8,128)(2,1)} %pad_maximum_fusion.13), channel_id=1, source_target_pairs={{0,8},{1,3},{2,10},{3,1},{4,12},{5,7},{6,14},{7,5},{8,0},{9,11},{1... | collective-permute-start | bytes 737288 | tf_op jit(solution)/shard_map/ppermute | solution.py:264
  40.5 18.3 %collective-permute-start.5 = (bf16[640,384]{1,0:T(8,128)(2,1)}, bf16[640,384]{1,0:T(8,128)(2,1)}, u32[]{:S(2)}, u32[]{:S(2)}) collective-permute-start(bf16[640,384]{1,0:T(8,128)(2,1)} %pad_maximum_fusion.6), channel_id=1, source_target_pairs={{0,4},{1,3},{2,6},{3,1},{4,0},{5,7},{6,2},{7,5},{8,12},{9,11},{10,... | collective-permute-start | bytes 1474568 | tf_op jit(solution)/shard_map/ppermute | solution.py:264
  43.3 17.5 %collective-permute-start.14 = (bf16[640,512]{1,0:T(8,128)(2,1)}, bf16[640,512]{1,0:T(8,128)(2,1)}, u32[]{:S(2)}, u32[]{:S(2)}) collective-permute-start(bf16[640,512]{1,0:T(8,128)(2,1)} %pad_maximum_fusion.4), channel_id=1, source_target_pairs={{0,2},{1,5},{2,0},{3,7},{4,6},{5,1},{6,4},{7,3},{8,10},{9,13},{10,... | collective-permute-start | bytes 1966088 | tf_op jit(solution)/shard_map/ppermute | solution.py:264
  55.5 29.0 %collective-permute-start.18 = (bf16[320,256]{1,0:T(8,128)(2,1)S(1)}, bf16[320,256]{1,0:T(8,128)(2,1)S(1)}, u32[]{:S(2)}, u32[]{:S(2)}) collective-permute-start(bf16[320,256]{1,0:T(8,128)(2,1)S(1)} %pad_maximum_fusion.14), channel_id=1, source_target_pairs={{0,4},{1,9},{2,6},{3,11},{4,0},{5,13},{6,2},{7,15},{8,12},{9,1},{1... | collective-permute-start | bytes 491528 | tf_op jit(solution)/shard_map/ppermute | solution.py:264
  57.0 14.6 %collective-permute-start.10 = (bf16[640,384]{1,0:T(8,128)(2,1)S(1)}, bf16[640,384]{1,0:T(8,128)(2,1)S(1)}, u32[]{:S(2)}, u32[]{:S(2)}) collective-permute-start(bf16[640,384]{1,0:T(8,128)(2,1)S(1)} %pad_maximum_fusion.7), channel_id=1, source_target_pairs={{0,4},{1,9},{2,6},{3,11},{4,0},{5,13},{6,2},{7,15},{8,12},{9,1},{1... | collective-permute-start | bytes 1474568 | tf_op jit(solution)/shard_map/ppermute | solution.py:264
  60.1 14.9 %collective-permute-start.6 = (bf16[1280,384]{1,0:T(8,128)(2,1)S(1)}, bf16[1280,384]{1,0:T(8,128)(2,1)S(1)}, u32[]{:S(2)}, u32[]{:S(2)}) collective-permute-start(bf16[1280,384]{1,0:T(8,128)(2,1)S(1)} %pad_maximum_fusion.2.low), channel_id=1, source_target_pairs={{0,8},{1,5},{2,10},{3,7},{4,12},{5,1},{6,14},{7,3},{8,0},{9,13},{1... | collective-permute-start | bytes 2949128 | tf_op jit(solution)/shard_map/ppermute | solution.py:264
  62.0 27.0 %collective-permute-start.15 = (bf16[1280,512]{1,0:T(8,128)(2,1)S(1)}, bf16[1280,512]{1,0:T(8,128)(2,1)S(1)}, u32[]{:S(2)}, u32[]{:S(2)}) collective-permute-start(bf16[1280,512]{1,0:T(8,128)(2,1)S(1)} %pad_maximum_fusion.1.low), channel_id=1, source_target_pairs={{0,8},{1,3},{2,10},{3,1},{4,12},{5,7},{6,14},{7,5},{8,0},{9,11},{1... | collective-permute-start | bytes 3932168 | tf_op jit(solution)/shard_map/ppermute | solution.py:264
  63.5 10.1 %collective-permute-start.1 = (bf16[16,2560]{1,0:T(8,128)(2,1)S(1)}, bf16[16,2560]{1,0:T(8,128)(2,1)S(1)}, u32[]{:S(2)}, u32[]{:S(2)}) collective-permute-start(bf16[16,2560]{1,0:T(8,128)(2,1)S(1)} %slice_select_fusion), channel_id=1, source_target_pairs={{0,2},{1,3},{4,6},{5,7},{8,10},{9,11},{12,14},{13,15},{16,18},{17,... | collective-permute-start | bytes 245768 | tf_op jit(solution)/shard_map/ppermute | solution.py:332
  72.7 23.0 %collective-permute-start.11 = (bf16[1280,384]{1,0:T(8,128)(2,1)S(1)}, bf16[1280,384]{1,0:T(8,128)(2,1)S(1)}, u32[]{:S(2)}, u32[]{:S(2)}) collective-permute-start(bf16[1280,384]{1,0:T(8,128)(2,1)S(1)} %pad_maximum_fusion.3.low), channel_id=1, source_target_pairs={{0,2},{1,5},{2,0},{3,7},{4,6},{5,1},{6,4},{7,3},{8,10},{9,13},{10,... | collective-permute-start | bytes 2949128 | tf_op jit(solution)/shard_map/ppermute | solution.py:264
  80.1 7.4 %collective-permute-start.7 = (bf16[1024,128]{1,0:T(8,128)(2,1)S(1)}, bf16[1024,128]{1,0:T(8,128)(2,1)S(1)}, u32[]{:S(2)}, u32[]{:S(2)}) collective-permute-start(bf16[1024,128]{1,0:T(8,128)(2,1)S(1)} %get-tuple-element.24), channel_id=1, source_target_pairs={{0,1},{1,0},{2,3},{3,2},{4,5},{5,4},{6,7},{7,6},{8,9},{9,8},{10,11... | collective-permute-start | bytes 786440 | tf_op jit(solution)/shard_map/ppermute | solution.py:264
  84.6 19.3 %collective-permute-start.19 = (bf16[640,256]{1,0:T(8,128)(2,1)S(1)}, bf16[640,256]{1,0:T(8,128)(2,1)S(1)}, u32[]{:S(2)}, u32[]{:S(2)}) collective-permute-start(bf16[640,256]{1,0:T(8,128)(2,1)S(1)} %pad_maximum_fusion.9), channel_id=1, source_target_pairs={{0,8},{1,3},{2,10},{3,1},{4,12},{5,7},{6,14},{7,5},{8,0},{9,11},{1... | collective-permute-start | bytes 983048 | tf_op jit(solution)/shard_map/ppermute | solution.py:264
  102.3 6.9 %collective-permute-start.16 = (bf16[144,1024]{1,0:T(8,128)(2,1)S(1)}, bf16[144,1024]{1,0:T(8,128)(2,1)S(1)}, u32[]{:S(2)}, u32[]{:S(2)}) collective-permute-start(bf16[144,1024]{1,0:T(8,128)(2,1)S(1)} %pad_maximum_fusion.10), channel_id=1, source_target_pairs={{0,2},{1,3},{2,0},{3,1},{4,6},{5,7},{6,4},{7,5},{8,10},{9,11},{10,... | collective-permute-start | bytes 884744 | tf_op jit(solution)/shard_map/ppermute | solution.py:264
  103.9 12.3 %collective-permute-start.20 = (bf16[1280,256]{1,0:T(8,128)(2,1)S(1)}, bf16[1280,256]{1,0:T(8,128)(2,1)S(1)}, u32[]{:S(2)}, u32[]{:S(2)}) collective-permute-start(bf16[1280,256]{1,0:T(8,128)(2,1)S(1)} %pad_maximum_fusion.5.low), channel_id=1, source_target_pairs={{0,2},{1,5},{2,0},{3,7},{4,6},{5,1},{6,4},{7,3},{8,10},{9,13},{10,... | collective-permute-start | bytes 1966088 | tf_op jit(solution)/shard_map/ppermute | solution.py:264
  113.6 39.9 %collective-permute-start.22 = (f32[512,1024]{1,0:T(8,128)}, f32[512,1024]{1,0:T(8,128)}, u32[]{:S(2)}, u32[]{:S(2)}) collective-permute-start(f32[512,1024]{1,0:T(8,128)} %get-tuple-element.42), channel_id=1, source_target_pairs={{0,1},{1,0},{2,3},{3,2},{4,5},{5,4},{6,7},{7,6},{8,9},{9,8},{10,11... | collective-permute-start | bytes 6291464 | tf_op jit(solution)/shard_map/ppermute | solution.py:264
  125.8 9.2 %collective-permute-start.27 = (bf16[128,128]{1,0:T(8,128)(2,1)S(1)}, bf16[128,128]{1,0:T(8,128)(2,1)S(1)}, u32[]{:S(2)}, u32[]{:S(2)}) collective-permute-start(bf16[128,128]{1,0:T(8,128)(2,1)S(1)} %get-tuple-element.45), channel_id=1, source_target_pairs={{0,16},{1,17},{2,18},{3,19},{4,20},{5,21},{6,22},{7,23},{8,24},{9,... | collective-permute-start | bytes 98312 | tf_op jit(solution)/shard_map/ppermute | solution.py:264
  138.1 7.0 %collective-permute-start.25 = (bf16[2,512,128]{2,1,0:T(8,128)(2,1)}, bf16[2,512,128]{2,1,0:T(8,128)(2,1)}, u32[]{:S(2)}, u32[]{:S(2)}) collective-permute-start(bf16[2,512,128]{2,1,0:T(8,128)(2,1)} %pad_maximum_fusion.11), channel_id=1, source_target_pairs={{0,8},{1,9},{2,10},{3,11},{4,12},{5,13},{6,14},{7,15},{8,0},{9,1},... | collective-permute-start | bytes 786440 | tf_op jit(solution)/shard_map/ppermute | solution.py:264
  141.7 11.8 %collective-permute-start.23 = (f32[512,256]{1,0:T(8,128)S(1)}, f32[512,256]{1,0:T(8,128)S(1)}, u32[]{:S(2)}, u32[]{:S(2)}) collective-permute-start(f32[512,256]{1,0:T(8,128)S(1)} %get-tuple-element.43), channel_id=1, source_target_pairs={{0,1},{1,0},{2,3},{3,2},{4,5},{5,4},{6,7},{7,6},{8,9},{9,8},{10,11... | collective-permute-start | bytes 1572872 | tf_op jit(solution)/shard_map/ppermute | solution.py:264
  141.8 6.9 %collective-permute-start.29 = (bf16[128,128]{1,0:T(8,128)(2,1)S(1)}, bf16[128,128]{1,0:T(8,128)(2,1)S(1)}, u32[]{:S(2)}, u32[]{:S(2)}) collective-permute-start(bf16[128,128]{1,0:T(8,128)(2,1)S(1)} %bitcast_select_fusion.3), channel_id=1, source_target_pairs={{0,4},{1,5},{2,6},{3,7},{4,0},{5,1},{6,2},{7,3},{8,12},{9,13},{10,... | collective-permute-start | bytes 98312 | tf_op jit(solution)/shard_map/ppermute | solution.py:264
  (24 other events, 259.0 us)

commit v3 on v2

--- a/solution.py
+++ b/solution.py
@@ -18,6 +18,12 @@
 FLIPS = {"a": 16, "b": 8, "y": 4, "x": 2}
 ROUTES = (("axyb", "abxy"), ("abyx", "axby"), ("ayxb", "abyx"), ("aybx", "abxy"))
 PAIRS = ((0,), (1, 2, 3), (4, 5, 6, 7), (8, 9))
+SCHEDULE = (
+    "0.0", "1.0", "tokens", "0.1", "2.0", "1.1", "0.2", "halo", "settings", "3.0",
+    "2.1", "1.2", "0.3", "own", "3.1", "2.2", "1.3", "3.2", "2.3", "K0",
+    "3.3", "K1", "K2", "xA", "K3", "xB", "JA", "fA0", "JB", "fB0",
+    "fA1", "fB1", "fA2", "fB2", "norm", "fA3", "fB3",
+)
 VMEM = pl.BlockSpec(memory_space=pltpu.VMEM)
 SMEM = pl.BlockSpec(memory_space=pltpu.SMEM)
 
@@ -54,11 +60,16 @@
 
 def project(chunk, ints, own, other, low, high, whole, padded, raw):
     block = low.shape[0] // 8
+    start, end, first, core = ints[0], ints[1], ints[2], ints[3]
     for p in range(16):
+        one, two = (
+            sum(FLIPS[step] // 2 for i, step in enumerate(route) if (p >> i) & 1)
+            for route in ROUTES[chunk]
+        )
+        chip = jnp.bitwise_xor(ints[5], jnp.where(core == 0, one, two))
         source = low if p < 8 else high
-        row = pl.multiple_of(ints[8 + 16 * chunk + p] * block, block)
+        row = pl.multiple_of(chip * block, block)
         whole[pl.ds(row, block), :] = source[(p % 8) * block : (p % 8 + 1) * block, :]
-    start, end, first, core = ints[0], ints[1], ints[2], ints[3]
     span = other.shape[0]
     spans = [i for i in range(low.shape[1] // LANES) if raw is None or i != 1]
     mine = dot(own[...], whole[...])
@@ -169,7 +180,7 @@
             y_bottom = dot(jnp.concatenate(bottom, axis=1), jnp.concatenate([x0, x1], axis=0))
             q = jnp.where(left, spread[0], spread[1])
             xf = x.astype(F32)
-            rest = skip_ref[0:1, lanes(i)] * xf
+            rest = skip_ref[2:3, lanes(i)] * xf
             if group:
                 rest = rest + jnp.exp2(q) * carried[:, lanes(i)]
             y_out[group * GROUP : group * GROUP + half, lanes(i)] = y_top + rest[0:half]
@@ -208,18 +219,25 @@
     core = ints[3]
     where = [(j, k) for j, size in enumerate(sizes) for k in range(size)]
     span = send_out.shape[0]
-    left = lax.broadcasted_iota(jnp.int32, (span, LANES), 1) < LANES // 2
     received = r_ref[0:LANES, :].astype(F32)
     entering = (received * jnp.where(later, 1.0, 0.0)).astype(BF16)
+    from_head = lax.broadcasted_iota(jnp.int32, (2 * LANES, LANES), 0) % LANES
+    second = lax.broadcasted_iota(jnp.int32, (2 * LANES, LANES), 1) // (LANES // 2)
+    spread = jnp.concatenate(
+        [jnp.where(from_head == head + second, 1.0, 0.0).astype(BF16) for head in heads], axis=1
+    )
     for out, at in ((send_out, (1 - core) * span), (keep_out, core * span)):
         rows = pl.ds(pl.multiple_of(at, span), span)
-        c, ca = c_ref[rows, :], ca_ref[rows, :]
-        carried = dot(c, entering)
-        for i, head in enumerate(heads):
+        decay = jnp.exp2(ca_ref[rows, :])
+        decay = dot(jnp.concatenate(split(decay), axis=1), spread)
+        carried = dot(c_ref[rows, :], entering)
+        for i in range(len(heads)):
             j, k = where[i]
-            q = jnp.where(left, column(ca, head), column(ca, head + 1))
-            out[:, lanes(i)] = y_refs[j][rows, lanes(k)] + jnp.exp2(q) * carried[:, lanes(i)]
+            out[:, lanes(i)] = (
+                y_refs[j][rows, lanes(k)] + decay[:, lanes(i)] * carried[:, lanes(i)]
+            )
     side = lax.broadcasted_iota(jnp.int32, (8, LANES), 1) < LANES // 2
+    tot = tot_ref[...]
     for i, (early, late) in enumerate(halves):
 
         def own_state(p):
@@ -228,7 +246,6 @@
 
         parts = r_ref[LANES:, lanes(early)].astype(F32)
         their_total = parts[0:1] + parts[1:2] + parts[2:3]
-        tot = tot_ref[...]
         my_total = jnp.where(side, column(tot, heads[late]), column(tot, heads[late] + 1))[0:1]
         at_first = jnp.exp2(their_total) * own_state(early) + received[:, lanes(early)]
         at_last = jnp.exp2(my_total) * received[:, lanes(late)] + own_state(late)
@@ -259,6 +276,65 @@
         out_ref[:, pl.ds(at, LANES)] = (v * factor * gain_ref[0:1, pl.ds(at, LANES)]).astype(BF16)
 
 
+def head_of(lane, core, share):
+    return jnp.where(lane < 2 * share, lane + core * share + (lane // share) * share, -1)
+
+
+def chosen_heads(core, heads):
+    row = lax.broadcasted_iota(jnp.int32, (heads, LANES), 0)
+    lane = lax.broadcasted_iota(jnp.int32, (heads, LANES), 1)
+    return jnp.where(row == head_of(lane, core, heads // 4), 1.0, 0.0)
+
+
+def columns_of(source, core, inner):
+    first = inner // 4 // LANES
+    blocks = [inner // LANES + core]
+    for i in range(first):
+        blocks += [first * core + i, 2 * first + first * core + i]
+    return [source[:, pl.ds(pl.multiple_of(at * LANES, LANES), LANES)] for at in blocks]
+
+
+def sort_kernel(inner, ints, mix, step, kept_out, given_out):
+    for out, core in ((kept_out, ints[3]), (given_out, 1 - ints[3])):
+        parts = columns_of(mix, core, inner)
+        out[:, lanes(0)] = parts[0]
+        out[:, lanes(1)] = dot(step[...], chosen_heads(core, step.shape[1]).astype(BF16)).astype(BF16)
+        for i, part in enumerate(parts[1:]):
+            out[:, lanes(2 + i)] = part
+
+
+def stack_kernel(ints, kept, got, *outs):
+    rows = kept.shape[0]
+    core = ints[3]
+    at = 0
+    for out in outs:
+        width = out.shape[1]
+        out[pl.ds(pl.multiple_of(core * rows, rows), rows), :] = kept[:, at : at + width]
+        out[pl.ds(pl.multiple_of((1 - core) * rows, rows), rows), :] = got[:, at : at + width]
+        at += width
+
+
+def settings_kernel(inner, ints, conv, bias, per_head, taps_out, rates_out, skip_out):
+    core = ints[3]
+    for i, (tap, more) in enumerate(
+        zip(columns_of(conv, core, inner), columns_of(bias, core, inner), strict=True)
+    ):
+        taps_out[0:4, lanes(i)] = tap
+        taps_out[4:5, lanes(i)] = more
+        taps_out[5:8, lanes(i)] = jnp.zeros((3, LANES), F32)
+    heads = per_head.shape[1]
+    exact = functools.partial(
+        jnp.dot, precision=lax.Precision.HIGHEST, preferred_element_type=F32
+    )
+    own = exact(per_head[...], chosen_heads(core, heads))
+    rates_out[...] = own
+    row = lax.broadcasted_iota(jnp.int32, (LANES, inner // 2), 0)
+    lane = lax.broadcasted_iota(jnp.int32, (LANES, inner // 2), 1)
+    pair, second = lane // LANES, (lane % LANES) // (LANES // 2)
+    mine = (pair % 2) * (heads // 4) + 2 * (pair // 2) + second
+    skip_out[...] = exact(own, jnp.where(row == mine, 1.0, 0.0))
+
+
 def swapped(x, masks):
     count = lax.axis_size("req") * lax.axis_size("seq")
     return lax.ppermute(x, AXES, [(i, i ^ masks[i % 2]) for i in range(count)])
@@ -279,89 +355,45 @@
     nstate = (mix_weight.shape[1] - inner) // 2
     share = heads // 4
     quarter = inner // 4
-    chip = req_index * 2 + along
-
-    def mine_of(a, b, who):
-        bc = lax.dynamic_slice_in_dim(a, inner + nstate * who, nstate, 1)
-        early = lax.dynamic_slice_in_dim(a, quarter * who, quarter, 1)
-        late = lax.dynamic_slice_in_dim(a, 2 * quarter + quarter * who, quarter, 1)
-        parts = [bc]
-        if b is not None:
-            parts += [steps_of(b, who)]
-        for i in range(quarter // LANES):
-            parts += [early[:, lanes(i)], late[:, lanes(i)]]
-        return jnp.concatenate(parts, axis=1)
-
-    def steps_of(b, who):
-        one = lax.dynamic_slice_in_dim(b, share * who, share, 1)
-        two = lax.dynamic_slice_in_dim(b, 2 * share + share * who, share, 1)
-        return jnp.concatenate(
-            [one, two, jnp.zeros((b.shape[0], LANES - 2 * share), b.dtype)], axis=1
-        )
-
-    kept = mine_of(mix_weight, step_weight, core)
-    given = mine_of(mix_weight, step_weight, 1 - core)
-    got = swapped(given, (1, 1))
-    weights = jnp.where(
-        core == 0, jnp.concatenate([kept, got], axis=0), jnp.concatenate([got, kept], axis=0)
-    )
-
-    order = []
-
-    def gathered(block, routes):
-        masks = [(FLIPS[one], FLIPS[two]) for one, two in zip(*routes, strict=True)]
-        for p in range(2 ** len(masks)):
-            one, two = (
-                sum(mask[who] // 2 for s, mask in enumerate(masks) if (p >> s) & 1)
-                for who in range(2)
-            )
-            order.append(jnp.bitwise_xor(chip, jnp.where(core == 0, one, two)))
-        for mask in masks[:-1]:
-            block = jnp.concatenate([block, swapped(block, mask)], axis=0)
-        return block, swapped(block, masks[-1])
-
-    chunks, at = [], 0
-    for i, routes in enumerate(ROUTES):
-        width = (len(PAIRS[i]) + (2 if i == 0 else 0)) * LANES
-        chunks.append(gathered(weights[:, at : at + width], routes))
-        at += width
-
-    other = swapped(rows, (1, 1))
-    last_rows = jnp.where(core == 1, rows[span - HALO :], other[span - HALO :])
-    count = lax.axis_size("req") * lax.axis_size("seq")
-    halo = lax.ppermute(
-        last_rows, AXES, [(i, i + 2) for i in range(count) if (i // 2) % 2 == 0]
-    )
-    own = jnp.concatenate([halo, rows], axis=0)
-
     slots = jnp.arange(deal.shape[0], dtype=jnp.int32)
     request = jnp.sum(jnp.where(slots == req_index, deal, 0))
     length = jnp.sum(jnp.where(slots == request, prompt_len, 0))
     start = jnp.sum(jnp.where(slots == request, prompt_start, 0))
-    taps = mine_of(
-        jnp.concatenate([conv_weight, conv_bias[None], jnp.zeros_like(conv_weight[:3])], axis=0),
-        None,
-        core,
-    )
-    rates = jnp.concatenate(
-        [
-            steps_of(step_bias[None], core),
-            steps_of(decay_rate[None] * (-LOG2E), core),
-            jnp.zeros((6, LANES), F32),
-        ],
-        axis=0,
-    )
-    skip_all = mine_of(
-        jnp.concatenate([jnp.repeat(skip_gain, head_dim), jnp.zeros((2 * nstate,), F32)])[None],
-        None,
-        core,
-    )
-    skip = jnp.broadcast_to(skip_all[:, LANES:], (8, inner // 2))
-    ints = jnp.stack(
-        [start, start + length, along * 2 * span, core, along]
-        + [jnp.zeros_like(core)] * 3
-        + order
-    ).astype(jnp.int32)
+    wanted = jnp.sum(jnp.where(deal == req_index, slots, 0))
+    partner_wanted = jnp.sum(jnp.where(deal == (req_index ^ 1), slots, 0))
+    chip = req_index * 2 + along
+    place = jnp.stack([along * 2 * span, core, along, chip])
+    early_ints = jnp.concatenate([jnp.zeros((2,), jnp.int32), place])
+    state = {}
+
+    def after(*values):
+        if "token" not in state:
+            return values if len(values) > 1 else values[0]
+        *out, state["token"] = lax.optimization_barrier((*values, state["token"]))
+        return tuple(out) if len(out) > 1 else out[0]
+
+    widths = [(len(held) + (2 if i == 0 else 0)) * LANES for i, held in enumerate(PAIRS)]
+    total = sum(widths)
+    portion = mix_weight.shape[0]
+    kept, given = pl.pallas_call(
+        functools.partial(sort_kernel, inner),
+        in_specs=[SMEM, VMEM, VMEM],
+        out_specs=[VMEM] * 2,
+        out_shape=[jax.ShapeDtypeStruct((portion, total), BF16)] * 2,
+        compiler_params=params(8),
+        name="sort",
+    )(early_ints, mix_weight, step_weight)
+    got = swapped(given, (1, 1))
+    blocks = pl.pallas_call(
+        stack_kernel,
+        in_specs=[SMEM, VMEM, VMEM],
+        out_specs=[VMEM] * len(widths),
+        out_shape=[jax.ShapeDtypeStruct((2 * portion, width), BF16) for width in widths],
+        compiler_params=params(8),
+        name="stack",
+    )(early_ints, kept, got)
+    blocks = list(blocks)
+    arrived = [None] * len(widths)
 
     chip_rows = 2 * span
     groups = chip_rows // GROUP
@@ -372,42 +404,39 @@
             pltpu.VMEM((spans, chip_rows + 8, LANES), F32),
         ]
 
-    width = chunks[0][0].shape[1]
     extra = len(PAIRS[0])
-    bc, x0, cq, kq, kt, ca, tot = pl.pallas_call(
-        first_kernel,
-        in_specs=[SMEM] + [VMEM] * 6,
-        out_specs=[VMEM] * 7,
-        scratch_shapes=scratch(width, 1 + extra) + [pltpu.VMEM((chip_rows, LANES), F32)],
-        out_shape=[
-            jax.ShapeDtypeStruct((chip_rows, LANES), BF16),
-            jax.ShapeDtypeStruct((chip_rows, extra * LANES), BF16),
-            jax.ShapeDtypeStruct((chip_rows, LANES), F32),
-            jax.ShapeDtypeStruct((chip_rows, LANES), F32),
-            jax.ShapeDtypeStruct((groups, 32, GROUP), F32),
-            jax.ShapeDtypeStruct((chip_rows, LANES), F32),
-            jax.ShapeDtypeStruct((8, LANES), F32),
-        ],
-        compiler_params=params(24),
-        cost_estimate=pl.CostEstimate(
-            flops=2 * chip_rows * depth * width, bytes_accessed=9000000, transcendentals=500000
-        ),
-        name="first",
-    )(ints, own, other, *chunks[0], taps[:, : (1 + extra) * LANES], rates)
-
-    bc_other = swapped(bc, (1, 1))
-    b = jnp.where(core == 0, bc, bc_other)
-    c = jnp.where(core == 0, bc_other, bc)
-
-    def scanned(index):
-        chunk = chunks[index]
+
+    def projected(ints, own, other, low, high, taps, rates):
+        width = widths[0]
+        return pl.pallas_call(
+            first_kernel,
+            in_specs=[SMEM] + [VMEM] * 6,
+            out_specs=[VMEM] * 7,
+            scratch_shapes=scratch(width, 1 + extra) + [pltpu.VMEM((chip_rows, LANES), F32)],
+            out_shape=[
+                jax.ShapeDtypeStruct((chip_rows, LANES), BF16),
+                jax.ShapeDtypeStruct((chip_rows, extra * LANES), BF16),
+                jax.ShapeDtypeStruct((chip_rows, LANES), F32),
+                jax.ShapeDtypeStruct((chip_rows, LANES), F32),
+                jax.ShapeDtypeStruct((groups, 32, GROUP), F32),
+                jax.ShapeDtypeStruct((chip_rows, LANES), F32),
+                jax.ShapeDtypeStruct((8, LANES), F32),
+            ],
+            compiler_params=params(24),
+            cost_estimate=pl.CostEstimate(
+                flops=2 * chip_rows * depth * width, bytes_accessed=9000000, transcendentals=500000
+            ),
+            name="first",
+        )(ints, own, other, low, high, taps[:, : (1 + extra) * LANES], rates)
+
+    def scanned(index, ints, own, other, low, high, taps, skip, x0, b, c, cq, kq, kt, tot):
         more = extra if index == 1 else 0
         held = (PAIRS[0] if more else ()) + PAIRS[index]
         pairs = len(held)
         new = pairs - more
         firsts = [first_head(p, share) for p in held]
         tap_at, skip_at = (1 + PAIRS[index][0]) * LANES, held[0] * LANES
-        width = chunk[0].shape[1]
+        width = widths[index]
         return pl.pallas_call(
             functools.partial(scan_kernel, index, firsts, more),
             in_specs=[SMEM] + [VMEM] * 13,
@@ -426,11 +455,11 @@
             ),
             name="scan",
         )(
-            ints, own, other, *chunk, taps[:, tap_at : tap_at + new * LANES],
+            ints, own, other, low, high, taps[:, tap_at : tap_at + new * LANES],
             x0, b, c, cq, kq, kt, tot, skip[:, skip_at : skip_at + pairs * LANES],
         )
 
-    def joined(held, ys, ss, r):
+    def joined(held, ints, c, ca, tot, ys, ss, r):
         pairs = len(held)
         halves = [(i, i + 1) for i in range(0, pairs, 2)]
         sizes = [y.shape[1] // LANES for y in ys]
@@ -452,66 +481,150 @@
             name="join",
         )(ints, c, ca, tot, r, *ys, *ss)
 
-    wanted = jnp.sum(jnp.where(deal == req_index, slots, 0))
-    partner_wanted = jnp.sum(jnp.where(deal == (req_index ^ 1), slots, 0))
-
-    def delivered(block):
-        one = swapped(block, (16, 16))
-        pair = jnp.stack([block, one])
-        two = swapped(pair, (8, 8))
-
-        def pick(row):
-            rel = row ^ req_index
-            far, near = (rel >> 2) & 1, (rel >> 1) & 1
-            return jnp.where(
-                near == 1,
-                jnp.where(far == 1, two[1], two[0]),
-                jnp.where(far == 1, one, block),
+    early_pairs = sum(PAIRS[:-1], ())
+
+    def normed(ints, keep_a, keep_b, got_a, got_b):
+        places = [
+            [(p % 2) * (2 * quarter // LANES) + p // 2 for p in held]
+            for held in (early_pairs, PAIRS[-1])
+        ]
+        block = span // 2
+        return pl.pallas_call(
+            functools.partial(norm_kernel, places),
+            grid_spec=pltpu.PrefetchScalarGridSpec(
+                num_scalar_prefetch=1,
+                grid=(span // block,),
+                in_specs=[pl.BlockSpec((1, inner), lambda i, ints: (0, 0))]
+                + [
+                    pl.BlockSpec((block, a.shape[1]), lambda i, ints: (i, 0))
+                    for a in (keep_a, keep_b, got_a, got_b)
+                ],
+                out_specs=pl.BlockSpec((block, inner), lambda i, ints: (i, 0)),
+            ),
+            out_shape=jax.ShapeDtypeStruct((span, inner), BF16),
+            compiler_params=params(24),
+            cost_estimate=pl.CostEstimate(
+                flops=6 * span * inner, bytes_accessed=6 * span * inner, transcendentals=span
+            ),
+            name="norm",
+        )(ints, norm_gain[None], keep_a, keep_b, got_a, got_b)
+
+    def pick(row, cand):
+        rel = row ^ req_index
+        far, near = (rel >> 2) & 1, (rel >> 1) & 1
+        here, one, two = cand
+        return jnp.where(
+            near == 1,
+            jnp.where(far == 1, two[1], two[0]),
+            jnp.where(far == 1, one, here),
+        )
+
+    v = state
+    last = len(PAIRS) - 1
+    for event in SCHEDULE:
+        if event[0].isdigit():
+            i, step = (int(part) for part in event.split("."))
+            if step:
+                blocks[i] = jnp.concatenate(after(blocks[i], arrived[i]), axis=0)
+                v["token"] = blocks[i]
+            route = ROUTES[i]
+            arrived[i] = swapped(blocks[i], (FLIPS[route[0][step]], FLIPS[route[1][step]]))
+        elif event == "tokens":
+            v["other"] = swapped(rows, (1, 1))
+        elif event == "halo":
+            other = after(v["other"])
+            edge = jnp.where(core == 1, rows[span - HALO :], other[span - HALO :])
+            count = lax.axis_size("req") * lax.axis_size("seq")
+            route = [(i, i + 2) for i in range(count) if (i // 2) % 2 == 0]
+            v["token"] = edge
+            v["halo"] = lax.ppermute(edge, AXES, route)
+        elif event == "settings":
+            front = jnp.stack([start, start + length])
+            v["ints"] = after(jnp.concatenate([front, place]))
+            per_head = jnp.concatenate(
+                [jnp.stack([step_bias, decay_rate * (-LOG2E), skip_gain]), jnp.zeros((5, heads))]
             )
-
-        three = swapped(pick(partner_wanted), (4, 4))
-        odd = (wanted ^ req_index) & 1
-        return jnp.where(odd == 1, three, pick(wanted)).astype(F32)
-
-    y1, s1, t1 = scanned(1)
-    y2, s2, t2 = scanned(2)
-    r12 = swapped(jnp.concatenate([t1, t2], axis=1), (2, 2))
-    first_pairs = PAIRS[0] + PAIRS[1] + PAIRS[2]
-    send_a, keep_a, fin_a = joined(first_pairs, (y1, y2), (s1, s2), r12)
-    got_a = swapped(send_a, (1, 1))
-    final_a = delivered(fin_a)
-    y3, s3, t3 = scanned(3)
-    r3 = swapped(t3, (2, 2))
-    send_b, keep_b, fin_b = joined(PAIRS[3], (y3,), (s3,), r3)
-    got_b = swapped(send_b, (1, 1))
-    final_b = delivered(fin_b)
-
-    final_state = jnp.concatenate([final_a, final_b], axis=0).reshape(1, share, head_dim, nstate)
-    places = [
-        [(p % 2) * (2 * quarter // LANES) + p // 2 for p in held]
-        for held in (first_pairs, PAIRS[3])
-    ]
-    block = span // 4
-    result = pl.pallas_call(
-        functools.partial(norm_kernel, places),
-        grid_spec=pltpu.PrefetchScalarGridSpec(
-            num_scalar_prefetch=1,
-            grid=(span // block,),
-            in_specs=[pl.BlockSpec((1, inner), lambda i, ints: (0, 0))]
-            + [
-                pl.BlockSpec((block, a.shape[1]), lambda i, ints: (i, 0))
-                for a in (keep_a, keep_b, got_a, got_b)
-            ],
-            out_specs=pl.BlockSpec((block, inner), lambda i, ints: (i, 0)),
-        ),
-        out_shape=jax.ShapeDtypeStruct((span, inner), BF16),
-        compiler_params=params(24),
-        cost_estimate=pl.CostEstimate(
-            flops=6 * span * inner, bytes_accessed=6 * span * inner, transcendentals=span
-        ),
-        name="norm",
-    )(ints, norm_gain[None], keep_a, keep_b, got_a, got_b)
-    return (result[None], final_state)
+            half = inner // 2
+            v["taps"], v["rates"], v["skip"] = pl.pallas_call(
+                functools.partial(settings_kernel, inner),
+                in_specs=[SMEM, VMEM, VMEM, VMEM],
+                out_specs=[VMEM] * 3,
+                out_shape=[
+                    jax.ShapeDtypeStruct((8, half + LANES), F32),
+                    jax.ShapeDtypeStruct((8, LANES), F32),
+                    jax.ShapeDtypeStruct((8, half), F32),
+                ],
+                compiler_params=params(8),
+                name="settings",
+            )(v["ints"], conv_weight, conv_bias[None], per_head)
+            v["token"] = v["rates"]
+        elif event == "own":
+            v["own"] = jnp.concatenate([after(v["halo"]), rows], axis=0)
+            v["token"] = v["own"]
+        elif event == "K0":
+            ints = after(v["ints"])
+            bc, x0, cq, kq, kt, ca, tot = projected(
+                ints, v["own"], v["other"], blocks[0], arrived[0], v["taps"], v["rates"]
+            )
+            v["token"] = tot
+            v["bc"] = swapped(bc, (1, 1))
+        elif event[0] == "K":
+            i = int(event[1:])
+            if i == 1:
+                two = after(v["bc"])
+                b = jnp.where(core == 0, bc, two)
+                c = jnp.where(core == 0, two, bc)
+            ints = after(v["ints"])
+            v["y", i], v["s", i], v["t", i] = scanned(
+                i, ints, v["own"], v["other"], blocks[i], arrived[i], v["taps"], v["skip"],
+                x0, b, c, cq, kq, kt, tot,
+            )
+            v["token"] = v["t", i]
+        elif event in ("xA", "xB"):
+            which = range(1, last) if event == "xA" else (last,)
+            sent = [v["t", i] for i in which]
+            if len(sent) > 1:
+                sent = jnp.concatenate(after(*sent), axis=1)
+                v["token"] = sent
+            else:
+                sent = sent[0]
+            v["r", event[1]] = swapped(sent, (2, 2))
+        elif event in ("JA", "JB"):
+            which = range(1, last) if event == "JA" else (last,)
+            held = early_pairs if event == "JA" else PAIRS[last]
+            ints, r = after(v["ints"], v["r", event[1]])
+            send, v["keep", event[1]], v["fin", event[1]] = joined(
+                held, ints, c, ca, tot, [v["y", i] for i in which], [v["s", i] for i in which], r
+            )
+            v["token"] = v["fin", event[1]]
+            v["got", event[1]] = swapped(send, (1, 1))
+        elif event[0] == "f":
+            key = event[1]
+            if event[2] == "0":
+                v["one", key] = swapped(v["fin", key], (16, 16))
+            elif event[2] == "1":
+                v["pair", key] = jnp.stack(after(v["fin", key], v["one", key]))
+                v["token"] = v["pair", key]
+                v["two", key] = swapped(v["pair", key], (8, 8))
+            elif event[2] == "2":
+                cand = (v["fin", key], v["one", key], after(v["two", key]))
+                v["cand", key] = cand
+                v["picked", key] = pick(partner_wanted, cand)
+                v["token"] = v["picked", key]
+                v["three", key] = swapped(v["picked", key], (4, 4))
+            else:
+                three = after(v["three", key])
+                odd = (wanted ^ req_index) & 1
+                v["final", key] = jnp.where(odd == 1, three, pick(wanted, v["cand", key])).astype(
+                    F32
+                )
+                v["token"] = v["final", key]
+        else:
+            ints = after(v["ints"])
+            result = normed(ints, v["keep", "A"], v["keep", "B"], v["got", "A"], v["got", "B"])
+            v["token"] = result
+    final_state = jnp.concatenate([v["final", "A"], v["final", "B"]], axis=0)
+    return (result[None], final_state.reshape(1, share, head_dim, nstate))
 
 
 def passed_along(block, axis, distance):

time: 159 us -> 142 us (0.89)
  other arithmetic: 22 us -> 9.39 us
  waiting for transfers between devices: 42.6 us -> 33.9 us
  Pallas kernels: 32.7 us -> 37.6 us
  local copies, waits for them, and re-layouts: 9.45 us -> 6.04 us
  starting transfers between devices: 48 us -> 51.3 us
    concatenate x23 -> x3, other arithmetic: 13.2 us -> 1.66 us  [the longest x1 0.75 us: on_device(): final_state = jnp.concatenate([v['final', 'A'], v['final', 'B']], axis=0)]
    ppermute x29, waiting for transfers between devices: 42.6 us -> 33.9 us  [swapped(): return lax.ppermute(x, AXES, [(i, i ^ masks[i % 2]) for i in range(count)])]
    ppermute x29, starting transfers between devices: 44.8 us -> 48.8 us  [swapped(): return lax.ppermute(x, AXES, [(i, i ^ masks[i % 2]) for i in range(count)])]
    slice x8 -> x5, local copies, waits for them, and re-layouts: 3.77 us -> 0.01 us  [the longest x3 0.01 us: scanned(): taps[:, tap_at:tap_at + new * LANES]]
    pallas_call x3, Pallas kernels: 17 us -> 20.7 us  [scanned(): pl.pallas_call(functools.partial(scan_kernel, index, firsts, more), in_sp...]
    pallas_call x2 -> x5, Pallas kernels: 10.1 us -> 12.9 us  [the longest x1 6.34 us: projected(): pl.pallas_call(first_kernel, in_specs=[SMEM] + [VMEM] * 6, out_specs=[VME...]
    concatenate x4 -> x16, local copies, waits for them, and re-layouts: 0.36 us -> 3.16 us  [the longest x12 2.25 us: on_device(): blocks[i] = jnp.concatenate(after(blocks[i], arrived[i]), axis=0)]
    pallas_call x2, Pallas kernels: 5.62 us -> 3.95 us  [joined(): pl.pallas_call(functools.partial(join_kernel, [first_head(p, share) for p...]
  transfers between devices with their start and end apart: 30 -> 30, of which waited for: 14 -> 10; matrix products, arithmetic and copies ran while one was open for 17% -> 10% of each run, Pallas kernels for 18% -> 24%
where the time goes in v3:
time: 142 us
  starting transfers between devices  51.3 us (36%)
  Pallas kernels  37.6 us (26%)
  waiting for transfers between devices  33.9 us (24%)
  other arithmetic  9.39 us (7%)
  local copies, waits for them, and re-layouts  6.04 us (4%)
  between operations  3.5 us (2%)
    ppermute x29, starting transfers between devices, swapped(): return lax.ppermute(x, AXES, [(i, i ^ masks[i % 2]) for i in range(count)])  48.8 us
    ppermute x29, waiting for transfers between devices, swapped(): return lax.ppermute(x, AXES, [(i, i ^ masks[i % 2]) for i in range(count)])  33.9 us
    pallas_call x3, Pallas kernels, scanned(): pl.pallas_call(functools.partial(scan_kernel, index, firsts, more), in_sp...  20.7 us
    pallas_call x1, Pallas kernels, projected(): pl.pallas_call(first_kernel, in_specs=[SMEM] + [VMEM] * 6, out_specs=[VME...  6.34 us
    pallas_call x1, Pallas kernels, normed(): pl.pallas_call(functools.partial(norm_kernel, places), grid_spec=pltpu.Pr...  4.18 us
    pallas_call x2, Pallas kernels, joined(): pl.pallas_call(functools.partial(join_kernel, [first_head(p, share) for p...  3.95 us
  transfers between devices with their start and end apart: 30, of which 10 were waited for; matrix products, arithmetic and copies ran while one was open for 10% of the time, Pallas kernels for 24%

profile of v3, /device:TPU:0, one launch (start us, length us, event | category | flops | bytes accessed | tf_op | source)
XLA Modules:
  0.0 141.7 jit_solution(16269798790652824334)
XLA Ops:
  6.6 4.0 %collective-permute-start.2 = (bf16[160,384]{1,0:T(8,128)(2,1)S(1)}, bf16[160,384]{1,0:T(8,128)(2,1)S(1)}, u32[]{:S(2)}, u32[]{:S(2)}) collective-permute-start(bf16[160,384]{1,0:T(8,128)(2,1)S(1)} %get-tuple-element.79), channel_id=1, source_target_pairs={{0,16},{1,17},{2,18},{3,19},{4,20},{5,21},{6,22},{7,23},{8,24},{9,... | collective-permute-start | bytes 368648 | tf_op jit(solution)/shard_map/ppermute | solution.py:340
  12.0 8.0 %collective-permute-done.2 = bf16[160,384]{1,0:T(8,128)(2,1)S(1)} collective-permute-done((bf16[160,384]{1,0:T(8,128)(2,1)S(1)}, bf16[160,384]{1,0:T(8,128)(2,1)S(1)}, u32[]{:S(2)}, u32[]{:S(2)}) %collective-permute-start.2) | collective-permute-done | bytes 122912 | tf_op jit(solution)/shard_map/ppermute | solution.py:340
  20.1 1.9 %collective-permute-start.3 = (bf16[320,384]{1,0:T(8,128)(2,1)S(1)}, bf16[320,384]{1,0:T(8,128)(2,1)}, u32[]{:S(2)}, u32[]{:S(2)}) collective-permute-start(bf16[320,384]{1,0:T(8,128)(2,1)S(1)} %constant_dynamic-update-slice_fusion), channel_id=1, source_target_pairs={{0,2},{1,9},{2,0},{3,11},{4,6},{5,13},{6,4},{7,15},{8,10},{9,1},{1... | collective-permute-start | bytes 737288 | tf_op jit(solution)/shard_map/ppermute | solution.py:340
  22.0 2.0 %fusion.4 = (s32[]{:T(128)}, s32[]{:T(128)}) fusion(s32[8]{0:T(128)} %param.22, s32[]{:T(128)} %get-tuple-element.153, s32[8]{0:T(128)} %param.21), kind=kLoop, calls=%fused_computation.47 | loop fusion | flops 38 | bytes 76 | tf_op jit(solution)/shard_map/reduce_sum | solution.py:361
  26.8 2.9 %collective-permute-start.11 = (bf16[160,256]{1,0:T(8,128)(2,1)S(1)}, bf16[160,256]{1,0:T(8,128)(2,1)S(1)}, u32[]{:S(2)}, u32[]{:S(2)}) collective-permute-start(bf16[160,256]{1,0:T(8,128)(2,1)S(1)} %get-tuple-element.97), channel_id=1, source_target_pairs={{0,16},{1,17},{2,18},{3,19},{4,20},{5,21},{6,22},{7,23},{8,24},{9,... | collective-permute-start | bytes 245768 | tf_op jit(solution)/shard_map/ppermute | solution.py:340
  34.7 2.4 %collective-permute-start.5 = (bf16[16,2560]{1,0:T(8,128)(2,1)S(1)}, bf16[16,2560]{1,0:T(8,128)(2,1)S(1)}, u32[]{:S(2)}, u32[]{:S(2)}) collective-permute-start(bf16[16,2560]{1,0:T(8,128)(2,1)S(1)} %bitcast_select_fusion.2), channel_id=1, source_target_pairs={{0,2},{1,3},{4,6},{5,7},{8,10},{9,11},{12,14},{13,15},{16,18},{17,... | collective-permute-start | bytes 245768 | tf_op jit(solution)/shard_map/ppermute | solution.py:540
  39.9 2.9 %collective-permute-done.7 = bf16[320,384]{1,0:T(8,128)(2,1)S(1)} collective-permute-done((bf16[320,384]{1,0:T(8,128)(2,1)S(1)}, bf16[320,384]{1,0:T(8,128)(2,1)S(1)}, u32[]{:S(2)}, u32[]{:S(2)}) %collective-permute-start.7) | collective-permute-done | bytes 245792 | tf_op jit(solution)/shard_map/ppermute | solution.py:340
  45.0 3.5 %collective-permute-done.10 = bf16[320,512]{1,0:T(8,128)(2,1)S(1)} collective-permute-done((bf16[320,512]{1,0:T(8,128)(2,1)S(1)}, bf16[320,512]{1,0:T(8,128)(2,1)S(1)}, u32[]{:S(2)}, u32[]{:S(2)}) %collective-permute-start.10) | collective-permute-done | bytes 327712 | tf_op jit(solution)/shard_map/ppermute | solution.py:340
  50.2 8.8 %collective-permute-done.9 = bf16[640,384]{1,0:T(8,128)(2,1)S(1)} collective-permute-done((bf16[640,384]{1,0:T(8,128)(2,1)S(1)}, bf16[640,384]{1,0:T(8,128)(2,1)S(1)}, u32[]{:S(2)}, u32[]{:S(2)}) %collective-permute-start.9) | collective-permute-done | bytes 491552 | tf_op jit(solution)/shard_map/ppermute | solution.py:340
  59.3 3.3 %collective-permute-done.14 = bf16[320,256]{1,0:T(8,128)(2,1)S(1)} collective-permute-done((bf16[320,256]{1,0:T(8,128)(2,1)S(1)}, bf16[320,256]{1,0:T(8,128)(2,1)S(1)}, u32[]{:S(2)}, u32[]{:S(2)}) %collective-permute-start.14) | collective-permute-done | bytes 163872 | tf_op jit(solution)/shard_map/ppermute | solution.py:340
  62.6 2.1 %collective-permute-start.17 = (bf16[640,256]{1,0:T(8,128)(2,1)S(1)}, bf16[640,256]{1,0:T(8,128)(2,1)S(1)}, u32[]{:S(2)}, u32[]{:S(2)}) collective-permute-start(bf16[640,256]{1,0:T(8,128)(2,1)S(1)} %constant_dynamic-update-slice_fusion.18), channel_id=1, source_target_pairs={{0,8},{1,3},{2,10},{3,1},{4,12},{5,7},{6,14},{7,5},{8,0},{9,11},{1... | collective-permute-start | bytes 983048 | tf_op jit(solution)/shard_map/ppermute | solution.py:340
  64.8 6.3 %first.1 = (bf16[1024,128]{1,0:T(8,128)(2,1)S(1)}, bf16[1024,128]{1,0:T(8,128)(2,1)S(1)}, f32[1024,128]{1,0:T(8,128)S(1)}, f32[1024,128]{1,0:T(8,128)S(1)}, f32[...) custom-call(s32[6]{0:T(128)S(1)} %concatenate.56.ints, ...), custom_call_target="tpu_custom_call" | custom-call | flops 2013265920 | bytes 9000000 | tf_op jit(solution)/shard_map/first/pallas_call | solution.py:411
  71.2 6.3 %collective-permute-start.16 = (bf16[1024,128]{1,0:T(8,128)(2,1)S(1)}, bf16[1024,128]{1,0:T(8,128)(2,1)S(1)}, u32[]{:S(2)}, u32[]{:S(2)}) collective-permute-start(bf16[1024,128]{1,0:T(8,128)(2,1)S(1)} %get-tuple-element.110), channel_id=1, source_target_pairs={{0,1},{1,0},{2,3},{3,2},{4,5},{5,4},{6,7},{7,6},{8,9},{9,8},{10,11... | collective-permute-start | bytes 786440 | tf_op jit(solution)/shard_map/ppermute | solution.py:340
  78.7 7.6 %scan.3 = (f32[1024,512]{1,0:T(8,128)S(1)}, f32[128,512]{1,0:T(8,128)S(1)}, bf16[144,512]{1,0:T(8,128)(2,1)S(1)}) custom-call(s32[6]{0:T(128)S(1)} %concatenate.56.ints, bf16[528,2560]{1,0:T(8,128)(2,1)S(1)} %pad_maximum_fusion.own, bf16[512,2560]{1,0:T(8,128)(2,1)} %collective-permute-done.other, ...), custom_call_target="tpu_custom_call" | custom-call | flops 4413265920 | bytes 12000000 | tf_op jit(solution)/shard_map/scan/pallas_call | solution.py:440
  86.3 8.0 %scan.4 = (f32[1024,512]{1,0:T(8,128)S(1)}, f32[128,512]{1,0:T(8,128)S(1)}, bf16[144,512]{1,0:T(8,128)(2,1)S(1)}) custom-call(s32[6]{0:T(128)S(1)} %concatenate.56.ints, bf16[528,2560]{1,0:T(8,128)(2,1)S(1)} %pad_maximum_fusion.own, bf16[512,2560]{1,0:T(8,128)(2,1)} %collective-permute-done.other, ...), custom_call_target="tpu_custom_call" | custom-call | flops 5084354560 | bytes 12000000 | tf_op jit(solution)/shard_map/scan/pallas_call | solution.py:440
  95.5 5.1 %scan.5 = (f32[1024,256]{1,0:T(8,128)S(1)}, f32[128,256]{1,0:T(8,128)S(1)}, bf16[144,256]{1,0:T(8,128)(2,1)S(1)}) custom-call(s32[6]{0:T(128)S(1)} %concatenate.56.ints, bf16[528,2560]{1,0:T(8,128)(2,1)S(1)} %pad_maximum_fusion.own, bf16[512,2560]{1,0:T(8,128)(2,1)} %collective-permute-done.other, ...), custom_call_target="tpu_custom_call" | custom-call | flops 2542177280 | bytes 12000000 | tf_op jit(solution)/shard_map/scan/pallas_call | solution.py:440
  101.1 3.0 %join.2 = (f32[512,1024]{1,0:T(8,128)}, f32[512,1024]{1,0:T(8,128)S(1)}, bf16[512,128]{1,0:T(8,128)(2,1)S(1)}) custom-call(s32[6]{0:T(128)S(1)} %concatenate.56.ints, bf16[1024,128]{1,0:T(8,128)(2,1)S(1)} %get-tuple-element.155.c_ref, f32[1024,128]{1,0:T(8,128)S(1)} %get-tuple-element.127.ca_ref, f32[8,128]{1,0:T(8,128)S(1)} %get-tuple-element.111.tot_ref, ...), custom_call_target="tpu_custom_call" | custom-call | flops 536870912 | bytes 8388608 | tf_op jit(solution)/shard_map/join/pallas_call | solution.py:466
  104.1 6.2 %collective-permute-start.26 = (f32[512,1024]{1,0:T(8,128)}, f32[512,1024]{1,0:T(8,128)}, u32[]{:S(2)}, u32[]{:S(2)}) collective-permute-start(f32[512,1024]{1,0:T(8,128)} %get-tuple-element.148), channel_id=1, source_target_pairs={{0,1},{1,0},{2,3},{3,2},{4,5},{5,4},{6,7},{7,6},{8,9},{9,8},{10,11... | collective-permute-start | bytes 6291464 | tf_op jit(solution)/shard_map/ppermute | solution.py:340
  110.3 3.9 %collective-permute-start.23 = (bf16[512,128]{1,0:T(8,128)(2,1)S(1)}, bf16[512,128]{1,0:T(8,128)(2,1)S(1)}, u32[]{:S(2)}, u32[]{:S(2)}) collective-permute-start(bf16[512,128]{1,0:T(8,128)(2,1)S(1)} %get-tuple-element.139), channel_id=1, source_target_pairs={{0,16},{1,17},{2,18},{3,19},{4,20},{5,21},{6,22},{7,23},{8,24},{9,... | collective-permute-start | bytes 393224 | tf_op jit(solution)/shard_map/ppermute | solution.py:340
  115.5 3.0 %collective-permute-done.20.r_ref = bf16[144,256]{1,0:T(8,128)(2,1)S(1)} collective-permute-done((bf16[144,256]{1,0:T(8,128)(2,1)S(1)}, bf16[144,256]{1,0:T(8,128)(2,1)S(1)}, u32[]{:S(2)}, u32[]{:S(2)}) %collective-permute-start.20) | collective-permute-done | bytes 73760 | tf_op jit(solution)/shard_map/ppermute | solution.py:340
  121.4 3.3 %collective-permute-start.22 = (bf16[128,128]{1,0:T(8,128)(2,1)S(1)}, bf16[128,128]{1,0:T(8,128)(2,1)S(1)}, u32[]{:S(2)}, u32[]{:S(2)}) collective-permute-start(bf16[128,128]{1,0:T(8,128)(2,1)S(1)} %get-tuple-element.141), channel_id=1, source_target_pairs={{0,16},{1,17},{2,18},{3,19},{4,20},{5,21},{6,22},{7,23},{8,24},{9,... | collective-permute-start | bytes 98312 | tf_op jit(solution)/shard_map/ppermute | solution.py:340
  127.8 3.5 %collective-permute-start.24 = (bf16[2,128,128]{2,1,0:T(8,128)(2,1)S(1)}, bf16[2,128,128]{2,1,0:T(8,128)(2,1)S(1)}, u32[]{:S(2)}, u32[]{:S(2)}) collective-permute-start(bf16[2,128,128]{2,1,0:T(8,128)(2,1)S(1)} %pad_maximum_fusion.3), channel_id=1, source_target_pairs={{0,8},{1,9},{2,10},{3,11},{4,12},{5,13},{6,14},{7,15},{8,0},{9,1},... | collective-permute-start | bytes 196616 | tf_op jit(solution)/shard_map/ppermute | solution.py:340
  132.4 2.1 %collective-permute-start.28 = (bf16[512,128]{1,0:T(8,128)(2,1)S(1)}, bf16[512,128]{1,0:T(8,128)(2,1)S(1)}, u32[]{:S(2)}, u32[]{:S(2)}) collective-permute-start(bf16[512,128]{1,0:T(8,128)(2,1)S(1)} %bitcast_select_fusion.1), channel_id=1, source_target_pairs={{0,4},{1,5},{2,6},{3,7},{4,0},{5,1},{6,2},{7,3},{8,12},{9,13},{10,... | collective-permute-start | bytes 393224 | tf_op jit(solution)/shard_map/ppermute | solution.py:340
  135.7 4.2 %norm.1 = bf16[512,2560]{1,0:T(8,128)(2,1)} custom-call(s32[6]{0:T(128)S(1)} %concatenate.56.ints, f32[1,2560]{1,0:T(1,128)S(1)} %broadcast_in_dim.23.gain_ref, f32[512,1024]{1,0:T(8,128)S(1)} %get-tuple-element.146.ka_ref, f32[512,256]{1,0:T(8,128)S(1)} %get-tuple-element.147.kb_ref, f32[512,1024]{1,0:T(8,128)} %collective-permute-done.26.ra_ref, ...), custom_call_target="tpu_custom_call" | custom-call | flops 7864320 | bytes 7864320 | tf_op jit(solution)/shard_map/norm/pallas_call | solution.py:492
  (107 shorter events, 33.6 us)
Async XLA Ops:
  0.6 33.2 %collective-permute-start = (bf16[512,2560]{1,0:T(8,128)(2,1)}, bf16[512,2560]{1,0:T(8,128)(2,1)}, u32[]{:S(2)}, u32[]{:S(2)}) collective-permute-start(bf16[512,2560]{1,0:T(8,128)(2,1)} %bitcast.37), channel_id=1, source_target_pairs={{0,1},{1,0},{2,3},{3,2},{4,5},{5,4},{6,7},{7,6},{8,9},{9,8},{10,11... | collective-permute-start | bytes 7864328 | tf_op jit(solution)/shard_map/ppermute | solution.py:340
  6.6 13.4 %collective-permute-start.2 = (bf16[160,384]{1,0:T(8,128)(2,1)S(1)}, bf16[160,384]{1,0:T(8,128)(2,1)S(1)}, u32[]{:S(2)}, u32[]{:S(2)}) collective-permute-start(bf16[160,384]{1,0:T(8,128)(2,1)S(1)} %get-tuple-element.79), channel_id=1, source_target_pairs={{0,16},{1,17},{2,18},{3,19},{4,20},{5,21},{6,22},{7,23},{8,24},{9,... | collective-permute-start | bytes 368648 | tf_op jit(solution)/shard_map/ppermute | solution.py:340
  12.0 17.8 %collective-permute-start.4 = (bf16[160,384]{1,0:T(8,128)(2,1)S(1)}, bf16[160,384]{1,0:T(8,128)(2,1)}, u32[]{:S(2)}, u32[]{:S(2)}) collective-permute-start(bf16[160,384]{1,0:T(8,128)(2,1)S(1)} %get-tuple-element.81), channel_id=1, source_target_pairs={{0,16},{1,17},{2,18},{3,19},{4,20},{5,21},{6,22},{7,23},{8,24},{9,... | collective-permute-start | bytes 368648 | tf_op jit(solution)/shard_map/ppermute | solution.py:340
  20.1 11.2 %collective-permute-start.3 = (bf16[320,384]{1,0:T(8,128)(2,1)S(1)}, bf16[320,384]{1,0:T(8,128)(2,1)}, u32[]{:S(2)}, u32[]{:S(2)}) collective-permute-start(bf16[320,384]{1,0:T(8,128)(2,1)S(1)} %constant_dynamic-update-slice_fusion), channel_id=1, source_target_pairs={{0,2},{1,9},{2,0},{3,11},{4,6},{5,13},{6,4},{7,15},{8,10},{9,1},{1... | collective-permute-start | bytes 737288 | tf_op jit(solution)/shard_map/ppermute | solution.py:340
  26.8 11.5 %collective-permute-start.8 = (bf16[160,512]{1,0:T(8,128)(2,1)S(1)}, bf16[160,512]{1,0:T(8,128)(2,1)S(1)}, u32[]{:S(2)}, u32[]{:S(2)}) collective-permute-start(bf16[160,512]{1,0:T(8,128)(2,1)S(1)} %get-tuple-element.89), channel_id=1, source_target_pairs={{0,16},{1,17},{2,18},{3,19},{4,20},{5,21},{6,22},{7,23},{8,24},{9,... | collective-permute-start | bytes 491528 | tf_op jit(solution)/shard_map/ppermute | solution.py:340
  26.8 18.1 %collective-permute-start.11 = (bf16[160,256]{1,0:T(8,128)(2,1)S(1)}, bf16[160,256]{1,0:T(8,128)(2,1)S(1)}, u32[]{:S(2)}, u32[]{:S(2)}) collective-permute-start(bf16[160,256]{1,0:T(8,128)(2,1)S(1)} %get-tuple-element.97), channel_id=1, source_target_pairs={{0,16},{1,17},{2,18},{3,19},{4,20},{5,21},{6,22},{7,23},{8,24},{9,... | collective-permute-start | bytes 245768 | tf_op jit(solution)/shard_map/ppermute | solution.py:340
  30.7 12.2 %collective-permute-start.7 = (bf16[320,384]{1,0:T(8,128)(2,1)S(1)}, bf16[320,384]{1,0:T(8,128)(2,1)S(1)}, u32[]{:S(2)}, u32[]{:S(2)}) collective-permute-start(bf16[320,384]{1,0:T(8,128)(2,1)S(1)} %constant_dynamic-update-slice_fusion.2), channel_id=1, source_target_pairs={{0,8},{1,3},{2,10},{3,1},{4,12},{5,7},{6,14},{7,5},{8,0},{9,11},{1... | collective-permute-start | bytes 737288 | tf_op jit(solution)/shard_map/ppermute | solution.py:340
  32.2 12.3 %collective-permute-start.6 = (bf16[640,384]{1,0:T(8,128)(2,1)S(1)}, bf16[640,384]{1,0:T(8,128)(2,1)S(1)}, u32[]{:S(2)}, u32[]{:S(2)}) collective-permute-start(bf16[640,384]{1,0:T(8,128)(2,1)S(1)} %constant_dynamic-update-slice_fusion.4), channel_id=1, source_target_pairs={{0,4},{1,3},{2,6},{3,1},{4,0},{5,7},{6,2},{7,5},{8,12},{9,11},{10,... | collective-permute-start | bytes 1474568 | tf_op jit(solution)/shard_map/ppermute | solution.py:340
  34.7 10.0 %collective-permute-start.5 = (bf16[16,2560]{1,0:T(8,128)(2,1)S(1)}, bf16[16,2560]{1,0:T(8,128)(2,1)S(1)}, u32[]{:S(2)}, u32[]{:S(2)}) collective-permute-start(bf16[16,2560]{1,0:T(8,128)(2,1)S(1)} %bitcast_select_fusion.2), channel_id=1, source_target_pairs={{0,2},{1,3},{4,6},{5,7},{8,10},{9,11},{12,14},{13,15},{16,18},{17,... | collective-permute-start | bytes 245768 | tf_op jit(solution)/shard_map/ppermute | solution.py:540
  38.3 10.2 %collective-permute-start.10 = (bf16[320,512]{1,0:T(8,128)(2,1)S(1)}, bf16[320,512]{1,0:T(8,128)(2,1)S(1)}, u32[]{:S(2)}, u32[]{:S(2)}) collective-permute-start(bf16[320,512]{1,0:T(8,128)(2,1)S(1)} %constant_dynamic-update-slice_fusion.6), channel_id=1, source_target_pairs={{0,4},{1,9},{2,6},{3,11},{4,0},{5,13},{6,2},{7,15},{8,12},{9,1},{1... | collective-permute-start | bytes 983048 | tf_op jit(solution)/shard_map/ppermute | solution.py:340
  42.9 16.1 %collective-permute-start.9 = (bf16[640,384]{1,0:T(8,128)(2,1)S(1)}, bf16[640,384]{1,0:T(8,128)(2,1)S(1)}, u32[]{:S(2)}, u32[]{:S(2)}) collective-permute-start(bf16[640,384]{1,0:T(8,128)(2,1)S(1)} %constant_dynamic-update-slice_fusion.8), channel_id=1, source_target_pairs={{0,4},{1,9},{2,6},{3,11},{4,0},{5,13},{6,2},{7,15},{8,12},{9,1},{1... | collective-permute-start | bytes 1474568 | tf_op jit(solution)/shard_map/ppermute | solution.py:340
  44.6 20.2 %collective-permute-start.15 = (bf16[1280,384]{1,0:T(8,128)(2,1)S(1)}, bf16[1280,384]{1,0:T(8,128)(2,1)S(1)}, u32[]{:S(2)}, u32[]{:S(2)}) collective-permute-start(bf16[1280,384]{1,0:T(8,128)(2,1)S(1)} %constant_dynamic-update-slice_fusion.10.low), channel_id=1, source_target_pairs={{0,8},{1,5},{2,10},{3,7},{4,12},{5,1},{6,14},{7,3},{8,0},{9,13},{1... | collective-permute-start | bytes 2949128 | tf_op jit(solution)/shard_map/ppermute | solution.py:340
  48.6 16.1 %collective-permute-start.13 = (bf16[640,512]{1,0:T(8,128)(2,1)S(1)}, bf16[640,512]{1,0:T(8,128)(2,1)S(1)}, u32[]{:S(2)}, u32[]{:S(2)}) collective-permute-start(bf16[640,512]{1,0:T(8,128)(2,1)S(1)} %constant_dynamic-update-slice_fusion.14), channel_id=1, source_target_pairs={{0,2},{1,5},{2,0},{3,7},{4,6},{5,1},{6,4},{7,3},{8,10},{9,13},{10,... | collective-permute-start | bytes 1966088 | tf_op jit(solution)/shard_map/ppermute | solution.py:340
  48.7 13.9 %collective-permute-start.14 = (bf16[320,256]{1,0:T(8,128)(2,1)S(1)}, bf16[320,256]{1,0:T(8,128)(2,1)S(1)}, u32[]{:S(2)}, u32[]{:S(2)}) collective-permute-start(bf16[320,256]{1,0:T(8,128)(2,1)S(1)} %constant_dynamic-update-slice_fusion.12), channel_id=1, source_target_pairs={{0,4},{1,9},{2,6},{3,11},{4,0},{5,13},{6,2},{7,15},{8,12},{9,1},{1... | collective-permute-start | bytes 491528 | tf_op jit(solution)/shard_map/ppermute | solution.py:340
  59.2 19.5 %collective-permute-start.12 = (bf16[1280,384]{1,0:T(8,128)(2,1)S(1)}, bf16[1280,384]{1,0:T(8,128)(2,1)S(1)}, u32[]{:S(2)}, u32[]{:S(2)}) collective-permute-start(bf16[1280,384]{1,0:T(8,128)(2,1)S(1)} %constant_dynamic-update-slice_fusion.16.low), channel_id=1, source_target_pairs={{0,2},{1,5},{2,0},{3,7},{4,6},{5,1},{6,4},{7,3},{8,10},{9,13},{10,... | collective-permute-start | bytes 2949128 | tf_op jit(solution)/shard_map/ppermute | solution.py:340
  62.6 14.9 %collective-permute-start.17 = (bf16[640,256]{1,0:T(8,128)(2,1)S(1)}, bf16[640,256]{1,0:T(8,128)(2,1)S(1)}, u32[]{:S(2)}, u32[]{:S(2)}) collective-permute-start(bf16[640,256]{1,0:T(8,128)(2,1)S(1)} %constant_dynamic-update-slice_fusion.18), channel_id=1, source_target_pairs={{0,8},{1,3},{2,10},{3,1},{4,12},{5,7},{6,14},{7,5},{8,0},{9,11},{1... | collective-permute-start | bytes 983048 | tf_op jit(solution)/shard_map/ppermute | solution.py:340
  64.7 21.6 %collective-permute-start.18 = (bf16[1280,512]{1,0:T(8,128)(2,1)S(1)}, bf16[1280,512]{1,0:T(8,128)(2,1)S(1)}, u32[]{:S(2)}, u32[]{:S(2)}) collective-permute-start(bf16[1280,512]{1,0:T(8,128)(2,1)S(1)} %constant_dynamic-update-slice_fusion.20.low), channel_id=1, source_target_pairs={{0,8},{1,3},{2,10},{3,1},{4,12},{5,7},{6,14},{7,5},{8,0},{9,11},{1... | collective-permute-start | bytes 3932168 | tf_op jit(solution)/shard_map/ppermute | solution.py:340
  71.2 7.5 %collective-permute-start.16 = (bf16[1024,128]{1,0:T(8,128)(2,1)S(1)}, bf16[1024,128]{1,0:T(8,128)(2,1)S(1)}, u32[]{:S(2)}, u32[]{:S(2)}) collective-permute-start(bf16[1024,128]{1,0:T(8,128)(2,1)S(1)} %get-tuple-element.110), channel_id=1, source_target_pairs={{0,1},{1,0},{2,3},{3,2},{4,5},{5,4},{6,7},{7,6},{8,9},{9,8},{10,11... | collective-permute-start | bytes 786440 | tf_op jit(solution)/shard_map/ppermute | solution.py:340
  77.6 17.9 %collective-permute-start.19 = (bf16[1280,256]{1,0:T(8,128)(2,1)S(1)}, bf16[1280,256]{1,0:T(8,128)(2,1)S(1)}, u32[]{:S(2)}, u32[]{:S(2)}) collective-permute-start(bf16[1280,256]{1,0:T(8,128)(2,1)S(1)} %constant_dynamic-update-slice_fusion.22.low), channel_id=1, source_target_pairs={{0,2},{1,5},{2,0},{3,7},{4,6},{5,1},{6,4},{7,3},{8,10},{9,13},{10,... | collective-permute-start | bytes 1966088 | tf_op jit(solution)/shard_map/ppermute | solution.py:340
  104.1 31.6 %collective-permute-start.26 = (f32[512,1024]{1,0:T(8,128)}, f32[512,1024]{1,0:T(8,128)}, u32[]{:S(2)}, u32[]{:S(2)}) collective-permute-start(f32[512,1024]{1,0:T(8,128)} %get-tuple-element.148), channel_id=1, source_target_pairs={{0,1},{1,0},{2,3},{3,2},{4,5},{5,4},{6,7},{7,6},{8,9},{9,8},{10,11... | collective-permute-start | bytes 6291464 | tf_op jit(solution)/shard_map/ppermute | solution.py:340
  110.3 10.4 %collective-permute-start.23 = (bf16[512,128]{1,0:T(8,128)(2,1)S(1)}, bf16[512,128]{1,0:T(8,128)(2,1)S(1)}, u32[]{:S(2)}, u32[]{:S(2)}) collective-permute-start(bf16[512,128]{1,0:T(8,128)(2,1)S(1)} %get-tuple-element.139), channel_id=1, source_target_pairs={{0,16},{1,17},{2,18},{3,19},{4,20},{5,21},{6,22},{7,23},{8,24},{9,... | collective-permute-start | bytes 393224 | tf_op jit(solution)/shard_map/ppermute | solution.py:340
  121.4 10.0 %collective-permute-start.25 = (bf16[2,512,128]{2,1,0:T(8,128)(2,1)}, bf16[2,512,128]{2,1,0:T(8,128)(2,1)}, u32[]{:S(2)}, u32[]{:S(2)}) collective-permute-start(bf16[2,512,128]{2,1,0:T(8,128)(2,1)} %pad_maximum_fusion.2), channel_id=1, source_target_pairs={{0,8},{1,9},{2,10},{3,11},{4,12},{5,13},{6,14},{7,15},{8,0},{9,1},... | collective-permute-start | bytes 786440 | tf_op jit(solution)/shard_map/ppermute | solution.py:340
  125.8 9.9 %collective-permute-start.27 = (f32[512,256]{1,0:T(8,128)S(1)}, f32[512,256]{1,0:T(8,128)S(1)}, u32[]{:S(2)}, u32[]{:S(2)}) collective-permute-start(f32[512,256]{1,0:T(8,128)S(1)} %get-tuple-element.149), channel_id=1, source_target_pairs={{0,1},{1,0},{2,3},{3,2},{4,5},{5,4},{6,7},{7,6},{8,9},{9,8},{10,11... | collective-permute-start | bytes 1572872 | tf_op jit(solution)/shard_map/ppermute | solution.py:340
  132.4 7.5 %collective-permute-start.28 = (bf16[512,128]{1,0:T(8,128)(2,1)S(1)}, bf16[512,128]{1,0:T(8,128)(2,1)S(1)}, u32[]{:S(2)}, u32[]{:S(2)}) collective-permute-start(bf16[512,128]{1,0:T(8,128)(2,1)S(1)} %bitcast_select_fusion.1), channel_id=1, source_target_pairs={{0,4},{1,5},{2,6},{3,7},{4,0},{5,1},{6,2},{7,3},{8,12},{9,13},{10,... | collective-permute-start | bytes 393224 | tf_op jit(solution)/shard_map/ppermute | solution.py:340
  (10 other events, 125.8 us)

commit v4 on v3

--- a/solution.py
+++ b/solution.py
@@ -12,17 +12,19 @@
 LOG2E = 1.4426950408889634
 LANES = 128
 HALO = 16
+KEYS, ROW = 32, 64
 F32 = jnp.float32
 BF16 = jnp.bfloat16
 AXES = ("req", "seq")
 FLIPS = {"a": 16, "b": 8, "y": 4, "x": 2}
 ROUTES = (("axyb", "abxy"), ("abyx", "axby"), ("ayxb", "abyx"), ("aybx", "abxy"))
 PAIRS = ((0,), (1, 2, 3), (4, 5, 6, 7), (8, 9))
+CUT = 3
 SCHEDULE = (
     "0.0", "1.0", "tokens", "0.1", "2.0", "1.1", "0.2", "halo", "settings", "3.0",
     "2.1", "1.2", "0.3", "own", "3.1", "2.2", "1.3", "3.2", "2.3", "K0",
-    "3.3", "K1", "K2", "xA", "K3", "xB", "JA", "fA0", "JB", "fB0",
-    "fA1", "fB1", "fA2", "fB2", "norm", "fA3", "fB3",
+    "K1", "3.3", "K2", "xA", "K3", "xB", "JA", "fA0", "JB", "fB0",
+    "fA1", "norm", "fB1", "fA2", "fB2", "fA3", "fB3",
 )
 VMEM = pl.BlockSpec(memory_space=pltpu.VMEM)
 SMEM = pl.BlockSpec(memory_space=pltpu.SMEM)
@@ -93,18 +95,18 @@
         raw[pl.ds(at_theirs, span), :] = theirs[:, lanes(1)]
 
 
-def convolved(at, group, taps, padded):
-    total = taps[4:5, lanes(at)]
+def convolved(at, tap, group, taps, padded):
+    total = taps[4:5, lanes(tap)]
     for k in range(4):
         rows = padded[at, group * GROUP + 5 + k : (group + 1) * GROUP + 5 + k, :]
-        total = total + taps[k : k + 1, lanes(at)] * rows
+        total = total + taps[k : k + 1, lanes(tap)] * rows
     half = 0.5 * total
     return (half + half * jnp.tanh(half)).astype(BF16)
 
 
 def first_kernel(
     ints, own, other, low, high, taps, rates,
-    bc_out, x_out, cq_out, kq_out, kt_out, ca_out, tot_out,
+    bc_out, x_out, table_out, kt_out, tot_out,
     whole, padded, raw,
 ):
     project(0, ints, own, other, low, high, whole, padded, raw)
@@ -114,9 +116,9 @@
     before = jnp.zeros((1, LANES), F32)
     for group in range(bc_out.shape[0] // GROUP):
         rows = slice(group * GROUP, (group + 1) * GROUP)
-        bc_out[rows, :] = convolved(0, group, taps, padded)
+        bc_out[rows, :] = convolved(0, 0, group, taps, padded)
         for at in range(1, padded.shape[0]):
-            x_out[rows, lanes(at - 1)] = convolved(at, group, taps, padded)
+            x_out[rows, lanes(at - 1)] = convolved(at, at, group, taps, padded)
         ok = valid_rows(ints[2] + group * GROUP, GROUP, ints[0], ints[1])
         step = raw[rows, :] + rates[0:1, :]
         size = (jnp.maximum(step, 0.0) + jnp.log1p(jnp.exp(-jnp.abs(step)))) * ok
@@ -126,16 +128,21 @@
         mid_part, low_part = split(rest)
         cum = dot(below, high_part) + dot(below, mid_part) + dot(below, low_part)
         from_key = jnp.log2(size) - cum
-        cq_out[rows, :] = cum
-        kq_out[rows, :] = from_key
         kt_out[group] = from_key.T[0:32, :]
-        ca_out[rows, :] = cum + before
+        lane = lax.broadcasted_iota(jnp.int32, (GROUP, LANES), 1)
+        table = jnp.where(lane < KEYS, cum, pltpu.roll(from_key, KEYS, 1))
+        table_out[rows, :] = jnp.where(lane < ROW, table, pltpu.roll(cum + before, ROW, 1))
         before = before + cum[GROUP - 1 : GROUP, :]
     tot_out[...] = jnp.broadcast_to(before, tot_out.shape)
 
 
+def sorted_bc(ints, mine, theirs):
+    first = ints[3] == 0
+    return jnp.where(first, mine, theirs), jnp.where(first, theirs, mine)
+
+
 def scan_kernel(
-    chunk, heads, extra, ints, own, other, low, high, taps, x_ref, b_ref, c_ref, cq_ref, kq_ref,
+    chunk, held, heads, extra, ints, own, other, low, high, taps, x_ref, mine_ref, their_ref, table_ref,
     kt_ref, tot_ref, skip_ref, y_out, s_out, send_out, whole, padded, carry,
 ):
     project(chunk, ints, own, other, low, high, whole, padded, None)
@@ -148,9 +155,9 @@
     zero = jnp.zeros((GROUP, LANES), BF16)
     for group in range(y_out.shape[0] // GROUP):
         rows = slice(group * GROUP, (group + 1) * GROUP)
-        b, c = b_ref[rows, :], c_ref[rows, :]
+        b, c = sorted_bc(ints, mine_ref[rows, :], their_ref[rows, :])
         scores = lax.dot_general(c, b, (((1,), (1,)), ((), ())), preferred_element_type=F32)
-        cq, kq, kt = cq_ref[rows, :], kq_ref[rows, :], kt_ref[group]
+        table, kt = table_ref[rows, :], kt_ref[group]
         carried = None
         if group:
             upper, lower = split(carry[...])
@@ -160,10 +167,10 @@
             if i < extra:
                 x = x_ref[rows, lanes(i)]
             else:
-                x = convolved(i - extra, group, taps, padded)
+                x = convolved(i - extra, held[i] + 1, group, taps, padded)
             top, bottom, spread = [], [], []
             for h in (head, head + 1):
-                q = column(cq, h)
+                q = column(table, h)
                 spread.append(q)
                 k0 = jnp.broadcast_to(kt[h : h + 1, 0:half], (half, half))
                 k1 = jnp.broadcast_to(kt[h : h + 1, half:], (half, half))
@@ -180,12 +187,12 @@
             y_bottom = dot(jnp.concatenate(bottom, axis=1), jnp.concatenate([x0, x1], axis=0))
             q = jnp.where(left, spread[0], spread[1])
             xf = x.astype(F32)
-            rest = skip_ref[2:3, lanes(i)] * xf
+            rest = skip_ref[2:3, lanes(held[i])] * xf
             if group:
                 rest = rest + jnp.exp2(q) * carried[:, lanes(i)]
             y_out[group * GROUP : group * GROUP + half, lanes(i)] = y_top + rest[0:half]
             y_out[group * GROUP + half : (group + 1) * GROUP, lanes(i)] = y_bottom + rest[half:]
-            k = jnp.where(left, column(kq, head), column(kq, head + 1))
+            k = jnp.where(left, column(table, KEYS + head), column(table, KEYS + head + 1))
             end = q[GROUP - 1 : GROUP, :]
             scaled.append((jnp.exp2(k + end) * xf).astype(BF16))
             ends.append(jnp.exp2(end))
@@ -211,7 +218,7 @@
         )
 
 
-def join_kernel(heads, sizes, halves, ints, c_ref, ca_ref, tot_ref, r_ref, *refs):
+def join_kernel(heads, sizes, halves, ints, mine_ref, their_ref, table_ref, tot_ref, r_ref, *refs):
     count = len(sizes)
     y_refs, s_refs = refs[:count], refs[count : 2 * count]
     send_out, keep_out, fin_out = refs[2 * count :]
@@ -224,13 +231,15 @@
     from_head = lax.broadcasted_iota(jnp.int32, (2 * LANES, LANES), 0) % LANES
     second = lax.broadcasted_iota(jnp.int32, (2 * LANES, LANES), 1) // (LANES // 2)
     spread = jnp.concatenate(
-        [jnp.where(from_head == head + second, 1.0, 0.0).astype(BF16) for head in heads], axis=1
+        [jnp.where(from_head == ROW + head + second, 1.0, 0.0).astype(BF16) for head in heads], axis=1
     )
     for out, at in ((send_out, (1 - core) * span), (keep_out, core * span)):
         rows = pl.ds(pl.multiple_of(at, span), span)
-        decay = jnp.exp2(ca_ref[rows, :])
+        lane = lax.broadcasted_iota(jnp.int32, (span, LANES), 1)
+        decay = jnp.exp2(jnp.where(lane < ROW, 0.0, table_ref[rows, :]))
         decay = dot(jnp.concatenate(split(decay), axis=1), spread)
-        carried = dot(c_ref[rows, :], entering)
+        _, c = sorted_bc(ints, mine_ref[rows, :], their_ref[rows, :])
+        carried = dot(c, entering)
         for i in range(len(heads)):
             j, k = where[i]
             out[:, lanes(i)] = (
@@ -280,9 +289,9 @@
     return jnp.where(lane < 2 * share, lane + core * share + (lane // share) * share, -1)
 
 
-def chosen_heads(core, heads):
-    row = lax.broadcasted_iota(jnp.int32, (heads, LANES), 0)
-    lane = lax.broadcasted_iota(jnp.int32, (heads, LANES), 1)
+def chosen_heads(core, heads, rows):
+    row = lax.broadcasted_iota(jnp.int32, (rows, LANES), 0)
+    lane = lax.broadcasted_iota(jnp.int32, (rows, LANES), 1)
     return jnp.where(row == head_of(lane, core, heads // 4), 1.0, 0.0)
 
 
@@ -295,17 +304,17 @@
 
 
 def sort_kernel(inner, ints, mix, step, kept_out, given_out):
-    for out, core in ((kept_out, ints[3]), (given_out, 1 - ints[3])):
+    for out, core in ((kept_out, ints[1]), (given_out, 1 - ints[1])):
         parts = columns_of(mix, core, inner)
         out[:, lanes(0)] = parts[0]
-        out[:, lanes(1)] = dot(step[...], chosen_heads(core, step.shape[1]).astype(BF16)).astype(BF16)
+        out[:, lanes(1)] = dot(step[...], chosen_heads(core, step.shape[1], step.shape[1]).astype(BF16)).astype(BF16)
         for i, part in enumerate(parts[1:]):
             out[:, lanes(2 + i)] = part
 
 
 def stack_kernel(ints, kept, got, *outs):
     rows = kept.shape[0]
-    core = ints[3]
+    core = ints[1]
     at = 0
     for out in outs:
         width = out.shape[1]
@@ -314,19 +323,34 @@
         at += width
 
 
-def settings_kernel(inner, ints, conv, bias, per_head, taps_out, rates_out, skip_out):
-    core = ints[3]
-    for i, (tap, more) in enumerate(
-        zip(columns_of(conv, core, inner), columns_of(bias, core, inner), strict=True)
-    ):
-        taps_out[0:4, lanes(i)] = tap
-        taps_out[4:5, lanes(i)] = more
-        taps_out[5:8, lanes(i)] = jnp.zeros((3, LANES), F32)
-    heads = per_head.shape[1]
+def settings_kernel(
+    inner, place, deal, lengths, starts, small, ints_out, taps_out, rates_out, skip_out
+):
+    request, wanted, near = jnp.int32(0), jnp.int32(0), jnp.int32(0)
+    req = place[4]
+    for i in range(deal.shape[0]):
+        request = jnp.where(req == i, deal[i], request)
+        wanted = jnp.where(deal[i] == req, i, wanted)
+        near = jnp.where(deal[i] == jnp.bitwise_xor(req, 1), i, near)
+    start, length = jnp.int32(0), jnp.int32(0)
+    for i in range(deal.shape[0]):
+        start = jnp.where(request == i, starts[i], start)
+        length = jnp.where(request == i, lengths[i], length)
+    ints_out[0] = start
+    ints_out[1] = start + length
+    for i in range(4):
+        ints_out[2 + i] = place[i]
+    ints_out[6] = wanted
+    ints_out[7] = near
+    core = place[1]
+    for i, part in enumerate(columns_of(small, core, inner)):
+        row = lax.broadcasted_iota(jnp.int32, (8, LANES), 0)
+        taps_out[:, lanes(i)] = jnp.where(row < 5, part[0:8], 0.0)
+    heads = inner // LANES * 2
     exact = functools.partial(
         jnp.dot, precision=lax.Precision.HIGHEST, preferred_element_type=F32
     )
-    own = exact(per_head[...], chosen_heads(core, heads))
+    own = exact(small[8:16, 0:LANES], chosen_heads(core, heads, LANES))
     rates_out[...] = own
     row = lax.broadcasted_iota(jnp.int32, (LANES, inner // 2), 0)
     lane = lax.broadcasted_iota(jnp.int32, (LANES, inner // 2), 1)
@@ -355,15 +379,8 @@
     nstate = (mix_weight.shape[1] - inner) // 2
     share = heads // 4
     quarter = inner // 4
-    slots = jnp.arange(deal.shape[0], dtype=jnp.int32)
-    request = jnp.sum(jnp.where(slots == req_index, deal, 0))
-    length = jnp.sum(jnp.where(slots == request, prompt_len, 0))
-    start = jnp.sum(jnp.where(slots == request, prompt_start, 0))
-    wanted = jnp.sum(jnp.where(deal == req_index, slots, 0))
-    partner_wanted = jnp.sum(jnp.where(deal == (req_index ^ 1), slots, 0))
     chip = req_index * 2 + along
-    place = jnp.stack([along * 2 * span, core, along, chip])
-    early_ints = jnp.concatenate([jnp.zeros((2,), jnp.int32), place])
+    place = jnp.stack([along * 2 * span, core, along, chip, req_index])
     state = {}
 
     def after(*values):
@@ -382,7 +399,7 @@
         out_shape=[jax.ShapeDtypeStruct((portion, total), BF16)] * 2,
         compiler_params=params(8),
         name="sort",
-    )(early_ints, mix_weight, step_weight)
+    )(place, mix_weight, step_weight)
     got = swapped(given, (1, 1))
     blocks = pl.pallas_call(
         stack_kernel,
@@ -391,7 +408,7 @@
         out_shape=[jax.ShapeDtypeStruct((2 * portion, width), BF16) for width in widths],
         compiler_params=params(8),
         name="stack",
-    )(early_ints, kept, got)
+    )(place, kept, got)
     blocks = list(blocks)
     arrived = [None] * len(widths)
 
@@ -411,35 +428,32 @@
         return pl.pallas_call(
             first_kernel,
             in_specs=[SMEM] + [VMEM] * 6,
-            out_specs=[VMEM] * 7,
+            out_specs=[VMEM] * 5,
             scratch_shapes=scratch(width, 1 + extra) + [pltpu.VMEM((chip_rows, LANES), F32)],
             out_shape=[
                 jax.ShapeDtypeStruct((chip_rows, LANES), BF16),
                 jax.ShapeDtypeStruct((chip_rows, extra * LANES), BF16),
                 jax.ShapeDtypeStruct((chip_rows, LANES), F32),
-                jax.ShapeDtypeStruct((chip_rows, LANES), F32),
                 jax.ShapeDtypeStruct((groups, 32, GROUP), F32),
-                jax.ShapeDtypeStruct((chip_rows, LANES), F32),
                 jax.ShapeDtypeStruct((8, LANES), F32),
             ],
-            compiler_params=params(24),
+            compiler_params=params(28),
             cost_estimate=pl.CostEstimate(
                 flops=2 * chip_rows * depth * width, bytes_accessed=9000000, transcendentals=500000
             ),
             name="first",
-        )(ints, own, other, low, high, taps[:, : (1 + extra) * LANES], rates)
-
-    def scanned(index, ints, own, other, low, high, taps, skip, x0, b, c, cq, kq, kt, tot):
+        )(ints, own, other, low, high, taps, rates)
+
+    def scanned(index, ints, own, other, low, high, taps, skip, x0, mine, theirs, table, kt, tot):
         more = extra if index == 1 else 0
         held = (PAIRS[0] if more else ()) + PAIRS[index]
         pairs = len(held)
         new = pairs - more
         firsts = [first_head(p, share) for p in held]
-        tap_at, skip_at = (1 + PAIRS[index][0]) * LANES, held[0] * LANES
         width = widths[index]
         return pl.pallas_call(
-            functools.partial(scan_kernel, index, firsts, more),
-            in_specs=[SMEM] + [VMEM] * 13,
+            functools.partial(scan_kernel, index, held, firsts, more),
+            in_specs=[SMEM] + [VMEM] * 12,
             out_specs=[VMEM] * 3,
             scratch_shapes=scratch(width, new) + [pltpu.VMEM((LANES, pairs * LANES), F32)],
             out_shape=[
@@ -455,17 +469,17 @@
             ),
             name="scan",
         )(
-            ints, own, other, low, high, taps[:, tap_at : tap_at + new * LANES],
-            x0, b, c, cq, kq, kt, tot, skip[:, skip_at : skip_at + pairs * LANES],
+            ints, own, other, low, high, taps,
+            x0, mine, theirs, table, kt, tot, skip,
         )
 
-    def joined(held, ints, c, ca, tot, ys, ss, r):
+    def joined(held, ints, mine, theirs, table, tot, ys, ss, r):
         pairs = len(held)
         halves = [(i, i + 1) for i in range(0, pairs, 2)]
         sizes = [y.shape[1] // LANES for y in ys]
         return pl.pallas_call(
             functools.partial(join_kernel, [first_head(p, share) for p in held], sizes, halves),
-            in_specs=[SMEM] + [VMEM] * (4 + 2 * len(ys)),
+            in_specs=[SMEM] + [VMEM] * (5 + 2 * len(ys)),
             out_specs=[VMEM] * 3,
             out_shape=[
                 jax.ShapeDtypeStruct((span, pairs * LANES), F32),
@@ -479,14 +493,14 @@
                 transcendentals=chip_rows * pairs * LANES,
             ),
             name="join",
-        )(ints, c, ca, tot, r, *ys, *ss)
-
-    early_pairs = sum(PAIRS[:-1], ())
+        )(ints, mine, theirs, table, tot, r, *ys, *ss)
+
+    early_pairs, late_pairs = sum(PAIRS[:CUT], ()), sum(PAIRS[CUT:], ())
 
     def normed(ints, keep_a, keep_b, got_a, got_b):
         places = [
             [(p % 2) * (2 * quarter // LANES) + p // 2 for p in held]
-            for held in (early_pairs, PAIRS[-1])
+            for held in (early_pairs, late_pairs)
         ]
         block = span // 2
         return pl.pallas_call(
@@ -502,7 +516,7 @@
                 out_specs=pl.BlockSpec((block, inner), lambda i, ints: (i, 0)),
             ),
             out_shape=jax.ShapeDtypeStruct((span, inner), BF16),
-            compiler_params=params(24),
+            compiler_params=params(28),
             cost_estimate=pl.CostEstimate(
                 flops=6 * span * inner, bytes_accessed=6 * span * inner, transcendentals=span
             ),
@@ -539,31 +553,41 @@
             v["token"] = edge
             v["halo"] = lax.ppermute(edge, AXES, route)
         elif event == "settings":
-            front = jnp.stack([start, start + length])
-            v["ints"] = after(jnp.concatenate([front, place]))
-            per_head = jnp.concatenate(
-                [jnp.stack([step_bias, decay_rate * (-LOG2E), skip_gain]), jnp.zeros((5, heads))]
+            half = inner // 2
+
+            conv_w, conv_b, step_b, rate, gain = after(
+                conv_weight, conv_bias, step_bias, decay_rate, skip_gain
             )
-            half = inner // 2
-            v["taps"], v["rates"], v["skip"] = pl.pallas_call(
+
+            def row(values):
+                return jnp.pad(values, (0, conv_weight.shape[1] - values.shape[0]))[None]
+
+            small = jnp.concatenate(
+                [conv_w, conv_b[None], jnp.zeros((3, conv_w.shape[1]), F32)]
+                + [row(step_b), row(rate * (-LOG2E)), row(gain)]
+                + [jnp.zeros((5, conv_weight.shape[1]), F32)],
+                axis=0,
+            )
+            v["ints"], v["taps"], v["rates"], v["skip"] = pl.pallas_call(
                 functools.partial(settings_kernel, inner),
-                in_specs=[SMEM, VMEM, VMEM, VMEM],
-                out_specs=[VMEM] * 3,
+                in_specs=[SMEM] * 4 + [VMEM],
+                out_specs=[SMEM] + [VMEM] * 3,
                 out_shape=[
+                    jax.ShapeDtypeStruct((8,), jnp.int32),
                     jax.ShapeDtypeStruct((8, half + LANES), F32),
                     jax.ShapeDtypeStruct((8, LANES), F32),
                     jax.ShapeDtypeStruct((8, half), F32),
                 ],
                 compiler_params=params(8),
                 name="settings",
-            )(v["ints"], conv_weight, conv_bias[None], per_head)
+            )(after(place), deal, prompt_len, prompt_start, small)
             v["token"] = v["rates"]
         elif event == "own":
             v["own"] = jnp.concatenate([after(v["halo"]), rows], axis=0)
             v["token"] = v["own"]
         elif event == "K0":
             ints = after(v["ints"])
-            bc, x0, cq, kq, kt, ca, tot = projected(
+            bc, x0, table, kt, tot = projected(
                 ints, v["own"], v["other"], blocks[0], arrived[0], v["taps"], v["rates"]
             )
             v["token"] = tot
@@ -571,17 +595,15 @@
         elif event[0] == "K":
             i = int(event[1:])
             if i == 1:
-                two = after(v["bc"])
-                b = jnp.where(core == 0, bc, two)
-                c = jnp.where(core == 0, two, bc)
+                theirs = after(v["bc"])
             ints = after(v["ints"])
             v["y", i], v["s", i], v["t", i] = scanned(
                 i, ints, v["own"], v["other"], blocks[i], arrived[i], v["taps"], v["skip"],
-                x0, b, c, cq, kq, kt, tot,
+                x0, bc, theirs, table, kt, tot,
             )
             v["token"] = v["t", i]
         elif event in ("xA", "xB"):
-            which = range(1, last) if event == "xA" else (last,)
+            which = range(1, CUT) if event == "xA" else range(CUT, last + 1)
             sent = [v["t", i] for i in which]
             if len(sent) > 1:
                 sent = jnp.concatenate(after(*sent), axis=1)
@@ -590,11 +612,11 @@
                 sent = sent[0]
             v["r", event[1]] = swapped(sent, (2, 2))
         elif event in ("JA", "JB"):
-            which = range(1, last) if event == "JA" else (last,)
-            held = early_pairs if event == "JA" else PAIRS[last]
+            which = range(1, CUT) if event == "JA" else range(CUT, last + 1)
+            held = early_pairs if event == "JA" else late_pairs
             ints, r = after(v["ints"], v["r", event[1]])
             send, v["keep", event[1]], v["fin", event[1]] = joined(
-                held, ints, c, ca, tot, [v["y", i] for i in which], [v["s", i] for i in which], r
+                held, ints, bc, theirs, table, tot, [v["y", i] for i in which], [v["s", i] for i in which], r
             )
             v["token"] = v["fin", event[1]]
             v["got", event[1]] = swapped(send, (1, 1))
@@ -609,13 +631,13 @@
             elif event[2] == "2":
                 cand = (v["fin", key], v["one", key], after(v["two", key]))
                 v["cand", key] = cand
-                v["picked", key] = pick(partner_wanted, cand)
+                v["picked", key] = pick(v["ints"][7], cand)
                 v["token"] = v["picked", key]
                 v["three", key] = swapped(v["picked", key], (4, 4))
             else:
                 three = after(v["three", key])
-                odd = (wanted ^ req_index) & 1
-                v["final", key] = jnp.where(odd == 1, three, pick(wanted, v["cand", key])).astype(
+                odd = (v["ints"][6] ^ req_index) & 1
+                v["final", key] = jnp.where(odd == 1, three, pick(v["ints"][6], v["cand", key])).astype(
                     F32
                 )
                 v["token"] = v["final", key]

time: 142 us -> 139 us (0.979)
  local copies, waits for them, and re-layouts: 6.04 us -> 13.6 us
  starting transfers between devices: 51.3 us -> 45.4 us
  other arithmetic: 9.39 us -> 4.59 us
  waiting for transfers between devices: 33.9 us -> 37.9 us
  Pallas kernels: 37.6 us -> 34.3 us
    ppermute x29, starting transfers between devices: 48.8 us -> 42.9 us  [swapped(): return lax.ppermute(x, AXES, [(i, i ^ masks[i % 2]) for i in range(count)])]
    concatenate x12, local copies, waits for them, and re-layouts: 2.25 us -> 6.4 us  [on_device(): blocks[i] = jnp.concatenate(after(blocks[i], arrived[i]), axis=0)]
    ppermute x29, waiting for transfers between devices: 33.9 us -> 37.9 us  [swapped(): return lax.ppermute(x, AXES, [(i, i ^ masks[i % 2]) for i in range(count)])]
    unnamed x22 -> x34, local copies, waits for them, and re-layouts: 2.14 us -> 5.48 us
    reduce_sum x2 -> x0, other arithmetic: 3.33 us -> none  [the longest x1 2.04 us: on_device(): start = jnp.sum(jnp.where(slots == request, prompt_start, 0))]
    pallas_call x4, Pallas kernels: 21.8 us -> 18.6 us  [the longest x3 17.2 us: scanned(): pl.pallas_call(functools.partial(scan_kernel, index, held, firsts, more),...]
  transfers between devices with their start and end apart: 30 -> 30, of which waited for: 10 -> 11; matrix products, arithmetic and copies ran while one was open for 10% -> 12% of each run, Pallas kernels for 24% -> 23%
where the time goes in v4:
time: 139 us; the launch traced here: 138 us
  starting transfers between devices  45.4 us (33%)
  waiting for transfers between devices  37.9 us (27%)
  Pallas kernels  34.3 us (25%)
  local copies, waits for them, and re-layouts  13.6 us (10%)
  other arithmetic  4.59 us (3%)
  between operations  2.39 us (2%)
    ppermute x29, starting transfers between devices, swapped(): return lax.ppermute(x, AXES, [(i, i ^ masks[i % 2]) for i in range(count)])  42.9 us
    ppermute x29, waiting for transfers between devices, swapped(): return lax.ppermute(x, AXES, [(i, i ^ masks[i % 2]) for i in range(count)])  37.9 us
    pallas_call x3, Pallas kernels, scanned(): pl.pallas_call(functools.partial(scan_kernel, index, held, firsts, more),...  17.2 us
    concatenate x12, local copies, waits for them, and re-layouts, on_device(): blocks[i] = jnp.concatenate(after(blocks[i], arrived[i]), axis=0)  6.4 us
    unnamed x34, local copies, waits for them, and re-layouts  5.48 us
    pallas_call x1, Pallas kernels, projected(): pl.pallas_call(first_kernel, in_specs=[SMEM] + [VMEM] * 6, out_specs=[VME...  5.39 us
    pallas_call x2, Pallas kernels, joined(): pl.pallas_call(functools.partial(join_kernel, [first_head(p, share) for p...  4.81 us
    pallas_call x1, Pallas kernels, normed(): pl.pallas_call(functools.partial(norm_kernel, places), grid_spec=pltpu.Pr...  4.11 us
  transfers between devices with their start and end apart: 30, of which 11 were waited for; matrix products, arithmetic and copies ran while one was open for 12% of the time, Pallas kernels for 23%

profile of v4, /device:TPU:0, one launch (start us, length us, event | category | flops | bytes accessed | tf_op | source)
XLA Modules:
  0.0 138.2 jit_solution(1363376483013213835)
XLA Ops:
  4.0 2.1 %collective-permute-done.1.got = bf16[80,1536]{1,0:T(8,128)(2,1)S(1)} collective-permute-done((bf16[80,1536]{1,0:T(8,128)(2,1)S(1)}, bf16[80,1536]{1,0:T(8,128)(2,1)S(1)}, u32[]{:S(2)}, u32[]{:S(2)}) %collective-permute-start.1) | collective-permute-done | bytes 245792 | tf_op jit(solution)/shard_map/ppermute | solution.py:364
  6.7 4.0 %collective-permute-start.2 = (bf16[160,384]{1,0:T(8,128)(2,1)S(1)}, bf16[160,384]{1,0:T(8,128)(2,1)S(1)}, u32[]{:S(2)}, u32[]{:S(2)}) collective-permute-start(bf16[160,384]{1,0:T(8,128)(2,1)S(1)} %get-tuple-element.82), channel_id=1, source_target_pairs={{0,16},{1,17},{2,18},{3,19},{4,20},{5,21},{6,22},{7,23},{8,24},{9,... | collective-permute-start | bytes 368648 | tf_op jit(solution)/shard_map/ppermute | solution.py:364
  10.8 9.3 %collective-permute-done.2 = bf16[160,384]{1,0:T(8,128)(2,1)S(1)} collective-permute-done((bf16[160,384]{1,0:T(8,128)(2,1)S(1)}, bf16[160,384]{1,0:T(8,128)(2,1)S(1)}, u32[]{:S(2)}, u32[]{:S(2)}) %collective-permute-start.2) | collective-permute-done | bytes 122912 | tf_op jit(solution)/shard_map/ppermute | solution.py:364
  20.1 1.9 %collective-permute-start.3 = (bf16[320,384]{1,0:T(8,128)(2,1)S(1)}, bf16[320,384]{1,0:T(8,128)(2,1)S(1)}, u32[]{:S(2)}, u32[]{:S(2)}) collective-permute-start(bf16[320,384]{1,0:T(8,128)(2,1)S(1)} %constant_dynamic-update-slice_fusion), channel_id=1, source_target_pairs={{0,2},{1,9},{2,0},{3,11},{4,6},{5,13},{6,4},{7,15},{8,10},{9,1},{1... | collective-permute-start | bytes 737288 | tf_op jit(solution)/shard_map/ppermute | solution.py:364
  22.0 2.9 %collective-permute-start.11 = (bf16[160,256]{1,0:T(8,128)(2,1)S(1)}, bf16[160,256]{1,0:T(8,128)(2,1)}, u32[]{:S(2)}, u32[]{:S(2)}) collective-permute-start(bf16[160,256]{1,0:T(8,128)(2,1)S(1)} %get-tuple-element.105), channel_id=1, source_target_pairs={{0,16},{1,17},{2,18},{3,19},{4,20},{5,21},{6,22},{7,23},{8,24},{9,... | collective-permute-start | bytes 245768 | tf_op jit(solution)/shard_map/ppermute | solution.py:364
  31.5 2.5 %collective-permute-start.5 = (bf16[16,2560]{1,0:T(8,128)(2,1)S(1)}, bf16[16,2560]{1,0:T(8,128)(2,1)S(1)}, u32[]{:S(2)}, u32[]{:S(2)}) collective-permute-start(bf16[16,2560]{1,0:T(8,128)(2,1)S(1)} %bitcast_select_fusion.2), channel_id=1, source_target_pairs={{0,2},{1,3},{4,6},{5,7},{8,10},{9,11},{12,14},{13,15},{16,18},{17,... | collective-permute-start | bytes 245768 | tf_op jit(solution)/shard_map/ppermute | solution.py:554
  46.8 7.1 %collective-permute-done.9 = bf16[640,384]{1,0:T(8,128)(2,1)S(1)} collective-permute-done((bf16[640,384]{1,0:T(8,128)(2,1)S(1)}, bf16[640,384]{1,0:T(8,128)(2,1)S(1)}, u32[]{:S(2)}, u32[]{:S(2)}) %collective-permute-start.9) | collective-permute-done | bytes 491552 | tf_op jit(solution)/shard_map/ppermute | solution.py:364
  54.2 3.3 %collective-permute-done.14 = bf16[320,256]{1,0:T(8,128)(2,1)S(1)} collective-permute-done((bf16[320,256]{1,0:T(8,128)(2,1)S(1)}, bf16[320,256]{1,0:T(8,128)(2,1)S(1)}, u32[]{:S(2)}, u32[]{:S(2)}) %collective-permute-start.14) | collective-permute-done | bytes 163872 | tf_op jit(solution)/shard_map/ppermute | solution.py:364
  57.6 2.8 %collective-permute-start.18 = (bf16[1280,512]{1,0:T(8,128)(2,1)S(1)}, bf16[1280,512]{1,0:T(8,128)(2,1)S(1)}, u32[]{:S(2)}, u32[]{:S(2)}) collective-permute-start(bf16[1280,512]{1,0:T(8,128)(2,1)S(1)} %constant_dynamic-update-slice_fusion.20.low), channel_id=1, source_target_pairs={{0,8},{1,3},{2,10},{3,1},{4,12},{5,7},{6,14},{7,5},{8,0},{9,11},{1... | collective-permute-start | bytes 3932168 | tf_op jit(solution)/shard_map/ppermute | solution.py:364
  60.4 5.4 %first.1 = (bf16[1024,128]{1,0:T(8,128)(2,1)S(1)}, bf16[1024,128]{1,0:T(8,128)(2,1)S(1)}, f32[1024,128]{1,0:T(8,128)S(1)}, f32[4,32,256]{2,1,0:T(8,128)S(1)}, f32[8,128]{1,0:T(8,128)S(1)}) custom-call(s32[8]{0:T(128)S(1)} %get-tuple-element.147.ints, bf16[528,2560]{1,0:T(8,128)(2,1)S(1)} %pad_maximum_fusion.own, ...), custom_call_target="tpu_custom_call" | custom-call | flops 2013265920 | bytes 9000000 | tf_op jit(solution)/shard_map/first/pallas_call | solution.py:428
  65.8 9.0 %collective-permute-start.16 = (bf16[1024,128]{1,0:T(8,128)(2,1)S(1)}, bf16[1024,128]{1,0:T(8,128)(2,1)S(1)}, u32[]{:S(2)}, u32[]{:S(2)}) collective-permute-start(bf16[1024,128]{1,0:T(8,128)(2,1)S(1)} %get-tuple-element.118.mine_ref), channel_id=1, source_target_pairs={{0,1},{1,0},{2,3},{3,2},{4,5},{5,4},{6,7},{7,6},{8,9},{9,8},{10,11... | collective-permute-start | bytes 786440 | tf_op jit(solution)/shard_map/ppermute | solution.py:364
  76.3 6.5 %scan.3 = (f32[1024,512]{1,0:T(8,128)S(1)}, f32[128,512]{1,0:T(8,128)S(1)}, bf16[144,512]{1,0:T(8,128)(2,1)S(1)}) custom-call(s32[8]{0:T(128)S(1)} %get-tuple-element.147.ints, bf16[528,2560]{1,0:T(8,128)(2,1)S(1)} %pad_maximum_fusion.own, bf16[512,2560]{1,0:T(8,128)(2,1)S(1)} %collective-permute-done.other, ...), custom_call_target="tpu_custom_call" | custom-call | flops 4413265920 | bytes 12000000 | tf_op jit(solution)/shard_map/scan/pallas_call | solution.py:454
  82.9 6.9 %scan.4 = (f32[1024,512]{1,0:T(8,128)S(1)}, f32[128,512]{1,0:T(8,128)S(1)}, bf16[144,512]{1,0:T(8,128)(2,1)S(1)}) custom-call(s32[8]{0:T(128)S(1)} %get-tuple-element.147.ints, bf16[528,2560]{1,0:T(8,128)(2,1)S(1)} %pad_maximum_fusion.own, bf16[512,2560]{1,0:T(8,128)(2,1)S(1)} %collective-permute-done.other, ...), custom_call_target="tpu_custom_call" | custom-call | flops 5084354560 | bytes 12000000 | tf_op jit(solution)/shard_map/scan/pallas_call | solution.py:454
  89.8 2.1 %collective-permute-start.19 = (bf16[144,1024]{1,0:T(8,128)(2,1)S(1)}, bf16[144,1024]{1,0:T(8,128)(2,1)S(1)}, u32[]{:S(2)}, u32[]{:S(2)}) collective-permute-start(bf16[144,1024]{1,0:T(8,128)(2,1)S(1)} %constant_dynamic-update-slice_fusion.24), channel_id=1, source_target_pairs={{0,2},{1,3},{2,0},{3,1},{4,6},{5,7},{6,4},{7,5},{8,10},{9,11},{10,... | collective-permute-start | bytes 884744 | tf_op jit(solution)/shard_map/ppermute | solution.py:364
  93.5 3.9 %scan.5 = (f32[1024,256]{1,0:T(8,128)S(1)}, f32[128,256]{1,0:T(8,128)S(1)}, bf16[144,256]{1,0:T(8,128)(2,1)S(1)}) custom-call(s32[8]{0:T(128)S(1)} %get-tuple-element.147.ints, bf16[528,2560]{1,0:T(8,128)(2,1)S(1)} %pad_maximum_fusion.own, bf16[512,2560]{1,0:T(8,128)(2,1)S(1)} %collective-permute-done.other, ...), custom_call_target="tpu_custom_call" | custom-call | flops 2542177280 | bytes 12000000 | tf_op jit(solution)/shard_map/scan/pallas_call | solution.py:454
  98.2 3.1 %join.2 = (f32[512,1024]{1,0:T(8,128)}, f32[512,1024]{1,0:T(8,128)S(1)}, bf16[512,128]{1,0:T(8,128)(2,1)S(1)}) custom-call(s32[8]{0:T(128)S(1)} %get-tuple-element.147.ints, bf16[1024,128]{1,0:T(8,128)(2,1)S(1)} %get-tuple-element.118.mine_ref, bf16[1024,128]{1,0:T(8,128)(2,1)S(1)} %collective-permute-done.16.their_ref, ...), custom_call_target="tpu_custom_call" | custom-call | flops 536870912 | bytes 8388608 | tf_op jit(solution)/shard_map/join/pallas_call | solution.py:480
  101.3 1.9 %collective-permute-start.23 = (f32[512,1024]{1,0:T(8,128)}, f32[512,1024]{1,0:T(8,128)}, u32[]{:S(2)}, u32[]{:S(2)}) collective-permute-start(f32[512,1024]{1,0:T(8,128)} %get-tuple-element.150), channel_id=1, source_target_pairs={{0,1},{1,0},{2,3},{3,2},{4,5},{5,4},{6,7},{7,6},{8,9},{9,8},{10,11... | collective-permute-start | bytes 6291464 | tf_op jit(solution)/shard_map/ppermute | solution.py:364
  104.7 2.8 %collective-permute-done.22.r_ref = bf16[144,256]{1,0:T(8,128)(2,1)S(1)} collective-permute-done((bf16[144,256]{1,0:T(8,128)(2,1)S(1)}, bf16[144,256]{1,0:T(8,128)(2,1)S(1)}, u32[]{:S(2)}, u32[]{:S(2)}) %collective-permute-start.22) | collective-permute-done | bytes 73760 | tf_op jit(solution)/shard_map/ppermute | solution.py:364
  107.5 1.7 %join.3 = (f32[512,256]{1,0:T(8,128)}, f32[512,256]{1,0:T(8,128)S(1)}, bf16[128,128]{1,0:T(8,128)(2,1)S(1)}) custom-call(s32[8]{0:T(128)S(1)} %get-tuple-element.147.ints, bf16[1024,128]{1,0:T(8,128)(2,1)S(1)} %get-tuple-element.118.mine_ref, bf16[1024,128]{1,0:T(8,128)(2,1)S(1)} %collective-permute-done.16.their_ref, ...), custom_call_target="tpu_custom_call" | custom-call | flops 134217728 | bytes 2097152 | tf_op jit(solution)/shard_map/join/pallas_call | solution.py:480
  109.3 2.9 %collective-permute-start.21 = (bf16[512,128]{1,0:T(8,128)(2,1)S(1)}, bf16[512,128]{1,0:T(8,128)(2,1)S(1)}, u32[]{:S(2)}, u32[]{:S(2)}) collective-permute-start(bf16[512,128]{1,0:T(8,128)(2,1)S(1)} %get-tuple-element.145), channel_id=1, source_target_pairs={{0,16},{1,17},{2,18},{3,19},{4,20},{5,21},{6,22},{7,23},{8,24},{9,... | collective-permute-start | bytes 393224 | tf_op jit(solution)/shard_map/ppermute | solution.py:364
  112.2 7.0 %collective-permute-done.21 = bf16[512,128]{1,0:T(8,128)(2,1)S(1)} collective-permute-done((bf16[512,128]{1,0:T(8,128)(2,1)S(1)}, bf16[512,128]{1,0:T(8,128)(2,1)S(1)}, u32[]{:S(2)}, u32[]{:S(2)}) %collective-permute-start.21) | collective-permute-done | bytes 131104 | tf_op jit(solution)/shard_map/ppermute | solution.py:364
  119.9 3.1 %collective-permute-start.26 = (bf16[128,128]{1,0:T(8,128)(2,1)S(1)}, bf16[128,128]{1,0:T(8,128)(2,1)S(1)}, u32[]{:S(2)}, u32[]{:S(2)}) collective-permute-start(bf16[128,128]{1,0:T(8,128)(2,1)S(1)} %get-tuple-element.152), channel_id=1, source_target_pairs={{0,16},{1,17},{2,18},{3,19},{4,20},{5,21},{6,22},{7,23},{8,24},{9,... | collective-permute-start | bytes 98312 | tf_op jit(solution)/shard_map/ppermute | solution.py:364
  125.0 4.1 %norm.1 = bf16[512,2560]{1,0:T(8,128)(2,1)} custom-call(s32[8]{0:T(128)S(1)} %get-tuple-element.147.ints, f32[1,2560]{1,0:T(1,128)S(1)} %broadcast_in_dim.30.gain_ref, f32[512,1024]{1,0:T(8,128)S(1)} %get-tuple-element.148.ka_ref, f32[512,256]{1,0:T(8,128)S(1)} %get-tuple-element.149.kb_ref, f32[512,1024]{1,0:T(8,128)} %collective-permute-done.23.ra_ref, ...), custom_call_target="tpu_custom_call" | custom-call | flops 7864320 | bytes 7864320 | tf_op jit(solution)/shard_map/norm/pallas_call | solution.py:506
  134.1 2.0 %collective-permute-done.27 = bf16[512,128]{1,0:T(8,128)(2,1)S(1)} collective-permute-done((bf16[512,128]{1,0:T(8,128)(2,1)S(1)}, bf16[512,128]{1,0:T(8,128)(2,1)S(1)}, u32[]{:S(2)}, u32[]{:S(2)}) %collective-permute-start.27) | collective-permute-done | bytes 131104 | tf_op jit(solution)/shard_map/ppermute | solution.py:364
  (116 shorter events, 37.4 us)
Async XLA Ops:
  0.7 29.9 %collective-permute-start = (bf16[512,2560]{1,0:T(8,128)(2,1)}, bf16[512,2560]{1,0:T(8,128)(2,1)S(1)}, u32[]{:S(2)}, u32[]{:S(2)}) collective-permute-start(bf16[512,2560]{1,0:T(8,128)(2,1)} %bitcast.34), channel_id=1, source_target_pairs={{0,1},{1,0},{2,3},{3,2},{4,5},{5,4},{6,7},{7,6},{8,9},{9,8},{10,11... | collective-permute-start | bytes 7864328 | tf_op jit(solution)/shard_map/ppermute | solution.py:364
  6.7 13.4 %collective-permute-start.2 = (bf16[160,384]{1,0:T(8,128)(2,1)S(1)}, bf16[160,384]{1,0:T(8,128)(2,1)S(1)}, u32[]{:S(2)}, u32[]{:S(2)}) collective-permute-start(bf16[160,384]{1,0:T(8,128)(2,1)S(1)} %get-tuple-element.82), channel_id=1, source_target_pairs={{0,16},{1,17},{2,18},{3,19},{4,20},{5,21},{6,22},{7,23},{8,24},{9,... | collective-permute-start | bytes 368648 | tf_op jit(solution)/shard_map/ppermute | solution.py:364
  10.7 14.2 %collective-permute-start.4 = (bf16[160,384]{1,0:T(8,128)(2,1)S(1)}, bf16[160,384]{1,0:T(8,128)(2,1)}, u32[]{:S(2)}, u32[]{:S(2)}) collective-permute-start(bf16[160,384]{1,0:T(8,128)(2,1)S(1)} %get-tuple-element.84), channel_id=1, source_target_pairs={{0,16},{1,17},{2,18},{3,19},{4,20},{5,21},{6,22},{7,23},{8,24},{9,... | collective-permute-start | bytes 368648 | tf_op jit(solution)/shard_map/ppermute | solution.py:364
  20.1 7.5 %collective-permute-start.3 = (bf16[320,384]{1,0:T(8,128)(2,1)S(1)}, bf16[320,384]{1,0:T(8,128)(2,1)S(1)}, u32[]{:S(2)}, u32[]{:S(2)}) collective-permute-start(bf16[320,384]{1,0:T(8,128)(2,1)S(1)} %constant_dynamic-update-slice_fusion), channel_id=1, source_target_pairs={{0,2},{1,9},{2,0},{3,11},{4,6},{5,13},{6,4},{7,15},{8,10},{9,1},{1... | collective-permute-start | bytes 737288 | tf_op jit(solution)/shard_map/ppermute | solution.py:364
  22.0 14.5 %collective-permute-start.8 = (bf16[160,512]{1,0:T(8,128)(2,1)S(1)}, bf16[160,512]{1,0:T(8,128)(2,1)}, u32[]{:S(2)}, u32[]{:S(2)}) collective-permute-start(bf16[160,512]{1,0:T(8,128)(2,1)S(1)} %get-tuple-element.97), channel_id=1, source_target_pairs={{0,16},{1,17},{2,18},{3,19},{4,20},{5,21},{6,22},{7,23},{8,24},{9,... | collective-permute-start | bytes 491528 | tf_op jit(solution)/shard_map/ppermute | solution.py:364
  22.0 22.0 %collective-permute-start.11 = (bf16[160,256]{1,0:T(8,128)(2,1)S(1)}, bf16[160,256]{1,0:T(8,128)(2,1)}, u32[]{:S(2)}, u32[]{:S(2)}) collective-permute-start(bf16[160,256]{1,0:T(8,128)(2,1)S(1)} %get-tuple-element.105), channel_id=1, source_target_pairs={{0,16},{1,17},{2,18},{3,19},{4,20},{5,21},{6,22},{7,23},{8,24},{9,... | collective-permute-start | bytes 245768 | tf_op jit(solution)/shard_map/ppermute | solution.py:364
  27.2 10.9 %collective-permute-start.7 = (bf16[320,384]{1,0:T(8,128)(2,1)}, bf16[320,384]{1,0:T(8,128)(2,1)}, u32[]{:S(2)}, u32[]{:S(2)}) collective-permute-start(bf16[320,384]{1,0:T(8,128)(2,1)} %constant_dynamic-update-slice_fusion.2), channel_id=1, source_target_pairs={{0,8},{1,3},{2,10},{3,1},{4,12},{5,7},{6,14},{7,5},{8,0},{9,11},{1... | collective-permute-start | bytes 737288 | tf_op jit(solution)/shard_map/ppermute | solution.py:364
  29.0 12.6 %collective-permute-start.6 = (bf16[640,384]{1,0:T(8,128)(2,1)}, bf16[640,384]{1,0:T(8,128)(2,1)}, u32[]{:S(2)}, u32[]{:S(2)}) collective-permute-start(bf16[640,384]{1,0:T(8,128)(2,1)} %constant_dynamic-update-slice_fusion.4), channel_id=1, source_target_pairs={{0,4},{1,3},{2,6},{3,1},{4,0},{5,7},{6,2},{7,5},{8,12},{9,11},{10,... | collective-permute-start | bytes 1474568 | tf_op jit(solution)/shard_map/ppermute | solution.py:364
  31.5 12.3 %collective-permute-start.5 = (bf16[16,2560]{1,0:T(8,128)(2,1)S(1)}, bf16[16,2560]{1,0:T(8,128)(2,1)S(1)}, u32[]{:S(2)}, u32[]{:S(2)}) collective-permute-start(bf16[16,2560]{1,0:T(8,128)(2,1)S(1)} %bitcast_select_fusion.2), channel_id=1, source_target_pairs={{0,2},{1,3},{4,6},{5,7},{8,10},{9,11},{12,14},{13,15},{16,18},{17,... | collective-permute-start | bytes 245768 | tf_op jit(solution)/shard_map/ppermute | solution.py:554
  40.0 13.9 %collective-permute-start.9 = (bf16[640,384]{1,0:T(8,128)(2,1)S(1)}, bf16[640,384]{1,0:T(8,128)(2,1)S(1)}, u32[]{:S(2)}, u32[]{:S(2)}) collective-permute-start(bf16[640,384]{1,0:T(8,128)(2,1)S(1)} %constant_dynamic-update-slice_fusion.8), channel_id=1, source_target_pairs={{0,4},{1,9},{2,6},{3,11},{4,0},{5,13},{6,2},{7,15},{8,12},{9,1},{1... | collective-permute-start | bytes 1474568 | tf_op jit(solution)/shard_map/ppermute | solution.py:364
  45.0 12.5 %collective-permute-start.13 = (bf16[640,512]{1,0:T(8,128)(2,1)S(1)}, bf16[640,512]{1,0:T(8,128)(2,1)S(1)}, u32[]{:S(2)}, u32[]{:S(2)}) collective-permute-start(bf16[640,512]{1,0:T(8,128)(2,1)S(1)} %constant_dynamic-update-slice_fusion.14), channel_id=1, source_target_pairs={{0,2},{1,5},{2,0},{3,7},{4,6},{5,1},{6,4},{7,3},{8,10},{9,13},{10,... | collective-permute-start | bytes 1966088 | tf_op jit(solution)/shard_map/ppermute | solution.py:364
  45.1 15.3 %collective-permute-start.15 = (bf16[1280,384]{1,0:T(8,128)(2,1)S(1)}, bf16[1280,384]{1,0:T(8,128)(2,1)S(1)}, u32[]{:S(2)}, u32[]{:S(2)}) collective-permute-start(bf16[1280,384]{1,0:T(8,128)(2,1)S(1)} %constant_dynamic-update-slice_fusion.10.low), channel_id=1, source_target_pairs={{0,8},{1,5},{2,10},{3,7},{4,12},{5,1},{6,14},{7,3},{8,0},{9,13},{1... | collective-permute-start | bytes 2949128 | tf_op jit(solution)/shard_map/ppermute | solution.py:364
  46.7 10.8 %collective-permute-start.14 = (bf16[320,256]{1,0:T(8,128)(2,1)S(1)}, bf16[320,256]{1,0:T(8,128)(2,1)S(1)}, u32[]{:S(2)}, u32[]{:S(2)}) collective-permute-start(bf16[320,256]{1,0:T(8,128)(2,1)S(1)} %constant_dynamic-update-slice_fusion.12), channel_id=1, source_target_pairs={{0,4},{1,9},{2,6},{3,11},{4,0},{5,13},{6,2},{7,15},{8,12},{9,1},{1... | collective-permute-start | bytes 491528 | tf_op jit(solution)/shard_map/ppermute | solution.py:364
  54.1 22.2 %collective-permute-start.12 = (bf16[1280,384]{1,0:T(8,128)(2,1)S(1)}, bf16[1280,384]{1,0:T(8,128)(2,1)S(1)}, u32[]{:S(2)}, u32[]{:S(2)}) collective-permute-start(bf16[1280,384]{1,0:T(8,128)(2,1)S(1)} %constant_dynamic-update-slice_fusion.16.low), channel_id=1, source_target_pairs={{0,2},{1,5},{2,0},{3,7},{4,6},{5,1},{6,4},{7,3},{8,10},{9,13},{10,... | collective-permute-start | bytes 2949128 | tf_op jit(solution)/shard_map/ppermute | solution.py:364
  57.6 25.3 %collective-permute-start.18 = (bf16[1280,512]{1,0:T(8,128)(2,1)S(1)}, bf16[1280,512]{1,0:T(8,128)(2,1)S(1)}, u32[]{:S(2)}, u32[]{:S(2)}) collective-permute-start(bf16[1280,512]{1,0:T(8,128)(2,1)S(1)} %constant_dynamic-update-slice_fusion.20.low), channel_id=1, source_target_pairs={{0,8},{1,3},{2,10},{3,1},{4,12},{5,7},{6,14},{7,5},{8,0},{9,11},{1... | collective-permute-start | bytes 3932168 | tf_op jit(solution)/shard_map/ppermute | solution.py:364
  65.8 10.5 %collective-permute-start.16 = (bf16[1024,128]{1,0:T(8,128)(2,1)S(1)}, bf16[1024,128]{1,0:T(8,128)(2,1)S(1)}, u32[]{:S(2)}, u32[]{:S(2)}) collective-permute-start(bf16[1024,128]{1,0:T(8,128)(2,1)S(1)} %get-tuple-element.118.mine_ref), channel_id=1, source_target_pairs={{0,1},{1,0},{2,3},{3,2},{4,5},{5,4},{6,7},{7,6},{8,9},{9,8},{10,11... | collective-permute-start | bytes 786440 | tf_op jit(solution)/shard_map/ppermute | solution.py:364
  74.8 8.0 %collective-permute-start.17 = (bf16[640,256]{1,0:T(8,128)(2,1)S(1)}, bf16[640,256]{1,0:T(8,128)(2,1)S(1)}, u32[]{:S(2)}, u32[]{:S(2)}) collective-permute-start(bf16[640,256]{1,0:T(8,128)(2,1)S(1)} %constant_dynamic-update-slice_fusion.18), channel_id=1, source_target_pairs={{0,8},{1,3},{2,10},{3,1},{4,12},{5,7},{6,14},{7,5},{8,0},{9,11},{1... | collective-permute-start | bytes 983048 | tf_op jit(solution)/shard_map/ppermute | solution.py:364
  82.8 10.7 %collective-permute-start.20 = (bf16[1280,256]{1,0:T(8,128)(2,1)S(1)}, bf16[1280,256]{1,0:T(8,128)(2,1)S(1)}, u32[]{:S(2)}, u32[]{:S(2)}) collective-permute-start(bf16[1280,256]{1,0:T(8,128)(2,1)S(1)} %constant_dynamic-update-slice_fusion.22.low), channel_id=1, source_target_pairs={{0,2},{1,5},{2,0},{3,7},{4,6},{5,1},{6,4},{7,3},{8,10},{9,13},{10,... | collective-permute-start | bytes 1966088 | tf_op jit(solution)/shard_map/ppermute | solution.py:364
  89.8 8.4 %collective-permute-start.19 = (bf16[144,1024]{1,0:T(8,128)(2,1)S(1)}, bf16[144,1024]{1,0:T(8,128)(2,1)S(1)}, u32[]{:S(2)}, u32[]{:S(2)}) collective-permute-start(bf16[144,1024]{1,0:T(8,128)(2,1)S(1)} %constant_dynamic-update-slice_fusion.24), channel_id=1, source_target_pairs={{0,2},{1,3},{2,0},{3,1},{4,6},{5,7},{6,4},{7,5},{8,10},{9,11},{10,... | collective-permute-start | bytes 884744 | tf_op jit(solution)/shard_map/ppermute | solution.py:364
  101.3 23.7 %collective-permute-start.23 = (f32[512,1024]{1,0:T(8,128)}, f32[512,1024]{1,0:T(8,128)}, u32[]{:S(2)}, u32[]{:S(2)}) collective-permute-start(f32[512,1024]{1,0:T(8,128)} %get-tuple-element.150), channel_id=1, source_target_pairs={{0,1},{1,0},{2,3},{3,2},{4,5},{5,4},{6,7},{7,6},{8,9},{9,8},{10,11... | collective-permute-start | bytes 6291464 | tf_op jit(solution)/shard_map/ppermute | solution.py:364
  109.3 15.7 %collective-permute-start.24 = (f32[512,256]{1,0:T(8,128)}, f32[512,256]{1,0:T(8,128)S(1)}, u32[]{:S(2)}, u32[]{:S(2)}) collective-permute-start(f32[512,256]{1,0:T(8,128)} %get-tuple-element.151), channel_id=1, source_target_pairs={{0,1},{1,0},{2,3},{3,2},{4,5},{5,4},{6,7},{7,6},{8,9},{9,8},{10,11... | collective-permute-start | bytes 1572872 | tf_op jit(solution)/shard_map/ppermute | solution.py:364
  109.3 9.9 %collective-permute-start.21 = (bf16[512,128]{1,0:T(8,128)(2,1)S(1)}, bf16[512,128]{1,0:T(8,128)(2,1)S(1)}, u32[]{:S(2)}, u32[]{:S(2)}) collective-permute-start(bf16[512,128]{1,0:T(8,128)(2,1)S(1)} %get-tuple-element.145), channel_id=1, source_target_pairs={{0,16},{1,17},{2,18},{3,19},{4,20},{5,21},{6,22},{7,23},{8,24},{9,... | collective-permute-start | bytes 393224 | tf_op jit(solution)/shard_map/ppermute | solution.py:364
  119.9 10.3 %collective-permute-start.25 = (bf16[2,512,128]{2,1,0:T(8,128)(2,1)}, bf16[2,512,128]{2,1,0:T(8,128)(2,1)}, u32[]{:S(2)}, u32[]{:S(2)}) collective-permute-start(bf16[2,512,128]{2,1,0:T(8,128)(2,1)} %pad_maximum_fusion.2), channel_id=1, source_target_pairs={{0,8},{1,9},{2,10},{3,11},{4,12},{5,13},{6,14},{7,15},{8,0},{9,1},... | collective-permute-start | bytes 786440 | tf_op jit(solution)/shard_map/ppermute | solution.py:364
  119.9 9.2 %collective-permute-start.26 = (bf16[128,128]{1,0:T(8,128)(2,1)S(1)}, bf16[128,128]{1,0:T(8,128)(2,1)S(1)}, u32[]{:S(2)}, u32[]{:S(2)}) collective-permute-start(bf16[128,128]{1,0:T(8,128)(2,1)S(1)} %get-tuple-element.152), channel_id=1, source_target_pairs={{0,16},{1,17},{2,18},{3,19},{4,20},{5,21},{6,22},{7,23},{8,24},{9,... | collective-permute-start | bytes 98312 | tf_op jit(solution)/shard_map/ppermute | solution.py:364
  (16 other events, 271.0 us)

commit v5 on v4

--- a/solution.py
+++ b/solution.py
@@ -19,14 +19,15 @@
 FLIPS = {"a": 16, "b": 8, "y": 4, "x": 2}
 ROUTES = (("axyb", "abxy"), ("abyx", "axby"), ("ayxb", "abyx"), ("aybx", "abxy"))
 PAIRS = ((0,), (1, 2, 3), (4, 5, 6, 7), (8, 9))
-CUT = 3
+CUT = 2
 SCHEDULE = (
     "0.0", "1.0", "tokens", "0.1", "2.0", "1.1", "0.2", "halo", "settings", "3.0",
     "2.1", "1.2", "0.3", "own", "3.1", "2.2", "1.3", "3.2", "2.3", "K0",
-    "K1", "3.3", "K2", "xA", "K3", "xB", "JA", "fA0", "JB", "fB0",
-    "fA1", "norm", "fB1", "fA2", "fB2", "fA3", "fB3",
+    "K1", "xA", "3.3", "K2", "JA", "fA0", "K3", "xB", "fA1", "JB",
+    "fB0", "fA2", "fB1", "norm", "fA3", "fB2", "fB3",
 )
 VMEM = pl.BlockSpec(memory_space=pltpu.VMEM)
+LIGHT = pl.CostEstimate(flops=1000, bytes_accessed=1000, transcendentals=0)
 SMEM = pl.BlockSpec(memory_space=pltpu.SMEM)
 
 
@@ -143,10 +144,14 @@
 
 def scan_kernel(
     chunk, held, heads, extra, ints, own, other, low, high, taps, x_ref, mine_ref, their_ref, table_ref,
-    kt_ref, tot_ref, skip_ref, y_out, s_out, send_out, whole, padded, carry,
+    kt_ref, tot_ref, skip_ref, *refs,
 ):
+    y_out, s_out, send_out, whole, padded, carry = refs[-6:]
     project(chunk, ints, own, other, low, high, whole, padded, None)
-    pairs = len(heads)
+    base = 0
+    for earlier in refs[:-6]:
+        base = earlier.shape[1] // LANES
+        send_out[:, 0 : base * LANES] = earlier[...]
     half = GROUP // 2
     row = lax.broadcasted_iota(jnp.int32, (half, half), 0)
     col = lax.broadcasted_iota(jnp.int32, (half, half), 1)
@@ -203,7 +208,7 @@
             local = jnp.concatenate(ends, axis=1) * carry[...] + local
         carry[...] = local
     s_out[...] = carry[...]
-    send_out[0:LANES, :] = carry[...].astype(BF16)
+    send_out[0:LANES, base * LANES :] = carry[...].astype(BF16)
     side = lax.broadcasted_iota(jnp.int32, (8, LANES), 1) < LANES // 2
     for i, head in enumerate(heads):
         total = jnp.where(side, column(tot_ref[...], head), column(tot_ref[...], head + 1))
@@ -213,7 +218,7 @@
         parts = jnp.where(place == 0, one.astype(F32), two.astype(F32))
         parts = jnp.where(place >= 2, three.astype(F32), parts)
         parts = jnp.where(place >= 3, 0.0, parts)
-        send_out[LANES:, lanes(i)] = jnp.concatenate([parts, jnp.zeros_like(parts)], axis=0).astype(
+        send_out[LANES:, lanes(base + i)] = jnp.concatenate([parts, jnp.zeros_like(parts)], axis=0).astype(
             BF16
         )
 
@@ -359,6 +364,28 @@
     skip_out[...] = exact(own, jnp.where(row == mine, 1.0, 0.0))
 
 
+def chosen(req, row, here, one, two):
+    rel = jnp.bitwise_xor(row, req)
+    far, near = (rel // 4) % 2 == 1, (rel // 2) % 2 == 1
+    return jnp.where(
+        near, jnp.where(far, two[1], two[0]), jnp.where(far, one[...], here[...])
+    )
+
+
+def pick_kernel(place, ints, here, one, two, out):
+    out[...] = chosen(place[4], ints[7], here, one, two)
+
+
+def last_kernel(place, ints, here, one, two, three, *refs):
+    odd = jnp.bitwise_xor(ints[6], place[4]) % 2 == 1
+    best = chosen(place[4], ints[6], here, one, two)
+    out, base = refs[-1], 0
+    for earlier in refs[:-1]:
+        base = earlier.shape[0]
+        out[0:base, :] = earlier[...]
+    out[base:, :] = jnp.where(odd, three[...], best).astype(F32)
+
+
 def swapped(x, masks):
     count = lax.axis_size("req") * lax.axis_size("seq")
     return lax.ppermute(x, AXES, [(i, i ^ masks[i % 2]) for i in range(count)])
@@ -398,6 +425,7 @@
         out_specs=[VMEM] * 2,
         out_shape=[jax.ShapeDtypeStruct((portion, total), BF16)] * 2,
         compiler_params=params(8),
+        cost_estimate=LIGHT,
         name="sort",
     )(place, mix_weight, step_weight)
     got = swapped(given, (1, 1))
@@ -407,6 +435,7 @@
         out_specs=[VMEM] * len(widths),
         out_shape=[jax.ShapeDtypeStruct((2 * portion, width), BF16) for width in widths],
         compiler_params=params(8),
+        cost_estimate=LIGHT,
         name="stack",
     )(place, kept, got)
     blocks = list(blocks)
@@ -438,13 +467,11 @@
                 jax.ShapeDtypeStruct((8, LANES), F32),
             ],
             compiler_params=params(28),
-            cost_estimate=pl.CostEstimate(
-                flops=2 * chip_rows * depth * width, bytes_accessed=9000000, transcendentals=500000
-            ),
+            cost_estimate=LIGHT,
             name="first",
         )(ints, own, other, low, high, taps, rates)
 
-    def scanned(index, ints, own, other, low, high, taps, skip, x0, mine, theirs, table, kt, tot):
+    def scanned(index, ints, own, other, low, high, taps, skip, x0, mine, theirs, table, kt, tot, *earlier):
         more = extra if index == 1 else 0
         held = (PAIRS[0] if more else ()) + PAIRS[index]
         pairs = len(held)
@@ -453,24 +480,22 @@
         width = widths[index]
         return pl.pallas_call(
             functools.partial(scan_kernel, index, held, firsts, more),
-            in_specs=[SMEM] + [VMEM] * 12,
+            in_specs=[SMEM] + [VMEM] * (12 + len(earlier)),
             out_specs=[VMEM] * 3,
             scratch_shapes=scratch(width, new) + [pltpu.VMEM((LANES, pairs * LANES), F32)],
             out_shape=[
                 jax.ShapeDtypeStruct((chip_rows, pairs * LANES), F32),
                 jax.ShapeDtypeStruct((LANES, pairs * LANES), F32),
-                jax.ShapeDtypeStruct((LANES + 16, pairs * LANES), BF16),
+                jax.ShapeDtypeStruct(
+                    (LANES + 16, pairs * LANES + sum(a.shape[1] for a in earlier)), BF16
+                ),
             ],
             compiler_params=params(28),
-            cost_estimate=pl.CostEstimate(
-                flops=2 * chip_rows * depth * width + pairs * 600000000,
-                bytes_accessed=12000000,
-                transcendentals=pairs * 400000,
-            ),
+            cost_estimate=LIGHT,
             name="scan",
         )(
             ints, own, other, low, high, taps,
-            x0, mine, theirs, table, kt, tot, skip,
+            x0, mine, theirs, table, kt, tot, skip, *earlier,
         )
 
     def joined(held, ints, mine, theirs, table, tot, ys, ss, r):
@@ -487,11 +512,7 @@
                 jax.ShapeDtypeStruct((len(halves) * LANES, nstate), BF16),
             ],
             compiler_params=params(28),
-            cost_estimate=pl.CostEstimate(
-                flops=4 * chip_rows * LANES * pairs * LANES,
-                bytes_accessed=chip_rows * pairs * LANES * 8,
-                transcendentals=chip_rows * pairs * LANES,
-            ),
+            cost_estimate=LIGHT,
             name="join",
         )(ints, mine, theirs, table, tot, r, *ys, *ss)
 
@@ -517,21 +538,20 @@
             ),
             out_shape=jax.ShapeDtypeStruct((span, inner), BF16),
             compiler_params=params(28),
-            cost_estimate=pl.CostEstimate(
-                flops=6 * span * inner, bytes_accessed=6 * span * inner, transcendentals=span
-            ),
+            cost_estimate=LIGHT,
             name="norm",
         )(ints, norm_gain[None], keep_a, keep_b, got_a, got_b)
 
-    def pick(row, cand):
-        rel = row ^ req_index
-        far, near = (rel >> 2) & 1, (rel >> 1) & 1
-        here, one, two = cand
-        return jnp.where(
-            near == 1,
-            jnp.where(far == 1, two[1], two[0]),
-            jnp.where(far == 1, one, here),
-        )
+    def picked(kernel, kind, *arrays, more=0):
+        return pl.pallas_call(
+            kernel,
+            in_specs=[SMEM] * 2 + [VMEM] * len(arrays),
+            out_specs=VMEM,
+            out_shape=jax.ShapeDtypeStruct((arrays[0].shape[0] + more, nstate), kind),
+            compiler_params=params(8),
+            cost_estimate=LIGHT,
+            name="pick",
+        )(place, v["ints"], *arrays)
 
     v = state
     last = len(PAIRS) - 1
@@ -579,6 +599,7 @@
                     jax.ShapeDtypeStruct((8, half), F32),
                 ],
                 compiler_params=params(8),
+                cost_estimate=LIGHT,
                 name="settings",
             )(after(place), deal, prompt_len, prompt_start, small)
             v["token"] = v["rates"]
@@ -599,18 +620,11 @@
             ints = after(v["ints"])
             v["y", i], v["s", i], v["t", i] = scanned(
                 i, ints, v["own"], v["other"], blocks[i], arrived[i], v["taps"], v["skip"],
-                x0, bc, theirs, table, kt, tot,
+                x0, bc, theirs, table, kt, tot, *([v["t", i - 1]] if i > 1 and i != CUT else []),
             )
             v["token"] = v["t", i]
         elif event in ("xA", "xB"):
-            which = range(1, CUT) if event == "xA" else range(CUT, last + 1)
-            sent = [v["t", i] for i in which]
-            if len(sent) > 1:
-                sent = jnp.concatenate(after(*sent), axis=1)
-                v["token"] = sent
-            else:
-                sent = sent[0]
-            v["r", event[1]] = swapped(sent, (2, 2))
+            v["r", event[1]] = swapped(v["t", CUT - 1 if event == "xA" else last], (2, 2))
         elif event in ("JA", "JB"):
             which = range(1, CUT) if event == "JA" else range(CUT, last + 1)
             held = early_pairs if event == "JA" else late_pairs
@@ -631,22 +645,22 @@
             elif event[2] == "2":
                 cand = (v["fin", key], v["one", key], after(v["two", key]))
                 v["cand", key] = cand
-                v["picked", key] = pick(v["ints"][7], cand)
+                v["picked", key] = picked(pick_kernel, BF16, *cand)
                 v["token"] = v["picked", key]
                 v["three", key] = swapped(v["picked", key], (4, 4))
             else:
                 three = after(v["three", key])
-                odd = (v["ints"][6] ^ req_index) & 1
-                v["final", key] = jnp.where(odd == 1, three, pick(v["ints"][6], v["cand", key])).astype(
-                    F32
+                earlier = [v["final", "A"]] if key == "B" else []
+                more = sum(a.shape[0] for a in earlier)
+                v["final", key] = picked(
+                    last_kernel, F32, *v["cand", key], three, *earlier, more=more
                 )
                 v["token"] = v["final", key]
         else:
             ints = after(v["ints"])
             result = normed(ints, v["keep", "A"], v["keep", "B"], v["got", "A"], v["got", "B"])
             v["token"] = result
-    final_state = jnp.concatenate([v["final", "A"], v["final", "B"]], axis=0)
-    return (result[None], final_state.reshape(1, share, head_dim, nstate))
+    return (result[None], v["final", "B"].reshape(1, share, head_dim, nstate))
 
 
 def passed_along(block, axis, distance):

time: 139 us -> 133 us (0.957)
  starting transfers between devices: 45.4 us -> 40.5 us
  waiting for transfers between devices: 37.9 us -> 42.7 us
  local copies, waits for them, and re-layouts: 13.6 us -> 11.6 us
  other arithmetic: 4.59 us -> 2.63 us
    ppermute x29, starting transfers between devices: 42.9 us -> 36.5 us  [swapped(): return lax.ppermute(x, AXES, [(i, i ^ masks[i % 2]) for i in range(count)])]
    ppermute x29, waiting for transfers between devices: 37.9 us -> 42.7 us  [swapped(): return lax.ppermute(x, AXES, [(i, i ^ masks[i % 2]) for i in range(count)])]
    pallas_call x0 -> x4, Pallas kernels: none -> 3.11 us  [picked(): pl.pallas_call(kernel, in_specs=[SMEM] * 2 + [VMEM] * len(arrays), out_sp...]
    pallas_call x2, Pallas kernels: 4.81 us -> 2.98 us  [joined(): pl.pallas_call(functools.partial(join_kernel, [first_head(p, share) for p...]
    unnamed x34 -> x33, local copies, waits for them, and re-layouts: 5.48 us -> 3.87 us
    ppermute x1, starting transfers between devices: 2.51 us -> 4.01 us  [on_device(): v['halo'] = lax.ppermute(edge, AXES, route)]
  transfers between devices with their start and end apart: 30 -> 30, of which waited for: 11 -> 12; matrix products, arithmetic and copies ran while one was open for 12% -> 10% of each run, Pallas kernels for 23% -> 20%
where the time goes in v5:
time: 133 us
  waiting for transfers between devices  42.7 us (32%)
  starting transfers between devices  40.5 us (30%)
  Pallas kernels  34.3 us (26%)
  local copies, waits for them, and re-layouts  11.6 us (9%)
  other arithmetic  2.63 us (2%)
    ppermute x29, waiting for transfers between devices, swapped(): return lax.ppermute(x, AXES, [(i, i ^ masks[i % 2]) for i in range(count)])  42.7 us
    ppermute x29, starting transfers between devices, swapped(): return lax.ppermute(x, AXES, [(i, i ^ masks[i % 2]) for i in range(count)])  36.5 us
    pallas_call x3, Pallas kernels, scanned(): pl.pallas_call(functools.partial(scan_kernel, index, held, firsts, more),...  17.2 us
    concatenate x12, local copies, waits for them, and re-layouts, on_device(): blocks[i] = jnp.concatenate(after(blocks[i], arrived[i]), axis=0)  6.71 us
    pallas_call x1, Pallas kernels, projected(): pl.pallas_call(first_kernel, in_specs=[SMEM] + [VMEM] * 6, out_specs=[VME...  5.39 us
    ppermute x1, starting transfers between devices, on_device(): v['halo'] = lax.ppermute(edge, AXES, route)  4.01 us
    unnamed x33, local copies, waits for them, and re-layouts  3.87 us
    pallas_call x4, Pallas kernels, picked(): pl.pallas_call(kernel, in_specs=[SMEM] * 2 + [VMEM] * len(arrays), out_sp...  3.11 us
  transfers between devices with their start and end apart: 30, of which 12 were waited for; matrix products, arithmetic and copies ran while one was open for 10% of the time, Pallas kernels for 20%

profile of v5, /device:TPU:0, one launch (start us, length us, event | category | flops | bytes accessed | tf_op | source)
XLA Modules:
  0.0 132.9 jit_solution(17371517994492837473)
XLA Ops:
  4.0 2.1 %collective-permute-done.1.got = bf16[80,1536]{1,0:T(8,128)(2,1)S(1)} collective-permute-done((bf16[80,1536]{1,0:T(8,128)(2,1)S(1)}, bf16[80,1536]{1,0:T(8,128)(2,1)S(1)}, u32[]{:S(2)}, u32[]{:S(2)}) %collective-permute-start.1) | collective-permute-done | bytes 245792 | tf_op jit(solution)/shard_map/ppermute | solution.py:391
  6.7 4.0 %collective-permute-start.2 = (bf16[160,384]{1,0:T(8,128)(2,1)S(1)}, bf16[160,384]{1,0:T(8,128)(2,1)S(1)}, u32[]{:S(2)}, u32[]{:S(2)}) collective-permute-start(bf16[160,384]{1,0:T(8,128)(2,1)S(1)} %get-tuple-element.80), channel_id=1, source_target_pairs={{0,16},{1,17},{2,18},{3,19},{4,20},{5,21},{6,22},{7,23},{8,24},{9,... | collective-permute-start | bytes 368648 | tf_op jit(solution)/shard_map/ppermute | solution.py:391
  10.8 9.3 %collective-permute-done.2 = bf16[160,384]{1,0:T(8,128)(2,1)S(1)} collective-permute-done((bf16[160,384]{1,0:T(8,128)(2,1)S(1)}, bf16[160,384]{1,0:T(8,128)(2,1)S(1)}, u32[]{:S(2)}, u32[]{:S(2)}) %collective-permute-start.2) | collective-permute-done | bytes 122912 | tf_op jit(solution)/shard_map/ppermute | solution.py:391
  20.1 1.9 %collective-permute-start.3 = (bf16[320,384]{1,0:T(8,128)(2,1)S(1)}, bf16[320,384]{1,0:T(8,128)(2,1)}, u32[]{:S(2)}, u32[]{:S(2)}) collective-permute-start(bf16[320,384]{1,0:T(8,128)(2,1)S(1)} %constant_dynamic-update-slice_fusion), channel_id=1, source_target_pairs={{0,2},{1,9},{2,0},{3,11},{4,6},{5,13},{6,4},{7,15},{8,10},{9,1},{1... | collective-permute-start | bytes 737288 | tf_op jit(solution)/shard_map/ppermute | solution.py:391
  22.0 2.9 %collective-permute-start.11 = (bf16[160,256]{1,0:T(8,128)(2,1)S(1)}, bf16[160,256]{1,0:T(8,128)(2,1)}, u32[]{:S(2)}, u32[]{:S(2)}) collective-permute-start(bf16[160,256]{1,0:T(8,128)(2,1)S(1)} %get-tuple-element.103), channel_id=1, source_target_pairs={{0,16},{1,17},{2,18},{3,19},{4,20},{5,21},{6,22},{7,23},{8,24},{9,... | collective-permute-start | bytes 245768 | tf_op jit(solution)/shard_map/ppermute | solution.py:391
  27.2 1.7 %constant_dynamic-update-slice_fusion.4 = bf16[640,384]{1,0:T(8,128)(2,1)} fusion(bf16[640,384]{1,0:T(8,128)(2,1)} %constant_dynamic-update-slice_fusion.5, bf16[320,384]{1,0:T(8,128)(2,1)} %collective-permute-done.3), kind=kLoop, calls=%fused_computation.8 | loop fusion | bytes 491520 | tf_op jit(solution)/shard_map/concatenate | solution.py:562
  28.9 1.9 %collective-permute-start.6 = (bf16[640,384]{1,0:T(8,128)(2,1)}, bf16[640,384]{1,0:T(8,128)(2,1)}, u32[]{:S(2)}, u32[]{:S(2)}) collective-permute-start(bf16[640,384]{1,0:T(8,128)(2,1)} %constant_dynamic-update-slice_fusion.4), channel_id=1, source_target_pairs={{0,4},{1,3},{2,6},{3,1},{4,0},{5,7},{6,2},{7,5},{8,12},{9,11},{10,... | collective-permute-start | bytes 1474568 | tf_op jit(solution)/shard_map/ppermute | solution.py:391
  32.3 4.0 %collective-permute-start.5 = (bf16[16,2560]{1,0:T(8,128)(2,1)}, bf16[16,2560]{1,0:T(8,128)(2,1)}, u32[]{:S(2)}, u32[]{:S(2)}) collective-permute-start(bf16[16,2560]{1,0:T(8,128)(2,1)} %bitcast_select_fusion), channel_id=1, source_target_pairs={{0,2},{1,3},{4,6},{5,7},{8,10},{9,11},{12,14},{13,15},{16,18},{17,... | collective-permute-start | bytes 245768 | tf_op jit(solution)/shard_map/ppermute | solution.py:574
  47.9 8.4 %collective-permute-done.9 = bf16[640,384]{1,0:T(8,128)(2,1)S(1)} collective-permute-done((bf16[640,384]{1,0:T(8,128)(2,1)S(1)}, bf16[640,384]{1,0:T(8,128)(2,1)S(1)}, u32[]{:S(2)}, u32[]{:S(2)}) %collective-permute-start.9) | collective-permute-done | bytes 491552 | tf_op jit(solution)/shard_map/ppermute | solution.py:391
  56.5 3.3 %collective-permute-done.14 = bf16[320,256]{1,0:T(8,128)(2,1)S(1)} collective-permute-done((bf16[320,256]{1,0:T(8,128)(2,1)S(1)}, bf16[320,256]{1,0:T(8,128)(2,1)S(1)}, u32[]{:S(2)}, u32[]{:S(2)}) %collective-permute-start.14) | collective-permute-done | bytes 163872 | tf_op jit(solution)/shard_map/ppermute | solution.py:391
  60.1 1.9 %collective-permute-start.18 = (bf16[640,256]{1,0:T(8,128)(2,1)S(1)}, bf16[640,256]{1,0:T(8,128)(2,1)S(1)}, u32[]{:S(2)}, u32[]{:S(2)}) collective-permute-start(bf16[640,256]{1,0:T(8,128)(2,1)S(1)} %constant_dynamic-update-slice_fusion.18), channel_id=1, source_target_pairs={{0,8},{1,3},{2,10},{3,1},{4,12},{5,7},{6,14},{7,5},{8,0},{9,11},{1... | collective-permute-start | bytes 983048 | tf_op jit(solution)/shard_map/ppermute | solution.py:391
  62.1 5.4 %first.1 = (bf16[1024,128]{1,0:T(8,128)(2,1)S(1)}, bf16[1024,128]{1,0:T(8,128)(2,1)S(1)}, f32[1024,128]{1,0:T(8,128)S(1)}, f32[4,32,256]{2,1,0:T(8,128)S(1)}, f32[8,128]{1,0:T(8,128)S(1)}) custom-call(s32[8]{0:T(128)S(1)} %get-tuple-element.146.ints, bf16[528,2560]{1,0:T(8,128)(2,1)S(1)} %pad_maximum_fusion.own, ...), custom_call_target="tpu_custom_call" | custom-call | flops 1000 | bytes 1000 | tf_op jit(solution)/shard_map/first/pallas_call | solution.py:457
  67.5 9.5 %collective-permute-start.16 = (bf16[1024,128]{1,0:T(8,128)(2,1)S(1)}, bf16[1024,128]{1,0:T(8,128)(2,1)S(1)}, u32[]{:S(2)}, u32[]{:S(2)}) collective-permute-start(bf16[1024,128]{1,0:T(8,128)(2,1)S(1)} %get-tuple-element.116.mine_ref), channel_id=1, source_target_pairs={{0,1},{1,0},{2,3},{3,2},{4,5},{5,4},{6,7},{7,6},{8,9},{9,8},{10,11... | collective-permute-start | bytes 786440 | tf_op jit(solution)/shard_map/ppermute | solution.py:391
  78.2 6.4 %scan.3 = (f32[1024,512]{1,0:T(8,128)S(1)}, f32[128,512]{1,0:T(8,128)S(1)}, bf16[144,512]{1,0:T(8,128)(2,1)S(1)}) custom-call(s32[8]{0:T(128)S(1)} %get-tuple-element.146.ints, bf16[528,2560]{1,0:T(8,128)(2,1)S(1)} %pad_maximum_fusion.own, bf16[512,2560]{1,0:T(8,128)(2,1)S(1)} %collective-permute-done.other, ...), custom_call_target="tpu_custom_call" | custom-call | flops 1000 | bytes 1000 | tf_op jit(solution)/shard_map/scan/pallas_call | solution.py:481
  84.7 2.0 %collective-permute-start.17 = (bf16[144,512]{1,0:T(8,128)(2,1)S(1)}, bf16[144,512]{1,0:T(8,128)(2,1)S(1)}, u32[]{:S(2)}, u32[]{:S(2)}) collective-permute-start(bf16[144,512]{1,0:T(8,128)(2,1)S(1)} %get-tuple-element.122), channel_id=1, source_target_pairs={{0,2},{1,3},{2,0},{3,1},{4,6},{5,7},{6,4},{7,5},{8,10},{9,11},{10,... | collective-permute-start | bytes 442376 | tf_op jit(solution)/shard_map/ppermute | solution.py:391
  86.7 6.9 %scan.4 = (f32[1024,512]{1,0:T(8,128)S(1)}, f32[128,512]{1,0:T(8,128)S(1)}, bf16[144,512]{1,0:T(8,128)(2,1)S(1)}) custom-call(s32[8]{0:T(128)S(1)} %get-tuple-element.146.ints, bf16[528,2560]{1,0:T(8,128)(2,1)S(1)} %pad_maximum_fusion.own, bf16[512,2560]{1,0:T(8,128)(2,1)S(1)} %collective-permute-done.other, ...), custom_call_target="tpu_custom_call" | custom-call | flops 1000 | bytes 1000 | tf_op jit(solution)/shard_map/scan/pallas_call | solution.py:481
  93.6 4.8 %collective-permute-done.17.r_ref = bf16[144,512]{1,0:T(8,128)(2,1)S(1)} collective-permute-done((bf16[144,512]{1,0:T(8,128)(2,1)S(1)}, bf16[144,512]{1,0:T(8,128)(2,1)S(1)}, u32[]{:S(2)}, u32[]{:S(2)}) %collective-permute-start.17) | collective-permute-done | bytes 147488 | tf_op jit(solution)/shard_map/ppermute | solution.py:391
  99.8 3.9 %scan.5 = (f32[1024,256]{1,0:T(8,128)S(1)}, f32[128,256]{1,0:T(8,128)S(1)}, bf16[144,768]{1,0:T(8,128)(2,1)S(1)}) custom-call(s32[8]{0:T(128)S(1)} %get-tuple-element.146.ints, bf16[528,2560]{1,0:T(8,128)(2,1)S(1)} %pad_maximum_fusion.own, bf16[512,2560]{1,0:T(8,128)(2,1)S(1)} %collective-permute-done.other, ...), custom_call_target="tpu_custom_call" | custom-call | flops 1000 | bytes 1000 | tf_op jit(solution)/shard_map/scan/pallas_call | solution.py:481
  105.3 4.3 %collective-permute-done.22.one = bf16[256,128]{1,0:T(8,128)(2,1)S(1)} collective-permute-done((bf16[256,128]{1,0:T(8,128)(2,1)S(1)}, bf16[256,128]{1,0:T(8,128)(2,1)S(1)}, u32[]{:S(2)}, u32[]{:S(2)}) %collective-permute-start.22) | collective-permute-done | bytes 65568 | tf_op jit(solution)/shard_map/ppermute | solution.py:391
  109.7 1.6 %join.3 = (f32[512,768]{1,0:T(8,128)S(1)}, f32[512,768]{1,0:T(8,128)S(1)}, bf16[384,128]{1,0:T(8,128)(2,1)S(1)}) custom-call(s32[8]{0:T(128)S(1)} %get-tuple-element.146.ints, bf16[1024,128]{1,0:T(8,128)(2,1)S(1)} %get-tuple-element.116.mine_ref, bf16[1024,128]{1,0:T(8,128)(2,1)S(1)} %collective-permute-done.16.their_ref, ...), custom_call_target="tpu_custom_call" | custom-call | flops 1000 | bytes 1000 | tf_op jit(solution)/shard_map/join/pallas_call | solution.py:505
  112.1 3.2 %collective-permute-start.23 = (bf16[384,128]{1,0:T(8,128)(2,1)S(1)}, bf16[384,128]{1,0:T(8,128)(2,1)S(1)}, u32[]{:S(2)}, u32[]{:S(2)}) collective-permute-start(bf16[384,128]{1,0:T(8,128)(2,1)S(1)} %get-tuple-element.144.here), channel_id=1, source_target_pairs={{0,16},{1,17},{2,18},{3,19},{4,20},{5,21},{6,22},{7,23},{8,24},{9,... | collective-permute-start | bytes 294920 | tf_op jit(solution)/shard_map/ppermute | solution.py:391
  115.3 4.2 %collective-permute-done.24.two = bf16[2,256,128]{2,1,0:T(8,128)(2,1)S(1)} collective-permute-done((bf16[2,256,128]{2,1,0:T(8,128)(2,1)S(1)}, bf16[2,256,128]{2,1,0:T(8,128)(2,1)S(1)}, u32[]{:S(2)}, u32[]{:S(2)}) %collective-permute-start.24) | collective-permute-done | bytes 131104 | tf_op jit(solution)/shard_map/ppermute | solution.py:391
  121.7 2.9 %norm.1 = bf16[512,2560]{1,0:T(8,128)(2,1)} custom-call(s32[8]{0:T(128)S(1)} %get-tuple-element.146.ints, f32[1,2560]{1,0:T(1,128)S(1)} %broadcast_in_dim.30.gain_ref, f32[512,512]{1,0:T(8,128)S(1)} %get-tuple-element.147.ka_ref, f32[512,768]{1,0:T(8,128)S(1)} %get-tuple-element.148.kb_ref, f32[512,512]{1,0:T(8,128)S(1)} %collective-permute-done.25.ra_ref, ...), custom_call_target="tpu_custom_call" | custom-call | flops 1000 | bytes 1000 | tf_op jit(solution)/shard_map/norm/pallas_call | solution.py:527
  127.5 4.0 %collective-permute-done.29.three = bf16[384,128]{1,0:T(8,128)(2,1)S(1)} collective-permute-done((bf16[384,128]{1,0:T(8,128)(2,1)S(1)}, bf16[384,128]{1,0:T(8,128)(2,1)S(1)}, u32[]{:S(2)}, u32[]{:S(2)}) %collective-permute-start.29) | collective-permute-done | bytes 98336 | tf_op jit(solution)/shard_map/ppermute | solution.py:391
  (112 shorter events, 31.1 us)
Async XLA Ops:
  0.7 30.1 %collective-permute-start = (bf16[512,2560]{1,0:T(8,128)(2,1)}, bf16[512,2560]{1,0:T(8,128)(2,1)S(1)}, u32[]{:S(2)}, u32[]{:S(2)}) collective-permute-start(bf16[512,2560]{1,0:T(8,128)(2,1)} %bitcast.18), channel_id=1, source_target_pairs={{0,1},{1,0},{2,3},{3,2},{4,5},{5,4},{6,7},{7,6},{8,9},{9,8},{10,11... | collective-permute-start | bytes 7864328 | tf_op jit(solution)/shard_map/ppermute | solution.py:391
  6.7 13.4 %collective-permute-start.2 = (bf16[160,384]{1,0:T(8,128)(2,1)S(1)}, bf16[160,384]{1,0:T(8,128)(2,1)S(1)}, u32[]{:S(2)}, u32[]{:S(2)}) collective-permute-start(bf16[160,384]{1,0:T(8,128)(2,1)S(1)} %get-tuple-element.80), channel_id=1, source_target_pairs={{0,16},{1,17},{2,18},{3,19},{4,20},{5,21},{6,22},{7,23},{8,24},{9,... | collective-permute-start | bytes 368648 | tf_op jit(solution)/shard_map/ppermute | solution.py:391
  10.7 14.2 %collective-permute-start.4 = (bf16[160,384]{1,0:T(8,128)(2,1)S(1)}, bf16[160,384]{1,0:T(8,128)(2,1)}, u32[]{:S(2)}, u32[]{:S(2)}) collective-permute-start(bf16[160,384]{1,0:T(8,128)(2,1)S(1)} %get-tuple-element.82), channel_id=1, source_target_pairs={{0,16},{1,17},{2,18},{3,19},{4,20},{5,21},{6,22},{7,23},{8,24},{9,... | collective-permute-start | bytes 368648 | tf_op jit(solution)/shard_map/ppermute | solution.py:391
  20.1 6.4 %collective-permute-start.3 = (bf16[320,384]{1,0:T(8,128)(2,1)S(1)}, bf16[320,384]{1,0:T(8,128)(2,1)}, u32[]{:S(2)}, u32[]{:S(2)}) collective-permute-start(bf16[320,384]{1,0:T(8,128)(2,1)S(1)} %constant_dynamic-update-slice_fusion), channel_id=1, source_target_pairs={{0,2},{1,9},{2,0},{3,11},{4,6},{5,13},{6,4},{7,15},{8,10},{9,1},{1... | collective-permute-start | bytes 737288 | tf_op jit(solution)/shard_map/ppermute | solution.py:391
  22.0 16.7 %collective-permute-start.8 = (bf16[160,512]{1,0:T(8,128)(2,1)S(1)}, bf16[160,512]{1,0:T(8,128)(2,1)}, u32[]{:S(2)}, u32[]{:S(2)}) collective-permute-start(bf16[160,512]{1,0:T(8,128)(2,1)S(1)} %get-tuple-element.95), channel_id=1, source_target_pairs={{0,16},{1,17},{2,18},{3,19},{4,20},{5,21},{6,22},{7,23},{8,24},{9,... | collective-permute-start | bytes 491528 | tf_op jit(solution)/shard_map/ppermute | solution.py:391
  22.0 24.1 %collective-permute-start.11 = (bf16[160,256]{1,0:T(8,128)(2,1)S(1)}, bf16[160,256]{1,0:T(8,128)(2,1)}, u32[]{:S(2)}, u32[]{:S(2)}) collective-permute-start(bf16[160,256]{1,0:T(8,128)(2,1)S(1)} %get-tuple-element.103), channel_id=1, source_target_pairs={{0,16},{1,17},{2,18},{3,19},{4,20},{5,21},{6,22},{7,23},{8,24},{9,... | collective-permute-start | bytes 245768 | tf_op jit(solution)/shard_map/ppermute | solution.py:391
  25.9 14.4 %collective-permute-start.7 = (bf16[320,384]{1,0:T(8,128)(2,1)S(1)}, bf16[320,384]{1,0:T(8,128)(2,1)}, u32[]{:S(2)}, u32[]{:S(2)}) collective-permute-start(bf16[320,384]{1,0:T(8,128)(2,1)S(1)} %constant_dynamic-update-slice_fusion.2), channel_id=1, source_target_pairs={{0,8},{1,3},{2,10},{3,1},{4,12},{5,7},{6,14},{7,5},{8,0},{9,11},{1... | collective-permute-start | bytes 737288 | tf_op jit(solution)/shard_map/ppermute | solution.py:391
  28.9 14.0 %collective-permute-start.6 = (bf16[640,384]{1,0:T(8,128)(2,1)}, bf16[640,384]{1,0:T(8,128)(2,1)}, u32[]{:S(2)}, u32[]{:S(2)}) collective-permute-start(bf16[640,384]{1,0:T(8,128)(2,1)} %constant_dynamic-update-slice_fusion.4), channel_id=1, source_target_pairs={{0,4},{1,3},{2,6},{3,1},{4,0},{5,7},{6,2},{7,5},{8,12},{9,11},{10,... | collective-permute-start | bytes 1474568 | tf_op jit(solution)/shard_map/ppermute | solution.py:391
  32.3 12.8 %collective-permute-start.5 = (bf16[16,2560]{1,0:T(8,128)(2,1)}, bf16[16,2560]{1,0:T(8,128)(2,1)}, u32[]{:S(2)}, u32[]{:S(2)}) collective-permute-start(bf16[16,2560]{1,0:T(8,128)(2,1)} %bitcast_select_fusion), channel_id=1, source_target_pairs={{0,2},{1,3},{4,6},{5,7},{8,10},{9,11},{12,14},{13,15},{16,18},{17,... | collective-permute-start | bytes 245768 | tf_op jit(solution)/shard_map/ppermute | solution.py:574
  39.7 7.4 %collective-permute-start.10 = (bf16[320,512]{1,0:T(8,128)(2,1)S(1)}, bf16[320,512]{1,0:T(8,128)(2,1)S(1)}, u32[]{:S(2)}, u32[]{:S(2)}) collective-permute-start(bf16[320,512]{1,0:T(8,128)(2,1)S(1)} %constant_dynamic-update-slice_fusion.6), channel_id=1, source_target_pairs={{0,4},{1,9},{2,6},{3,11},{4,0},{5,13},{6,2},{7,15},{8,12},{9,1},{1... | collective-permute-start | bytes 983048 | tf_op jit(solution)/shard_map/ppermute | solution.py:391
  41.3 15.0 %collective-permute-start.9 = (bf16[640,384]{1,0:T(8,128)(2,1)S(1)}, bf16[640,384]{1,0:T(8,128)(2,1)S(1)}, u32[]{:S(2)}, u32[]{:S(2)}) collective-permute-start(bf16[640,384]{1,0:T(8,128)(2,1)S(1)} %constant_dynamic-update-slice_fusion.8), channel_id=1, source_target_pairs={{0,4},{1,9},{2,6},{3,11},{4,0},{5,13},{6,2},{7,15},{8,12},{9,1},{1... | collective-permute-start | bytes 1474568 | tf_op jit(solution)/shard_map/ppermute | solution.py:391
  47.2 12.7 %collective-permute-start.13 = (bf16[640,512]{1,0:T(8,128)(2,1)S(1)}, bf16[640,512]{1,0:T(8,128)(2,1)S(1)}, u32[]{:S(2)}, u32[]{:S(2)}) collective-permute-start(bf16[640,512]{1,0:T(8,128)(2,1)S(1)} %constant_dynamic-update-slice_fusion.14), channel_id=1, source_target_pairs={{0,2},{1,5},{2,0},{3,7},{4,6},{5,1},{6,4},{7,3},{8,10},{9,13},{10,... | collective-permute-start | bytes 1966088 | tf_op jit(solution)/shard_map/ppermute | solution.py:391
  47.2 14.8 %collective-permute-start.15 = (bf16[1280,384]{1,0:T(8,128)(2,1)S(1)}, bf16[1280,384]{1,0:T(8,128)(2,1)S(1)}, u32[]{:S(2)}, u32[]{:S(2)}) collective-permute-start(bf16[1280,384]{1,0:T(8,128)(2,1)S(1)} %constant_dynamic-update-slice_fusion.10.low), channel_id=1, source_target_pairs={{0,8},{1,5},{2,10},{3,7},{4,12},{5,1},{6,14},{7,3},{8,0},{9,13},{1... | collective-permute-start | bytes 2949128 | tf_op jit(solution)/shard_map/ppermute | solution.py:391
  47.5 12.3 %collective-permute-start.14 = (bf16[320,256]{1,0:T(8,128)(2,1)S(1)}, bf16[320,256]{1,0:T(8,128)(2,1)S(1)}, u32[]{:S(2)}, u32[]{:S(2)}) collective-permute-start(bf16[320,256]{1,0:T(8,128)(2,1)S(1)} %constant_dynamic-update-slice_fusion.12), channel_id=1, source_target_pairs={{0,4},{1,9},{2,6},{3,11},{4,0},{5,13},{6,2},{7,15},{8,12},{9,1},{1... | collective-permute-start | bytes 491528 | tf_op jit(solution)/shard_map/ppermute | solution.py:391
  56.5 21.7 %collective-permute-start.12 = (bf16[1280,384]{1,0:T(8,128)(2,1)S(1)}, bf16[1280,384]{1,0:T(8,128)(2,1)S(1)}, u32[]{:S(2)}, u32[]{:S(2)}) collective-permute-start(bf16[1280,384]{1,0:T(8,128)(2,1)S(1)} %constant_dynamic-update-slice_fusion.16.low), channel_id=1, source_target_pairs={{0,2},{1,5},{2,0},{3,7},{4,6},{5,1},{6,4},{7,3},{8,10},{9,13},{10,... | collective-permute-start | bytes 2949128 | tf_op jit(solution)/shard_map/ppermute | solution.py:391
  60.0 26.7 %collective-permute-start.19 = (bf16[1280,512]{1,0:T(8,128)(2,1)S(1)}, bf16[1280,512]{1,0:T(8,128)(2,1)S(1)}, u32[]{:S(2)}, u32[]{:S(2)}) collective-permute-start(bf16[1280,512]{1,0:T(8,128)(2,1)S(1)} %constant_dynamic-update-slice_fusion.20.low), channel_id=1, source_target_pairs={{0,8},{1,3},{2,10},{3,1},{4,12},{5,7},{6,14},{7,5},{8,0},{9,11},{1... | collective-permute-start | bytes 3932168 | tf_op jit(solution)/shard_map/ppermute | solution.py:391
  60.1 24.4 %collective-permute-start.18 = (bf16[640,256]{1,0:T(8,128)(2,1)S(1)}, bf16[640,256]{1,0:T(8,128)(2,1)S(1)}, u32[]{:S(2)}, u32[]{:S(2)}) collective-permute-start(bf16[640,256]{1,0:T(8,128)(2,1)S(1)} %constant_dynamic-update-slice_fusion.18), channel_id=1, source_target_pairs={{0,8},{1,3},{2,10},{3,1},{4,12},{5,7},{6,14},{7,5},{8,0},{9,11},{1... | collective-permute-start | bytes 983048 | tf_op jit(solution)/shard_map/ppermute | solution.py:391
  67.5 10.7 %collective-permute-start.16 = (bf16[1024,128]{1,0:T(8,128)(2,1)S(1)}, bf16[1024,128]{1,0:T(8,128)(2,1)S(1)}, u32[]{:S(2)}, u32[]{:S(2)}) collective-permute-start(bf16[1024,128]{1,0:T(8,128)(2,1)S(1)} %get-tuple-element.116.mine_ref), channel_id=1, source_target_pairs={{0,1},{1,0},{2,3},{3,2},{4,5},{5,4},{6,7},{7,6},{8,9},{9,8},{10,11... | collective-permute-start | bytes 786440 | tf_op jit(solution)/shard_map/ppermute | solution.py:391
  84.6 15.2 %collective-permute-start.20 = (bf16[1280,256]{1,0:T(8,128)(2,1)S(1)}, bf16[1280,256]{1,0:T(8,128)(2,1)S(1)}, u32[]{:S(2)}, u32[]{:S(2)}) collective-permute-start(bf16[1280,256]{1,0:T(8,128)(2,1)S(1)} %constant_dynamic-update-slice_fusion.22.low), channel_id=1, source_target_pairs={{0,2},{1,5},{2,0},{3,7},{4,6},{5,1},{6,4},{7,3},{8,10},{9,13},{10,... | collective-permute-start | bytes 1966088 | tf_op jit(solution)/shard_map/ppermute | solution.py:391
  84.7 13.7 %collective-permute-start.17 = (bf16[144,512]{1,0:T(8,128)(2,1)S(1)}, bf16[144,512]{1,0:T(8,128)(2,1)S(1)}, u32[]{:S(2)}, u32[]{:S(2)}) collective-permute-start(bf16[144,512]{1,0:T(8,128)(2,1)S(1)} %get-tuple-element.122), channel_id=1, source_target_pairs={{0,2},{1,3},{2,0},{3,1},{4,6},{5,7},{6,4},{7,5},{8,10},{9,11},{10,... | collective-permute-start | bytes 442376 | tf_op jit(solution)/shard_map/ppermute | solution.py:391
  111.3 10.4 %collective-permute-start.26 = (f32[512,768]{1,0:T(8,128)S(1)}, f32[512,768]{1,0:T(8,128)S(1)}, u32[]{:S(2)}, u32[]{:S(2)}) collective-permute-start(f32[512,768]{1,0:T(8,128)S(1)} %get-tuple-element.150), channel_id=1, source_target_pairs={{0,1},{1,0},{2,3},{3,2},{4,5},{5,4},{6,7},{7,6},{8,9},{9,8},{10,11... | collective-permute-start | bytes 4718600 | tf_op jit(solution)/shard_map/ppermute | solution.py:391
  111.4 10.3 %collective-permute-start.25 = (f32[512,512]{1,0:T(8,128)S(1)}, f32[512,512]{1,0:T(8,128)S(1)}, u32[]{:S(2)}, u32[]{:S(2)}) collective-permute-start(f32[512,512]{1,0:T(8,128)S(1)} %get-tuple-element.149), channel_id=1, source_target_pairs={{0,1},{1,0},{2,3},{3,2},{4,5},{5,4},{6,7},{7,6},{8,9},{9,8},{10,11... | collective-permute-start | bytes 3145736 | tf_op jit(solution)/shard_map/ppermute | solution.py:391
  111.9 7.6 %collective-permute-start.24 = (bf16[2,256,128]{2,1,0:T(8,128)(2,1)S(1)}, bf16[2,256,128]{2,1,0:T(8,128)(2,1)S(1)}, u32[]{:S(2)}, u32[]{:S(2)}) collective-permute-start(bf16[2,256,128]{2,1,0:T(8,128)(2,1)S(1)} %pad_maximum_fusion.2), channel_id=1, source_target_pairs={{0,8},{1,9},{2,10},{3,11},{4,12},{5,13},{6,14},{7,15},{8,0},{9,1},... | collective-permute-start | bytes 393224 | tf_op jit(solution)/shard_map/ppermute | solution.py:391
  112.1 8.0 %collective-permute-start.23 = (bf16[384,128]{1,0:T(8,128)(2,1)S(1)}, bf16[384,128]{1,0:T(8,128)(2,1)S(1)}, u32[]{:S(2)}, u32[]{:S(2)}) collective-permute-start(bf16[384,128]{1,0:T(8,128)(2,1)S(1)} %get-tuple-element.144.here), channel_id=1, source_target_pairs={{0,16},{1,17},{2,18},{3,19},{4,20},{5,21},{6,22},{7,23},{8,24},{9,... | collective-permute-start | bytes 294920 | tf_op jit(solution)/shard_map/ppermute | solution.py:391
  (16 other events, 303.4 us)

commit v6 on v5

--- a/solution.py
+++ b/solution.py
@@ -17,7 +17,7 @@
 BF16 = jnp.bfloat16
 AXES = ("req", "seq")
 FLIPS = {"a": 16, "b": 8, "y": 4, "x": 2}
-ROUTES = (("axyb", "abxy"), ("abyx", "axby"), ("ayxb", "abyx"), ("aybx", "abxy"))
+ROUTES = (("axyb", "abxy"), ("abyx", "axby"), ("ayxb", "abyx"), ("axyb", "abxy"))
 PAIRS = ((0,), (1, 2, 3), (4, 5, 6, 7), (8, 9))
 CUT = 2
 SCHEDULE = (
@@ -564,7 +564,8 @@
             route = ROUTES[i]
             arrived[i] = swapped(blocks[i], (FLIPS[route[0][step]], FLIPS[route[1][step]]))
         elif event == "tokens":
-            v["other"] = swapped(rows, (1, 1))
+            given_rows, _ = lax.optimization_barrier((rows, blocks[0]))
+            v["other"] = swapped(given_rows, (1, 1))
         elif event == "halo":
             other = after(v["other"])
             edge = jnp.where(core == 1, rows[span - HALO :], other[span - HALO :])

time: 133 us -> 132 us (level)
  waiting for transfers between devices: 42.7 us -> 38.9 us
  starting transfers between devices: 40.5 us -> 43.4 us
    ppermute x29, waiting for transfers between devices: 42.7 us -> 38.9 us  [swapped(): return lax.ppermute(x, AXES, [(i, i ^ masks[i % 2]) for i in range(count)])]
    ppermute x29, starting transfers between devices: 36.5 us -> 39.3 us  [swapped(): return lax.ppermute(x, AXES, [(i, i ^ masks[i % 2]) for i in range(count)])]
  transfers between devices with their start and end apart: 30 -> 30, of which waited for: 12 -> 13; matrix products, arithmetic and copies ran while one was open for 10% -> 9% of each run, Pallas kernels for 20% -> 19%
where the time goes in v6:
time: 132 us
  starting transfers between devices  43.4 us (33%)
  waiting for transfers between devices  38.9 us (29%)
  Pallas kernels  33.9 us (26%)
  local copies, waits for them, and re-layouts  11.6 us (9%)
  other arithmetic  2.64 us (2%)
    ppermute x29, starting transfers between devices, swapped(): return lax.ppermute(x, AXES, [(i, i ^ masks[i % 2]) for i in range(count)])  39.3 us
    ppermute x29, waiting for transfers between devices, swapped(): return lax.ppermute(x, AXES, [(i, i ^ masks[i % 2]) for i in range(count)])  38.9 us
    pallas_call x3, Pallas kernels, scanned(): pl.pallas_call(functools.partial(scan_kernel, index, held, firsts, more),...  16.7 us
    concatenate x12, local copies, waits for them, and re-layouts, on_device(): blocks[i] = jnp.concatenate(after(blocks[i], arrived[i]), axis=0)  6.71 us
    pallas_call x1, Pallas kernels, projected(): pl.pallas_call(first_kernel, in_specs=[SMEM] + [VMEM] * 6, out_specs=[VME...  5.37 us
    ppermute x1, starting transfers between devices, on_device(): v['halo'] = lax.ppermute(edge, AXES, route)  4.01 us
    unnamed x33, local copies, waits for them, and re-layouts  3.9 us
    pallas_call x2, Pallas kernels, joined(): pl.pallas_call(functools.partial(join_kernel, [first_head(p, share) for p...  3.13 us
  transfers between devices with their start and end apart: 30, of which 13 were waited for; matrix products, arithmetic and copies ran while one was open for 9% of the time, Pallas kernels for 19%

profile of v6, /device:TPU:0, one launch (start us, length us, event | category | flops | bytes accessed | tf_op | source)
XLA Modules:
  0.0 131.5 jit_solution(13004281137495576369)
XLA Ops:
  6.1 3.8 %collective-permute-start.2 = (bf16[160,384]{1,0:T(8,128)(2,1)S(1)}, bf16[160,384]{1,0:T(8,128)(2,1)S(1)}, u32[]{:S(2)}, u32[]{:S(2)}) collective-permute-start(bf16[160,384]{1,0:T(8,128)(2,1)S(1)} %get-tuple-element.81), channel_id=1, source_target_pairs={{0,16},{1,17},{2,18},{3,19},{4,20},{5,21},{6,22},{7,23},{8,24},{9,... | collective-permute-start | bytes 368648 | tf_op jit(solution)/shard_map/ppermute | solution.py:391
  9.9 9.4 %collective-permute-done.2 = bf16[160,384]{1,0:T(8,128)(2,1)S(1)} collective-permute-done((bf16[160,384]{1,0:T(8,128)(2,1)S(1)}, bf16[160,384]{1,0:T(8,128)(2,1)S(1)}, u32[]{:S(2)}, u32[]{:S(2)}) %collective-permute-start.2) | collective-permute-done | bytes 122912 | tf_op jit(solution)/shard_map/ppermute | solution.py:391
  19.3 1.9 %collective-permute-start.3 = (bf16[320,384]{1,0:T(8,128)(2,1)S(1)}, bf16[320,384]{1,0:T(8,128)(2,1)}, u32[]{:S(2)}, u32[]{:S(2)}) collective-permute-start(bf16[320,384]{1,0:T(8,128)(2,1)S(1)} %constant_dynamic-update-slice_fusion), channel_id=1, source_target_pairs={{0,2},{1,9},{2,0},{3,11},{4,6},{5,13},{6,4},{7,15},{8,10},{9,1},{1... | collective-permute-start | bytes 737288 | tf_op jit(solution)/shard_map/ppermute | solution.py:391
  21.1 2.9 %collective-permute-start.11 = (bf16[160,256]{1,0:T(8,128)(2,1)S(1)}, bf16[160,256]{1,0:T(8,128)(2,1)}, u32[]{:S(2)}, u32[]{:S(2)}) collective-permute-start(bf16[160,256]{1,0:T(8,128)(2,1)S(1)} %get-tuple-element.105), channel_id=1, source_target_pairs={{0,16},{1,17},{2,18},{3,19},{4,20},{5,21},{6,22},{7,23},{8,24},{9,... | collective-permute-start | bytes 245768 | tf_op jit(solution)/shard_map/ppermute | solution.py:391
  26.4 1.7 %constant_dynamic-update-slice_fusion.4 = bf16[640,384]{1,0:T(8,128)(2,1)} fusion(bf16[640,384]{1,0:T(8,128)(2,1)} %constant_dynamic-update-slice_fusion.5, bf16[320,384]{1,0:T(8,128)(2,1)} %collective-permute-done.3), kind=kLoop, calls=%fused_computation.8 | loop fusion | bytes 491520 | tf_op jit(solution)/shard_map/concatenate | solution.py:562
  28.1 1.7 %collective-permute-start.6 = (bf16[640,384]{1,0:T(8,128)(2,1)}, bf16[640,384]{1,0:T(8,128)(2,1)}, u32[]{:S(2)}, u32[]{:S(2)}) collective-permute-start(bf16[640,384]{1,0:T(8,128)(2,1)} %constant_dynamic-update-slice_fusion.4), channel_id=1, source_target_pairs={{0,4},{1,3},{2,6},{3,1},{4,0},{5,7},{6,2},{7,5},{8,12},{9,11},{10,... | collective-permute-start | bytes 1474568 | tf_op jit(solution)/shard_map/ppermute | solution.py:391
  31.4 4.0 %collective-permute-start.5 = (bf16[16,2560]{1,0:T(8,128)(2,1)}, bf16[16,2560]{1,0:T(8,128)(2,1)}, u32[]{:S(2)}, u32[]{:S(2)}) collective-permute-start(bf16[16,2560]{1,0:T(8,128)(2,1)} %bitcast_select_fusion), channel_id=1, source_target_pairs={{0,2},{1,3},{4,6},{5,7},{8,10},{9,11},{12,14},{13,15},{16,18},{17,... | collective-permute-start | bytes 245768 | tf_op jit(solution)/shard_map/ppermute | solution.py:575
  46.6 1.9 %collective-permute-start.14 = (bf16[320,256]{1,0:T(8,128)(2,1)S(1)}, bf16[320,256]{1,0:T(8,128)(2,1)S(1)}, u32[]{:S(2)}, u32[]{:S(2)}) collective-permute-start(bf16[320,256]{1,0:T(8,128)(2,1)S(1)} %constant_dynamic-update-slice_fusion.12), channel_id=1, source_target_pairs={{0,2},{1,9},{2,0},{3,11},{4,6},{5,13},{6,4},{7,15},{8,10},{9,1},{1... | collective-permute-start | bytes 491528 | tf_op jit(solution)/shard_map/ppermute | solution.py:391
  48.5 6.2 %collective-permute-done.9 = bf16[640,384]{1,0:T(8,128)(2,1)S(1)} collective-permute-done((bf16[640,384]{1,0:T(8,128)(2,1)S(1)}, bf16[640,384]{1,0:T(8,128)(2,1)S(1)}, u32[]{:S(2)}, u32[]{:S(2)}) %collective-permute-start.9) | collective-permute-done | bytes 491552 | tf_op jit(solution)/shard_map/ppermute | solution.py:391
  55.0 3.6 %collective-permute-done.14 = bf16[320,256]{1,0:T(8,128)(2,1)S(1)} collective-permute-done((bf16[320,256]{1,0:T(8,128)(2,1)S(1)}, bf16[320,256]{1,0:T(8,128)(2,1)S(1)}, u32[]{:S(2)}, u32[]{:S(2)}) %collective-permute-start.14) | collective-permute-done | bytes 163872 | tf_op jit(solution)/shard_map/ppermute | solution.py:391
  59.5 2.2 %collective-permute-done.15.high = bf16[1280,384]{1,0:T(8,128)(2,1)S(1)} collective-permute-done((bf16[1280,384]{1,0:T(8,128)(2,1)S(1)}, bf16[1280,384]{1,0:T(8,128)(2,1)S(1)}, u32[]{:S(2)}, u32[]{:S(2)}) %collective-permute-start.15) | collective-permute-done | bytes 983072 | tf_op jit(solution)/shard_map/ppermute | solution.py:391
  61.7 5.4 %first.1 = (bf16[1024,128]{1,0:T(8,128)(2,1)S(1)}, bf16[1024,128]{1,0:T(8,128)(2,1)S(1)}, f32[1024,128]{1,0:T(8,128)S(1)}, f32[4,32,256]{2,1,0:T(8,128)S(1)}, f32[8,128]{1,0:T(8,128)S(1)}) custom-call(s32[8]{0:T(128)S(1)} %get-tuple-element.148.ints, bf16[528,2560]{1,0:T(8,128)(2,1)S(1)} %pad_maximum_fusion.own, ...), custom_call_target="tpu_custom_call" | custom-call | flops 1000 | bytes 1000 | tf_op jit(solution)/shard_map/first/pallas_call | solution.py:457
  67.1 10.7 %collective-permute-start.16 = (bf16[1024,128]{1,0:T(8,128)(2,1)S(1)}, bf16[1024,128]{1,0:T(8,128)(2,1)S(1)}, u32[]{:S(2)}, u32[]{:S(2)}) collective-permute-start(bf16[1024,128]{1,0:T(8,128)(2,1)S(1)} %get-tuple-element.118.mine_ref), channel_id=1, source_target_pairs={{0,1},{1,0},{2,3},{3,2},{4,5},{5,4},{6,7},{7,6},{8,9},{9,8},{10,11... | collective-permute-start | bytes 786440 | tf_op jit(solution)/shard_map/ppermute | solution.py:391
  79.0 6.2 %scan.3 = (f32[1024,512]{1,0:T(8,128)S(1)}, f32[128,512]{1,0:T(8,128)S(1)}, bf16[144,512]{1,0:T(8,128)(2,1)S(1)}) custom-call(s32[8]{0:T(128)S(1)} %get-tuple-element.148.ints, bf16[528,2560]{1,0:T(8,128)(2,1)S(1)} %pad_maximum_fusion.own, bf16[512,2560]{1,0:T(8,128)(2,1)S(1)} %collective-permute-done.1.other, ...), custom_call_target="tpu_custom_call" | custom-call | flops 1000 | bytes 1000 | tf_op jit(solution)/shard_map/scan/pallas_call | solution.py:481
  85.5 6.6 %scan.4 = (f32[1024,512]{1,0:T(8,128)S(1)}, f32[128,512]{1,0:T(8,128)S(1)}, bf16[144,512]{1,0:T(8,128)(2,1)S(1)}) custom-call(s32[8]{0:T(128)S(1)} %get-tuple-element.148.ints, bf16[528,2560]{1,0:T(8,128)(2,1)S(1)} %pad_maximum_fusion.own, bf16[512,2560]{1,0:T(8,128)(2,1)S(1)} %collective-permute-done.1.other, ...), custom_call_target="tpu_custom_call" | custom-call | flops 1000 | bytes 1000 | tf_op jit(solution)/shard_map/scan/pallas_call | solution.py:481
  93.6 2.3 %collective-permute-done.20.high = bf16[1280,256]{1,0:T(8,128)(2,1)S(1)} collective-permute-done((bf16[1280,256]{1,0:T(8,128)(2,1)S(1)}, bf16[1280,256]{1,0:T(8,128)(2,1)S(1)}, u32[]{:S(2)}, u32[]{:S(2)}) %collective-permute-start.20) | collective-permute-done | bytes 655392 | tf_op jit(solution)/shard_map/ppermute | solution.py:391
  95.9 3.8 %scan.5 = (f32[1024,256]{1,0:T(8,128)S(1)}, f32[128,256]{1,0:T(8,128)S(1)}, bf16[144,768]{1,0:T(8,128)(2,1)S(1)}) custom-call(s32[8]{0:T(128)S(1)} %get-tuple-element.148.ints, bf16[528,2560]{1,0:T(8,128)(2,1)S(1)} %pad_maximum_fusion.own, bf16[512,2560]{1,0:T(8,128)(2,1)S(1)} %collective-permute-done.1.other, ...), custom_call_target="tpu_custom_call" | custom-call | flops 1000 | bytes 1000 | tf_op jit(solution)/shard_map/scan/pallas_call | solution.py:481
  99.8 3.1 %collective-permute-start.22 = (bf16[256,128]{1,0:T(8,128)(2,1)S(1)}, bf16[256,128]{1,0:T(8,128)(2,1)S(1)}, u32[]{:S(2)}, u32[]{:S(2)}) collective-permute-start(bf16[256,128]{1,0:T(8,128)(2,1)S(1)} %get-tuple-element.136.here), channel_id=1, source_target_pairs={{0,16},{1,17},{2,18},{3,19},{4,20},{5,21},{6,22},{7,23},{8,24},{9,... | collective-permute-start | bytes 196616 | tf_op jit(solution)/shard_map/ppermute | solution.py:391
  102.9 2.2 %collective-permute-done.22.one = bf16[256,128]{1,0:T(8,128)(2,1)S(1)} collective-permute-done((bf16[256,128]{1,0:T(8,128)(2,1)S(1)}, bf16[256,128]{1,0:T(8,128)(2,1)S(1)}, u32[]{:S(2)}, u32[]{:S(2)}) %collective-permute-start.22) | collective-permute-done | bytes 65568 | tf_op jit(solution)/shard_map/ppermute | solution.py:391
  106.5 1.8 %join.3 = (f32[512,768]{1,0:T(8,128)S(1)}, f32[512,768]{1,0:T(8,128)S(1)}, bf16[384,128]{1,0:T(8,128)(2,1)S(1)}) custom-call(s32[8]{0:T(128)S(1)} %get-tuple-element.148.ints, bf16[1024,128]{1,0:T(8,128)(2,1)S(1)} %get-tuple-element.118.mine_ref, bf16[1024,128]{1,0:T(8,128)(2,1)S(1)} %collective-permute-done.16.their_ref, ...), custom_call_target="tpu_custom_call" | custom-call | flops 1000 | bytes 1000 | tf_op jit(solution)/shard_map/join/pallas_call | solution.py:505
  110.0 3.3 %collective-permute-start.23 = (bf16[384,128]{1,0:T(8,128)(2,1)S(1)}, bf16[384,128]{1,0:T(8,128)(2,1)S(1)}, u32[]{:S(2)}, u32[]{:S(2)}) collective-permute-start(bf16[384,128]{1,0:T(8,128)(2,1)S(1)} %get-tuple-element.146.here), channel_id=1, source_target_pairs={{0,16},{1,17},{2,18},{3,19},{4,20},{5,21},{6,22},{7,23},{8,24},{9,... | collective-permute-start | bytes 294920 | tf_op jit(solution)/shard_map/ppermute | solution.py:391
  113.4 4.4 %collective-permute-done.24.two = bf16[2,256,128]{2,1,0:T(8,128)(2,1)S(1)} collective-permute-done((bf16[2,256,128]{2,1,0:T(8,128)(2,1)S(1)}, bf16[2,256,128]{2,1,0:T(8,128)(2,1)S(1)}, u32[]{:S(2)}, u32[]{:S(2)}) %collective-permute-start.24) | collective-permute-done | bytes 131104 | tf_op jit(solution)/shard_map/ppermute | solution.py:391
  120.3 2.9 %norm.1 = bf16[512,2560]{1,0:T(8,128)(2,1)} custom-call(s32[8]{0:T(128)S(1)} %get-tuple-element.148.ints, f32[1,2560]{1,0:T(1,128)S(1)} %broadcast_in_dim.30.gain_ref, f32[512,512]{1,0:T(8,128)S(1)} %get-tuple-element.149.ka_ref, f32[512,768]{1,0:T(8,128)S(1)} %get-tuple-element.150.kb_ref, f32[512,512]{1,0:T(8,128)S(1)} %collective-permute-done.25.ra_ref, ...), custom_call_target="tpu_custom_call" | custom-call | flops 1000 | bytes 1000 | tf_op jit(solution)/shard_map/norm/pallas_call | solution.py:527
  126.6 3.6 %collective-permute-done.29.three = bf16[384,128]{1,0:T(8,128)(2,1)S(1)} collective-permute-done((bf16[384,128]{1,0:T(8,128)(2,1)S(1)}, bf16[384,128]{1,0:T(8,128)(2,1)S(1)}, u32[]{:S(2)}, u32[]{:S(2)}) %collective-permute-start.29) | collective-permute-done | bytes 98336 | tf_op jit(solution)/shard_map/ppermute | solution.py:391
  (112 shorter events, 34.7 us)
Async XLA Ops:
  5.7 24.2 %collective-permute-start.1 = (bf16[512,2560]{1,0:T(8,128)(2,1)}, bf16[512,2560]{1,0:T(8,128)(2,1)S(1)}, u32[]{:S(2)}, u32[]{:S(2)}) collective-permute-start(bf16[512,2560]{1,0:T(8,128)(2,1)} %bitcast.18), channel_id=1, source_target_pairs={{0,1},{1,0},{2,3},{3,2},{4,5},{5,4},{6,7},{7,6},{8,9},{9,8},{10,11... | collective-permute-start | bytes 7864328 | tf_op jit(solution)/shard_map/ppermute | solution.py:391
  6.1 13.2 %collective-permute-start.2 = (bf16[160,384]{1,0:T(8,128)(2,1)S(1)}, bf16[160,384]{1,0:T(8,128)(2,1)S(1)}, u32[]{:S(2)}, u32[]{:S(2)}) collective-permute-start(bf16[160,384]{1,0:T(8,128)(2,1)S(1)} %get-tuple-element.81), channel_id=1, source_target_pairs={{0,16},{1,17},{2,18},{3,19},{4,20},{5,21},{6,22},{7,23},{8,24},{9,... | collective-permute-start | bytes 368648 | tf_op jit(solution)/shard_map/ppermute | solution.py:391
  9.8 14.2 %collective-permute-start.4 = (bf16[160,384]{1,0:T(8,128)(2,1)S(1)}, bf16[160,384]{1,0:T(8,128)(2,1)}, u32[]{:S(2)}, u32[]{:S(2)}) collective-permute-start(bf16[160,384]{1,0:T(8,128)(2,1)S(1)} %get-tuple-element.84), channel_id=1, source_target_pairs={{0,16},{1,17},{2,18},{3,19},{4,20},{5,21},{6,22},{7,23},{8,24},{9,... | collective-permute-start | bytes 368648 | tf_op jit(solution)/shard_map/ppermute | solution.py:391
  21.1 16.7 %collective-permute-start.8 = (bf16[160,512]{1,0:T(8,128)(2,1)S(1)}, bf16[160,512]{1,0:T(8,128)(2,1)}, u32[]{:S(2)}, u32[]{:S(2)}) collective-permute-start(bf16[160,512]{1,0:T(8,128)(2,1)S(1)} %get-tuple-element.97), channel_id=1, source_target_pairs={{0,16},{1,17},{2,18},{3,19},{4,20},{5,21},{6,22},{7,23},{8,24},{9,... | collective-permute-start | bytes 491528 | tf_op jit(solution)/shard_map/ppermute | solution.py:391
  21.1 24.1 %collective-permute-start.11 = (bf16[160,256]{1,0:T(8,128)(2,1)S(1)}, bf16[160,256]{1,0:T(8,128)(2,1)}, u32[]{:S(2)}, u32[]{:S(2)}) collective-permute-start(bf16[160,256]{1,0:T(8,128)(2,1)S(1)} %get-tuple-element.105), channel_id=1, source_target_pairs={{0,16},{1,17},{2,18},{3,19},{4,20},{5,21},{6,22},{7,23},{8,24},{9,... | collective-permute-start | bytes 245768 | tf_op jit(solution)/shard_map/ppermute | solution.py:391
  25.0 14.4 %collective-permute-start.7 = (bf16[320,384]{1,0:T(8,128)(2,1)S(1)}, bf16[320,384]{1,0:T(8,128)(2,1)}, u32[]{:S(2)}, u32[]{:S(2)}) collective-permute-start(bf16[320,384]{1,0:T(8,128)(2,1)S(1)} %constant_dynamic-update-slice_fusion.2), channel_id=1, source_target_pairs={{0,8},{1,3},{2,10},{3,1},{4,12},{5,7},{6,14},{7,5},{8,0},{9,11},{1... | collective-permute-start | bytes 737288 | tf_op jit(solution)/shard_map/ppermute | solution.py:391
  28.1 13.9 %collective-permute-start.6 = (bf16[640,384]{1,0:T(8,128)(2,1)}, bf16[640,384]{1,0:T(8,128)(2,1)}, u32[]{:S(2)}, u32[]{:S(2)}) collective-permute-start(bf16[640,384]{1,0:T(8,128)(2,1)} %constant_dynamic-update-slice_fusion.4), channel_id=1, source_target_pairs={{0,4},{1,3},{2,6},{3,1},{4,0},{5,7},{6,2},{7,5},{8,12},{9,11},{10,... | collective-permute-start | bytes 1474568 | tf_op jit(solution)/shard_map/ppermute | solution.py:391
  31.4 12.8 %collective-permute-start.5 = (bf16[16,2560]{1,0:T(8,128)(2,1)}, bf16[16,2560]{1,0:T(8,128)(2,1)}, u32[]{:S(2)}, u32[]{:S(2)}) collective-permute-start(bf16[16,2560]{1,0:T(8,128)(2,1)} %bitcast_select_fusion), channel_id=1, source_target_pairs={{0,2},{1,3},{4,6},{5,7},{8,10},{9,11},{12,14},{13,15},{16,18},{17,... | collective-permute-start | bytes 245768 | tf_op jit(solution)/shard_map/ppermute | solution.py:575
  38.8 7.4 %collective-permute-start.10 = (bf16[320,512]{1,0:T(8,128)(2,1)S(1)}, bf16[320,512]{1,0:T(8,128)(2,1)S(1)}, u32[]{:S(2)}, u32[]{:S(2)}) collective-permute-start(bf16[320,512]{1,0:T(8,128)(2,1)S(1)} %constant_dynamic-update-slice_fusion.6), channel_id=1, source_target_pairs={{0,4},{1,9},{2,6},{3,11},{4,0},{5,13},{6,2},{7,15},{8,12},{9,1},{1... | collective-permute-start | bytes 983048 | tf_op jit(solution)/shard_map/ppermute | solution.py:391
  40.4 14.4 %collective-permute-start.9 = (bf16[640,384]{1,0:T(8,128)(2,1)S(1)}, bf16[640,384]{1,0:T(8,128)(2,1)S(1)}, u32[]{:S(2)}, u32[]{:S(2)}) collective-permute-start(bf16[640,384]{1,0:T(8,128)(2,1)S(1)} %constant_dynamic-update-slice_fusion.8), channel_id=1, source_target_pairs={{0,4},{1,9},{2,6},{3,11},{4,0},{5,13},{6,2},{7,15},{8,12},{9,1},{1... | collective-permute-start | bytes 1474568 | tf_op jit(solution)/shard_map/ppermute | solution.py:391
  46.2 12.4 %collective-permute-start.13 = (bf16[640,512]{1,0:T(8,128)(2,1)S(1)}, bf16[640,512]{1,0:T(8,128)(2,1)S(1)}, u32[]{:S(2)}, u32[]{:S(2)}) collective-permute-start(bf16[640,512]{1,0:T(8,128)(2,1)S(1)} %constant_dynamic-update-slice_fusion.14), channel_id=1, source_target_pairs={{0,2},{1,5},{2,0},{3,7},{4,6},{5,1},{6,4},{7,3},{8,10},{9,13},{10,... | collective-permute-start | bytes 1966088 | tf_op jit(solution)/shard_map/ppermute | solution.py:391
  46.3 15.4 %collective-permute-start.15 = (bf16[1280,384]{1,0:T(8,128)(2,1)S(1)}, bf16[1280,384]{1,0:T(8,128)(2,1)S(1)}, u32[]{:S(2)}, u32[]{:S(2)}) collective-permute-start(bf16[1280,384]{1,0:T(8,128)(2,1)S(1)} %constant_dynamic-update-slice_fusion.10.low), channel_id=1, source_target_pairs={{0,8},{1,5},{2,10},{3,7},{4,12},{5,1},{6,14},{7,3},{8,0},{9,13},{1... | collective-permute-start | bytes 2949128 | tf_op jit(solution)/shard_map/ppermute | solution.py:391
  46.6 12.1 %collective-permute-start.14 = (bf16[320,256]{1,0:T(8,128)(2,1)S(1)}, bf16[320,256]{1,0:T(8,128)(2,1)S(1)}, u32[]{:S(2)}, u32[]{:S(2)}) collective-permute-start(bf16[320,256]{1,0:T(8,128)(2,1)S(1)} %constant_dynamic-update-slice_fusion.12), channel_id=1, source_target_pairs={{0,2},{1,9},{2,0},{3,11},{4,6},{5,13},{6,4},{7,15},{8,10},{9,1},{1... | collective-permute-start | bytes 491528 | tf_op jit(solution)/shard_map/ppermute | solution.py:391
  54.9 24.1 %collective-permute-start.12 = (bf16[1280,384]{1,0:T(8,128)(2,1)S(1)}, bf16[1280,384]{1,0:T(8,128)(2,1)S(1)}, u32[]{:S(2)}, u32[]{:S(2)}) collective-permute-start(bf16[1280,384]{1,0:T(8,128)(2,1)S(1)} %constant_dynamic-update-slice_fusion.16.low), channel_id=1, source_target_pairs={{0,2},{1,5},{2,0},{3,7},{4,6},{5,1},{6,4},{7,3},{8,10},{9,13},{10,... | collective-permute-start | bytes 2949128 | tf_op jit(solution)/shard_map/ppermute | solution.py:391
  58.8 26.7 %collective-permute-start.19 = (bf16[1280,512]{1,0:T(8,128)(2,1)S(1)}, bf16[1280,512]{1,0:T(8,128)(2,1)S(1)}, u32[]{:S(2)}, u32[]{:S(2)}) collective-permute-start(bf16[1280,512]{1,0:T(8,128)(2,1)S(1)} %constant_dynamic-update-slice_fusion.20.low), channel_id=1, source_target_pairs={{0,8},{1,3},{2,10},{3,1},{4,12},{5,7},{6,14},{7,5},{8,0},{9,11},{1... | collective-permute-start | bytes 3932168 | tf_op jit(solution)/shard_map/ppermute | solution.py:391
  59.1 26.1 %collective-permute-start.18 = (bf16[640,256]{1,0:T(8,128)(2,1)S(1)}, bf16[640,256]{1,0:T(8,128)(2,1)S(1)}, u32[]{:S(2)}, u32[]{:S(2)}) collective-permute-start(bf16[640,256]{1,0:T(8,128)(2,1)S(1)} %constant_dynamic-update-slice_fusion.18), channel_id=1, source_target_pairs={{0,4},{1,3},{2,6},{3,1},{4,0},{5,7},{6,2},{7,5},{8,12},{9,11},{10,... | collective-permute-start | bytes 983048 | tf_op jit(solution)/shard_map/ppermute | solution.py:391
  67.1 11.9 %collective-permute-start.16 = (bf16[1024,128]{1,0:T(8,128)(2,1)S(1)}, bf16[1024,128]{1,0:T(8,128)(2,1)S(1)}, u32[]{:S(2)}, u32[]{:S(2)}) collective-permute-start(bf16[1024,128]{1,0:T(8,128)(2,1)S(1)} %get-tuple-element.118.mine_ref), channel_id=1, source_target_pairs={{0,1},{1,0},{2,3},{3,2},{4,5},{5,4},{6,7},{7,6},{8,9},{9,8},{10,11... | collective-permute-start | bytes 786440 | tf_op jit(solution)/shard_map/ppermute | solution.py:391
  85.3 10.7 %collective-permute-start.20 = (bf16[1280,256]{1,0:T(8,128)(2,1)S(1)}, bf16[1280,256]{1,0:T(8,128)(2,1)S(1)}, u32[]{:S(2)}, u32[]{:S(2)}) collective-permute-start(bf16[1280,256]{1,0:T(8,128)(2,1)S(1)} %constant_dynamic-update-slice_fusion.22.low), channel_id=1, source_target_pairs={{0,8},{1,5},{2,10},{3,7},{4,12},{5,1},{6,14},{7,3},{8,0},{9,13},{1... | collective-permute-start | bytes 1966088 | tf_op jit(solution)/shard_map/ppermute | solution.py:391
  85.5 6.7 %collective-permute-start.17 = (bf16[144,512]{1,0:T(8,128)(2,1)S(1)}, bf16[144,512]{1,0:T(8,128)(2,1)S(1)}, u32[]{:S(2)}, u32[]{:S(2)}) collective-permute-start(bf16[144,512]{1,0:T(8,128)(2,1)S(1)} %get-tuple-element.124), channel_id=1, source_target_pairs={{0,2},{1,3},{2,0},{3,1},{4,6},{5,7},{6,4},{7,5},{8,10},{9,11},{10,... | collective-permute-start | bytes 442376 | tf_op jit(solution)/shard_map/ppermute | solution.py:391
  99.7 6.8 %collective-permute-start.21 = (bf16[144,768]{1,0:T(8,128)(2,1)S(1)}, bf16[144,768]{1,0:T(8,128)(2,1)S(1)}, u32[]{:S(2)}, u32[]{:S(2)}) collective-permute-start(bf16[144,768]{1,0:T(8,128)(2,1)S(1)} %get-tuple-element.135), channel_id=1, source_target_pairs={{0,2},{1,3},{2,0},{3,1},{4,6},{5,7},{6,4},{7,5},{8,10},{9,11},{10,... | collective-permute-start | bytes 663560 | tf_op jit(solution)/shard_map/ppermute | solution.py:391
  108.3 12.0 %collective-permute-start.26 = (f32[512,768]{1,0:T(8,128)S(1)}, f32[512,768]{1,0:T(8,128)S(1)}, u32[]{:S(2)}, u32[]{:S(2)}) collective-permute-start(f32[512,768]{1,0:T(8,128)S(1)} %get-tuple-element.152), channel_id=1, source_target_pairs={{0,1},{1,0},{2,3},{3,2},{4,5},{5,4},{6,7},{7,6},{8,9},{9,8},{10,11... | collective-permute-start | bytes 4718600 | tf_op jit(solution)/shard_map/ppermute | solution.py:391
  109.7 10.6 %collective-permute-start.25 = (f32[512,512]{1,0:T(8,128)S(1)}, f32[512,512]{1,0:T(8,128)S(1)}, u32[]{:S(2)}, u32[]{:S(2)}) collective-permute-start(f32[512,512]{1,0:T(8,128)S(1)} %get-tuple-element.151), channel_id=1, source_target_pairs={{0,1},{1,0},{2,3},{3,2},{4,5},{5,4},{6,7},{7,6},{8,9},{9,8},{10,11... | collective-permute-start | bytes 3145736 | tf_op jit(solution)/shard_map/ppermute | solution.py:391
  109.8 8.0 %collective-permute-start.24 = (bf16[2,256,128]{2,1,0:T(8,128)(2,1)S(1)}, bf16[2,256,128]{2,1,0:T(8,128)(2,1)S(1)}, u32[]{:S(2)}, u32[]{:S(2)}) collective-permute-start(bf16[2,256,128]{2,1,0:T(8,128)(2,1)S(1)} %pad_maximum_fusion.2), channel_id=1, source_target_pairs={{0,8},{1,9},{2,10},{3,11},{4,12},{5,13},{6,14},{7,15},{8,0},{9,1},... | collective-permute-start | bytes 393224 | tf_op jit(solution)/shard_map/ppermute | solution.py:391
  110.0 8.3 %collective-permute-start.23 = (bf16[384,128]{1,0:T(8,128)(2,1)S(1)}, bf16[384,128]{1,0:T(8,128)(2,1)S(1)}, u32[]{:S(2)}, u32[]{:S(2)}) collective-permute-start(bf16[384,128]{1,0:T(8,128)(2,1)S(1)} %get-tuple-element.146.here), channel_id=1, source_target_pairs={{0,16},{1,17},{2,18},{3,19},{4,20},{5,21},{6,22},{7,23},{8,24},{9,... | collective-permute-start | bytes 294920 | tf_op jit(solution)/shard_map/ppermute | solution.py:391
  (16 other events, 298.5 us)

commit v7 on v6

--- a/solution.py
+++ b/solution.py
@@ -21,7 +21,7 @@
 PAIRS = ((0,), (1, 2, 3), (4, 5, 6, 7), (8, 9))
 CUT = 2
 SCHEDULE = (
-    "0.0", "1.0", "tokens", "0.1", "2.0", "1.1", "0.2", "halo", "settings", "3.0",
+    "0.0", "1.0", "settings", "tokens", "0.1", "2.0", "1.1", "0.2", "halo", "3.0",
     "2.1", "1.2", "0.3", "own", "3.1", "2.2", "1.3", "3.2", "2.3", "K0",
     "K1", "xA", "3.3", "K2", "JA", "fA0", "K3", "xB", "fA1", "JB",
     "fB0", "fA2", "fB1", "norm", "fA3", "fB2", "fB3",
@@ -554,6 +554,7 @@
         )(place, v["ints"], *arrays)
 
     v = state
+    v["token"] = blocks[0]
     last = len(PAIRS) - 1
     for event in SCHEDULE:
         if event[0].isdigit():

time: 132 us -> 128 us (0.970)
  waiting for transfers between devices: 38.9 us -> 28.6 us
  starting transfers between devices: 43.4 us -> 51.7 us
    ppermute x29, waiting for transfers between devices: 38.9 us -> 28.6 us  [swapped(): return lax.ppermute(x, AXES, [(i, i ^ masks[i % 2]) for i in range(count)])]
    ppermute x29, starting transfers between devices: 39.3 us -> 49.2 us  [swapped(): return lax.ppermute(x, AXES, [(i, i ^ masks[i % 2]) for i in range(count)])]
    concatenate x12, local copies, waits for them, and re-layouts: 6.71 us -> 3.34 us  [on_device(): blocks[i] = jnp.concatenate(after(blocks[i], arrived[i]), axis=0)]
    ppermute x1, starting transfers between devices: 4.01 us -> 2.44 us  [on_device(): v['halo'] = lax.ppermute(edge, AXES, route)]
    unnamed x33 -> x25, local copies, waits for them, and re-layouts: 3.9 us -> 4.08 us
  transfers between devices with their start and end apart: 30 -> 30, of which waited for: 13 -> 11; matrix products, arithmetic and copies ran while one was open for 9% -> 7% of each run, Pallas kernels for 19% -> 20%
where the time goes in v7:
time: 128 us
  starting transfers between devices  51.7 us (40%)
  Pallas kernels  34.2 us (27%)
  waiting for transfers between devices  28.6 us (22%)
  local copies, waits for them, and re-layouts  10.5 us (8%)
  other arithmetic  1.77 us (1%)
    ppermute x29, starting transfers between devices, swapped(): return lax.ppermute(x, AXES, [(i, i ^ masks[i % 2]) for i in range(count)])  49.2 us
    ppermute x29, waiting for transfers between devices, swapped(): return lax.ppermute(x, AXES, [(i, i ^ masks[i % 2]) for i in range(count)])  28.6 us
    pallas_call x3, Pallas kernels, scanned(): pl.pallas_call(functools.partial(scan_kernel, index, held, firsts, more),...  16.9 us
    pallas_call x1, Pallas kernels, projected(): pl.pallas_call(first_kernel, in_specs=[SMEM] + [VMEM] * 6, out_specs=[VME...  5.37 us
    unnamed x25, local copies, waits for them, and re-layouts  4.08 us
    concatenate x12, local copies, waits for them, and re-layouts, on_device(): blocks[i] = jnp.concatenate(after(blocks[i], arrived[i]), axis=0)  3.34 us
    pallas_call x2, Pallas kernels, joined(): pl.pallas_call(functools.partial(join_kernel, [first_head(p, share) for p...  3.15 us
    pallas_call x4, Pallas kernels, picked(): pl.pallas_call(kernel, in_specs=[SMEM] * 2 + [VMEM] * len(arrays), out_sp...  3.1 us
  transfers between devices with their start and end apart: 30, of which 11 were waited for; matrix products, arithmetic and copies ran while one was open for 7% of the time, Pallas kernels for 20%

profile of v7, /device:TPU:0, one launch (start us, length us, event | category | flops | bytes accessed | tf_op | source)
XLA Modules:
  0.0 127.8 jit_solution(10705751788297905615)
XLA Ops:
  6.0 3.7 %collective-permute-start.2 = (bf16[160,384]{1,0:T(8,128)(2,1)S(1)}, bf16[160,384]{1,0:T(8,128)(2,1)}, u32[]{:S(2)}, u32[]{:S(2)}) collective-permute-start(bf16[160,384]{1,0:T(8,128)(2,1)S(1)} %get-tuple-element.92), channel_id=1, source_target_pairs={{0,16},{1,17},{2,18},{3,19},{4,20},{5,21},{6,22},{7,23},{8,24},{9,... | collective-permute-start | bytes 368648 | tf_op jit(solution)/shard_map/ppermute | solution.py:391
  17.8 1.9 %collective-permute-start.3 = (bf16[320,384]{1,0:T(8,128)(2,1)S(1)}, bf16[320,384]{1,0:T(8,128)(2,1)}, u32[]{:S(2)}, u32[]{:S(2)}) collective-permute-start(bf16[320,384]{1,0:T(8,128)(2,1)S(1)} %constant_dynamic-update-slice_fusion), channel_id=1, source_target_pairs={{0,2},{1,9},{2,0},{3,11},{4,6},{5,13},{6,4},{7,15},{8,10},{9,1},{1... | collective-permute-start | bytes 737288 | tf_op jit(solution)/shard_map/ppermute | solution.py:391
  19.7 2.6 %collective-permute-start.8 = (bf16[160,512]{1,0:T(8,128)(2,1)S(1)}, bf16[160,512]{1,0:T(8,128)(2,1)S(1)}, u32[]{:S(2)}, u32[]{:S(2)}) collective-permute-start(bf16[160,512]{1,0:T(8,128)(2,1)S(1)} %get-tuple-element.101), channel_id=1, source_target_pairs={{0,16},{1,17},{2,18},{3,19},{4,20},{5,21},{6,22},{7,23},{8,24},{9,... | collective-permute-start | bytes 491528 | tf_op jit(solution)/shard_map/ppermute | solution.py:391
  23.7 3.1 %collective-permute-start.7 = (bf16[320,384]{1,0:T(8,128)(2,1)S(1)}, bf16[320,384]{1,0:T(8,128)(2,1)S(1)}, u32[]{:S(2)}, u32[]{:S(2)}) collective-permute-start(bf16[320,384]{1,0:T(8,128)(2,1)S(1)} %constant_dynamic-update-slice_fusion.2), channel_id=1, source_target_pairs={{0,8},{1,3},{2,10},{3,1},{4,12},{5,7},{6,14},{7,5},{8,0},{9,11},{1... | collective-permute-start | bytes 737288 | tf_op jit(solution)/shard_map/ppermute | solution.py:391
  30.3 2.4 %collective-permute-start.5 = (bf16[16,2560]{1,0:T(8,128)(2,1)S(1)}, bf16[16,2560]{1,0:T(8,128)(2,1)S(1)}, u32[]{:S(2)}, u32[]{:S(2)}) collective-permute-start(bf16[16,2560]{1,0:T(8,128)(2,1)S(1)} %bitcast_select_fusion), channel_id=1, source_target_pairs={{0,2},{1,3},{4,6},{5,7},{8,10},{9,11},{12,14},{13,15},{16,18},{17,... | collective-permute-start | bytes 245768 | tf_op jit(solution)/shard_map/ppermute | solution.py:576
  35.1 1.7 %collective-permute-done.6 = bf16[640,384]{1,0:T(8,128)(2,1)S(1)} collective-permute-done((bf16[640,384]{1,0:T(8,128)(2,1)S(1)}, bf16[640,384]{1,0:T(8,128)(2,1)S(1)}, u32[]{:S(2)}, u32[]{:S(2)}) %collective-permute-start.6) | collective-permute-done | bytes 491552 | tf_op jit(solution)/shard_map/ppermute | solution.py:391
  37.1 3.1 %collective-permute-done.10 = bf16[320,512]{1,0:T(8,128)(2,1)S(1)} collective-permute-done((bf16[320,512]{1,0:T(8,128)(2,1)S(1)}, bf16[320,512]{1,0:T(8,128)(2,1)S(1)}, u32[]{:S(2)}, u32[]{:S(2)}) %collective-permute-start.10) | collective-permute-done | bytes 327712 | tf_op jit(solution)/shard_map/ppermute | solution.py:391
  43.2 4.8 %collective-permute-done.9 = bf16[640,384]{1,0:T(8,128)(2,1)S(1)} collective-permute-done((bf16[640,384]{1,0:T(8,128)(2,1)S(1)}, bf16[640,384]{1,0:T(8,128)(2,1)S(1)}, u32[]{:S(2)}, u32[]{:S(2)}) %collective-permute-start.9) | collective-permute-done | bytes 491552 | tf_op jit(solution)/shard_map/ppermute | solution.py:391
  48.4 4.3 %collective-permute-done.14 = bf16[320,256]{1,0:T(8,128)(2,1)S(1)} collective-permute-done((bf16[320,256]{1,0:T(8,128)(2,1)S(1)}, bf16[320,256]{1,0:T(8,128)(2,1)S(1)}, u32[]{:S(2)}, u32[]{:S(2)}) %collective-permute-start.14) | collective-permute-done | bytes 163872 | tf_op jit(solution)/shard_map/ppermute | solution.py:391
  55.2 2.5 %collective-permute-done.15.high = bf16[1280,384]{1,0:T(8,128)(2,1)S(1)} collective-permute-done((bf16[1280,384]{1,0:T(8,128)(2,1)S(1)}, bf16[1280,384]{1,0:T(8,128)(2,1)S(1)}, u32[]{:S(2)}, u32[]{:S(2)}) %collective-permute-start.15) | collective-permute-done | bytes 983072 | tf_op jit(solution)/shard_map/ppermute | solution.py:391
  57.7 5.4 %first.1 = (bf16[1024,128]{1,0:T(8,128)(2,1)S(1)}, bf16[1024,128]{1,0:T(8,128)(2,1)S(1)}, f32[1024,128]{1,0:T(8,128)S(1)}, f32[4,32,256]{2,1,0:T(8,128)S(1)}, f32[8,128]{1,0:T(8,128)S(1)}) custom-call(s32[8]{0:T(128)S(1)} %get-tuple-element.152.ints, bf16[528,2560]{1,0:T(8,128)(2,1)S(1)} %pad_maximum_fusion.own, ...), custom_call_target="tpu_custom_call" | custom-call | flops 1000 | bytes 1000 | tf_op jit(solution)/shard_map/first/pallas_call | solution.py:457
  63.1 9.0 %collective-permute-start.16 = (bf16[1024,128]{1,0:T(8,128)(2,1)S(1)}, bf16[1024,128]{1,0:T(8,128)(2,1)S(1)}, u32[]{:S(2)}, u32[]{:S(2)}) collective-permute-start(bf16[1024,128]{1,0:T(8,128)(2,1)S(1)} %get-tuple-element.122.mine_ref), channel_id=1, source_target_pairs={{0,1},{1,0},{2,3},{3,2},{4,5},{5,4},{6,7},{7,6},{8,9},{9,8},{10,11... | collective-permute-start | bytes 786440 | tf_op jit(solution)/shard_map/ppermute | solution.py:391
  73.3 6.3 %scan.3 = (f32[1024,512]{1,0:T(8,128)S(1)}, f32[128,512]{1,0:T(8,128)S(1)}, bf16[144,512]{1,0:T(8,128)(2,1)S(1)}) custom-call(s32[8]{0:T(128)S(1)} %get-tuple-element.152.ints, bf16[528,2560]{1,0:T(8,128)(2,1)S(1)} %pad_maximum_fusion.own, bf16[512,2560]{1,0:T(8,128)(2,1)S(1)} %collective-permute-done.1.other, ...), custom_call_target="tpu_custom_call" | custom-call | flops 1000 | bytes 1000 | tf_op jit(solution)/shard_map/scan/pallas_call | solution.py:481
  81.9 6.8 %scan.4 = (f32[1024,512]{1,0:T(8,128)S(1)}, f32[128,512]{1,0:T(8,128)S(1)}, bf16[144,512]{1,0:T(8,128)(2,1)S(1)}) custom-call(s32[8]{0:T(128)S(1)} %get-tuple-element.152.ints, bf16[528,2560]{1,0:T(8,128)(2,1)S(1)} %pad_maximum_fusion.own, bf16[512,2560]{1,0:T(8,128)(2,1)S(1)} %collective-permute-done.1.other, ...), custom_call_target="tpu_custom_call" | custom-call | flops 1000 | bytes 1000 | tf_op jit(solution)/shard_map/scan/pallas_call | solution.py:481
  90.3 3.9 %scan.5 = (f32[1024,256]{1,0:T(8,128)S(1)}, f32[128,256]{1,0:T(8,128)S(1)}, bf16[144,768]{1,0:T(8,128)(2,1)S(1)}) custom-call(s32[8]{0:T(128)S(1)} %get-tuple-element.152.ints, bf16[528,2560]{1,0:T(8,128)(2,1)S(1)} %pad_maximum_fusion.own, bf16[512,2560]{1,0:T(8,128)(2,1)S(1)} %collective-permute-done.1.other, ...), custom_call_target="tpu_custom_call" | custom-call | flops 1000 | bytes 1000 | tf_op jit(solution)/shard_map/scan/pallas_call | solution.py:481
  94.8 4.7 %collective-permute-start.22 = (bf16[256,128]{1,0:T(8,128)(2,1)S(1)}, bf16[256,128]{1,0:T(8,128)(2,1)S(1)}, u32[]{:S(2)}, u32[]{:S(2)}) collective-permute-start(bf16[256,128]{1,0:T(8,128)(2,1)S(1)} %get-tuple-element.140.here), channel_id=1, source_target_pairs={{0,16},{1,17},{2,18},{3,19},{4,20},{5,21},{6,22},{7,23},{8,24},{9,... | collective-permute-start | bytes 196616 | tf_op jit(solution)/shard_map/ppermute | solution.py:391
  99.5 2.9 %collective-permute-done.22.one = bf16[256,128]{1,0:T(8,128)(2,1)S(1)} collective-permute-done((bf16[256,128]{1,0:T(8,128)(2,1)S(1)}, bf16[256,128]{1,0:T(8,128)(2,1)S(1)}, u32[]{:S(2)}, u32[]{:S(2)}) %collective-permute-start.22) | collective-permute-done | bytes 65568 | tf_op jit(solution)/shard_map/ppermute | solution.py:391
  102.4 1.8 %join.3 = (f32[512,768]{1,0:T(8,128)S(1)}, f32[512,768]{1,0:T(8,128)S(1)}, bf16[384,128]{1,0:T(8,128)(2,1)S(1)}) custom-call(s32[8]{0:T(128)S(1)} %get-tuple-element.152.ints, bf16[1024,128]{1,0:T(8,128)(2,1)S(1)} %get-tuple-element.122.mine_ref, bf16[1024,128]{1,0:T(8,128)(2,1)S(1)} %collective-permute-done.16.their_ref, ...), custom_call_target="tpu_custom_call" | custom-call | flops 1000 | bytes 1000 | tf_op jit(solution)/shard_map/join/pallas_call | solution.py:505
  104.8 2.3 %collective-permute-start.24 = (bf16[2,256,128]{2,1,0:T(8,128)(2,1)S(1)}, bf16[2,256,128]{2,1,0:T(8,128)(2,1)S(1)}, u32[]{:S(2)}, u32[]{:S(2)}) collective-permute-start(bf16[2,256,128]{2,1,0:T(8,128)(2,1)S(1)} %pad_maximum_fusion.2), channel_id=1, source_target_pairs={{0,8},{1,9},{2,10},{3,11},{4,12},{5,13},{6,14},{7,15},{8,0},{9,1},... | collective-permute-start | bytes 393224 | tf_op jit(solution)/shard_map/ppermute | solution.py:391
  107.1 2.8 %collective-permute-start.23 = (bf16[384,128]{1,0:T(8,128)(2,1)S(1)}, bf16[384,128]{1,0:T(8,128)(2,1)S(1)}, u32[]{:S(2)}, u32[]{:S(2)}) collective-permute-start(bf16[384,128]{1,0:T(8,128)(2,1)S(1)} %get-tuple-element.150.here), channel_id=1, source_target_pairs={{0,16},{1,17},{2,18},{3,19},{4,20},{5,21},{6,22},{7,23},{8,24},{9,... | collective-permute-start | bytes 294920 | tf_op jit(solution)/shard_map/ppermute | solution.py:391
  109.9 3.4 %collective-permute-done.24.two = bf16[2,256,128]{2,1,0:T(8,128)(2,1)S(1)} collective-permute-done((bf16[2,256,128]{2,1,0:T(8,128)(2,1)S(1)}, bf16[2,256,128]{2,1,0:T(8,128)(2,1)S(1)}, u32[]{:S(2)}, u32[]{:S(2)}) %collective-permute-start.24) | collective-permute-done | bytes 131104 | tf_op jit(solution)/shard_map/ppermute | solution.py:391
  113.9 2.2 %collective-permute-start.27 = (bf16[2,384,128]{2,1,0:T(8,128)(2,1)S(1)}, bf16[2,384,128]{2,1,0:T(8,128)(2,1)S(1)}, u32[]{:S(2)}, u32[]{:S(2)}) collective-permute-start(bf16[2,384,128]{2,1,0:T(8,128)(2,1)S(1)} %pad_maximum_fusion.1), channel_id=1, source_target_pairs={{0,8},{1,9},{2,10},{3,11},{4,12},{5,13},{6,14},{7,15},{8,0},{9,1},... | collective-permute-start | bytes 589832 | tf_op jit(solution)/shard_map/ppermute | solution.py:391
  117.7 2.9 %norm.1 = bf16[512,2560]{1,0:T(8,128)(2,1)} custom-call(s32[8]{0:T(128)S(1)} %get-tuple-element.152.ints, f32[1,2560]{1,0:T(1,128)S(1)} %broadcast_in_dim.30.gain_ref, f32[512,512]{1,0:T(8,128)S(1)} %get-tuple-element.153.ka_ref, f32[512,768]{1,0:T(8,128)S(1)} %get-tuple-element.154.kb_ref, f32[512,512]{1,0:T(8,128)S(1)} %collective-permute-done.25.ra_ref, ...), custom_call_target="tpu_custom_call" | custom-call | flops 1000 | bytes 1000 | tf_op jit(solution)/shard_map/norm/pallas_call | solution.py:527
  123.2 3.2 %collective-permute-done.29.three = bf16[384,128]{1,0:T(8,128)(2,1)S(1)} collective-permute-done((bf16[384,128]{1,0:T(8,128)(2,1)S(1)}, bf16[384,128]{1,0:T(8,128)(2,1)S(1)}, u32[]{:S(2)}, u32[]{:S(2)}) %collective-permute-start.29) | collective-permute-done | bytes 98336 | tf_op jit(solution)/shard_map/ppermute | solution.py:391
  (104 shorter events, 39.1 us)
Async XLA Ops:
  5.6 23.9 %collective-permute-start.1 = (bf16[512,2560]{1,0:T(8,128)(2,1)}, bf16[512,2560]{1,0:T(8,128)(2,1)S(1)}, u32[]{:S(2)}, u32[]{:S(2)}) collective-permute-start(bf16[512,2560]{1,0:T(8,128)(2,1)} %bitcast.18), channel_id=1, source_target_pairs={{0,1},{1,0},{2,3},{3,2},{4,5},{5,4},{6,7},{7,6},{8,9},{9,8},{10,11... | collective-permute-start | bytes 7864328 | tf_op jit(solution)/shard_map/ppermute | solution.py:391
  6.0 10.9 %collective-permute-start.2 = (bf16[160,384]{1,0:T(8,128)(2,1)S(1)}, bf16[160,384]{1,0:T(8,128)(2,1)}, u32[]{:S(2)}, u32[]{:S(2)}) collective-permute-start(bf16[160,384]{1,0:T(8,128)(2,1)S(1)} %get-tuple-element.92), channel_id=1, source_target_pairs={{0,16},{1,17},{2,18},{3,19},{4,20},{5,21},{6,22},{7,23},{8,24},{9,... | collective-permute-start | bytes 368648 | tf_op jit(solution)/shard_map/ppermute | solution.py:391
  12.5 10.1 %collective-permute-start.4 = (bf16[160,384]{1,0:T(8,128)(2,1)S(1)}, bf16[160,384]{1,0:T(8,128)(2,1)}, u32[]{:S(2)}, u32[]{:S(2)}) collective-permute-start(bf16[160,384]{1,0:T(8,128)(2,1)S(1)} %get-tuple-element.95), channel_id=1, source_target_pairs={{0,16},{1,17},{2,18},{3,19},{4,20},{5,21},{6,22},{7,23},{8,24},{9,... | collective-permute-start | bytes 368648 | tf_op jit(solution)/shard_map/ppermute | solution.py:391
  17.8 9.0 %collective-permute-start.3 = (bf16[320,384]{1,0:T(8,128)(2,1)S(1)}, bf16[320,384]{1,0:T(8,128)(2,1)}, u32[]{:S(2)}, u32[]{:S(2)}) collective-permute-start(bf16[320,384]{1,0:T(8,128)(2,1)S(1)} %constant_dynamic-update-slice_fusion), channel_id=1, source_target_pairs={{0,2},{1,9},{2,0},{3,11},{4,6},{5,13},{6,4},{7,15},{8,10},{9,1},{1... | collective-permute-start | bytes 737288 | tf_op jit(solution)/shard_map/ppermute | solution.py:391
  19.7 13.1 %collective-permute-start.8 = (bf16[160,512]{1,0:T(8,128)(2,1)S(1)}, bf16[160,512]{1,0:T(8,128)(2,1)S(1)}, u32[]{:S(2)}, u32[]{:S(2)}) collective-permute-start(bf16[160,512]{1,0:T(8,128)(2,1)S(1)} %get-tuple-element.101), channel_id=1, source_target_pairs={{0,16},{1,17},{2,18},{3,19},{4,20},{5,21},{6,22},{7,23},{8,24},{9,... | collective-permute-start | bytes 491528 | tf_op jit(solution)/shard_map/ppermute | solution.py:391
  22.3 14.8 %collective-permute-start.11 = (bf16[160,256]{1,0:T(8,128)(2,1)S(1)}, bf16[160,256]{1,0:T(8,128)(2,1)S(1)}, u32[]{:S(2)}, u32[]{:S(2)}) collective-permute-start(bf16[160,256]{1,0:T(8,128)(2,1)S(1)} %get-tuple-element.109), channel_id=1, source_target_pairs={{0,16},{1,17},{2,18},{3,19},{4,20},{5,21},{6,22},{7,23},{8,24},{9,... | collective-permute-start | bytes 245768 | tf_op jit(solution)/shard_map/ppermute | solution.py:391
  23.7 10.0 %collective-permute-start.7 = (bf16[320,384]{1,0:T(8,128)(2,1)S(1)}, bf16[320,384]{1,0:T(8,128)(2,1)S(1)}, u32[]{:S(2)}, u32[]{:S(2)}) collective-permute-start(bf16[320,384]{1,0:T(8,128)(2,1)S(1)} %constant_dynamic-update-slice_fusion.2), channel_id=1, source_target_pairs={{0,8},{1,3},{2,10},{3,1},{4,12},{5,7},{6,14},{7,5},{8,0},{9,11},{1... | collective-permute-start | bytes 737288 | tf_op jit(solution)/shard_map/ppermute | solution.py:391
  27.8 8.9 %collective-permute-start.6 = (bf16[640,384]{1,0:T(8,128)(2,1)S(1)}, bf16[640,384]{1,0:T(8,128)(2,1)S(1)}, u32[]{:S(2)}, u32[]{:S(2)}) collective-permute-start(bf16[640,384]{1,0:T(8,128)(2,1)S(1)} %constant_dynamic-update-slice_fusion.4), channel_id=1, source_target_pairs={{0,4},{1,3},{2,6},{3,1},{4,0},{5,7},{6,2},{7,5},{8,12},{9,11},{10,... | collective-permute-start | bytes 1474568 | tf_op jit(solution)/shard_map/ppermute | solution.py:391
  32.8 7.4 %collective-permute-start.10 = (bf16[320,512]{1,0:T(8,128)(2,1)S(1)}, bf16[320,512]{1,0:T(8,128)(2,1)S(1)}, u32[]{:S(2)}, u32[]{:S(2)}) collective-permute-start(bf16[320,512]{1,0:T(8,128)(2,1)S(1)} %constant_dynamic-update-slice_fusion.6), channel_id=1, source_target_pairs={{0,4},{1,9},{2,6},{3,11},{4,0},{5,13},{6,2},{7,15},{8,12},{9,1},{1... | collective-permute-start | bytes 983048 | tf_op jit(solution)/shard_map/ppermute | solution.py:391
  33.8 14.1 %collective-permute-start.9 = (bf16[640,384]{1,0:T(8,128)(2,1)S(1)}, bf16[640,384]{1,0:T(8,128)(2,1)S(1)}, u32[]{:S(2)}, u32[]{:S(2)}) collective-permute-start(bf16[640,384]{1,0:T(8,128)(2,1)S(1)} %constant_dynamic-update-slice_fusion.8), channel_id=1, source_target_pairs={{0,4},{1,9},{2,6},{3,11},{4,0},{5,13},{6,2},{7,15},{8,12},{9,1},{1... | collective-permute-start | bytes 1474568 | tf_op jit(solution)/shard_map/ppermute | solution.py:391
  40.3 12.4 %collective-permute-start.13 = (bf16[640,512]{1,0:T(8,128)(2,1)S(1)}, bf16[640,512]{1,0:T(8,128)(2,1)S(1)}, u32[]{:S(2)}, u32[]{:S(2)}) collective-permute-start(bf16[640,512]{1,0:T(8,128)(2,1)S(1)} %constant_dynamic-update-slice_fusion.14), channel_id=1, source_target_pairs={{0,2},{1,5},{2,0},{3,7},{4,6},{5,1},{6,4},{7,3},{8,10},{9,13},{10,... | collective-permute-start | bytes 1966088 | tf_op jit(solution)/shard_map/ppermute | solution.py:391
  40.9 16.8 %collective-permute-start.15 = (bf16[1280,384]{1,0:T(8,128)(2,1)S(1)}, bf16[1280,384]{1,0:T(8,128)(2,1)S(1)}, u32[]{:S(2)}, u32[]{:S(2)}) collective-permute-start(bf16[1280,384]{1,0:T(8,128)(2,1)S(1)} %constant_dynamic-update-slice_fusion.10.low), channel_id=1, source_target_pairs={{0,8},{1,5},{2,10},{3,7},{4,12},{5,1},{6,14},{7,3},{8,0},{9,13},{1... | collective-permute-start | bytes 2949128 | tf_op jit(solution)/shard_map/ppermute | solution.py:391
  42.5 10.2 %collective-permute-start.14 = (bf16[320,256]{1,0:T(8,128)(2,1)S(1)}, bf16[320,256]{1,0:T(8,128)(2,1)S(1)}, u32[]{:S(2)}, u32[]{:S(2)}) collective-permute-start(bf16[320,256]{1,0:T(8,128)(2,1)S(1)} %constant_dynamic-update-slice_fusion.12), channel_id=1, source_target_pairs={{0,2},{1,9},{2,0},{3,11},{4,6},{5,13},{6,4},{7,15},{8,10},{9,1},{1... | collective-permute-start | bytes 491528 | tf_op jit(solution)/shard_map/ppermute | solution.py:391
  48.1 25.2 %collective-permute-start.12 = (bf16[1280,384]{1,0:T(8,128)(2,1)S(1)}, bf16[1280,384]{1,0:T(8,128)(2,1)S(1)}, u32[]{:S(2)}, u32[]{:S(2)}) collective-permute-start(bf16[1280,384]{1,0:T(8,128)(2,1)S(1)} %constant_dynamic-update-slice_fusion.16.low), channel_id=1, source_target_pairs={{0,2},{1,5},{2,0},{3,7},{4,6},{5,1},{6,4},{7,3},{8,10},{9,13},{10,... | collective-permute-start | bytes 2949128 | tf_op jit(solution)/shard_map/ppermute | solution.py:391
  52.8 29.0 %collective-permute-start.19 = (bf16[1280,512]{1,0:T(8,128)(2,1)S(1)}, bf16[1280,512]{1,0:T(8,128)(2,1)S(1)}, u32[]{:S(2)}, u32[]{:S(2)}) collective-permute-start(bf16[1280,512]{1,0:T(8,128)(2,1)S(1)} %constant_dynamic-update-slice_fusion.20.low), channel_id=1, source_target_pairs={{0,8},{1,3},{2,10},{3,1},{4,12},{5,7},{6,14},{7,5},{8,0},{9,11},{1... | collective-permute-start | bytes 3932168 | tf_op jit(solution)/shard_map/ppermute | solution.py:391
  53.7 25.9 %collective-permute-start.18 = (bf16[640,256]{1,0:T(8,128)(2,1)S(1)}, bf16[640,256]{1,0:T(8,128)(2,1)S(1)}, u32[]{:S(2)}, u32[]{:S(2)}) collective-permute-start(bf16[640,256]{1,0:T(8,128)(2,1)S(1)} %constant_dynamic-update-slice_fusion.18), channel_id=1, source_target_pairs={{0,4},{1,3},{2,6},{3,1},{4,0},{5,7},{6,2},{7,5},{8,12},{9,11},{10,... | collective-permute-start | bytes 983048 | tf_op jit(solution)/shard_map/ppermute | solution.py:391
  63.1 10.2 %collective-permute-start.16 = (bf16[1024,128]{1,0:T(8,128)(2,1)S(1)}, bf16[1024,128]{1,0:T(8,128)(2,1)S(1)}, u32[]{:S(2)}, u32[]{:S(2)}) collective-permute-start(bf16[1024,128]{1,0:T(8,128)(2,1)S(1)} %get-tuple-element.122.mine_ref), channel_id=1, source_target_pairs={{0,1},{1,0},{2,3},{3,2},{4,5},{5,4},{6,7},{7,6},{8,9},{9,8},{10,11... | collective-permute-start | bytes 786440 | tf_op jit(solution)/shard_map/ppermute | solution.py:391
  79.7 10.7 %collective-permute-start.20 = (bf16[1280,256]{1,0:T(8,128)(2,1)S(1)}, bf16[1280,256]{1,0:T(8,128)(2,1)S(1)}, u32[]{:S(2)}, u32[]{:S(2)}) collective-permute-start(bf16[1280,256]{1,0:T(8,128)(2,1)S(1)} %constant_dynamic-update-slice_fusion.22.low), channel_id=1, source_target_pairs={{0,8},{1,5},{2,10},{3,7},{4,12},{5,1},{6,14},{7,3},{8,0},{9,13},{1... | collective-permute-start | bytes 1966088 | tf_op jit(solution)/shard_map/ppermute | solution.py:391
  80.6 8.1 %collective-permute-start.17 = (bf16[144,512]{1,0:T(8,128)(2,1)S(1)}, bf16[144,512]{1,0:T(8,128)(2,1)S(1)}, u32[]{:S(2)}, u32[]{:S(2)}) collective-permute-start(bf16[144,512]{1,0:T(8,128)(2,1)S(1)} %get-tuple-element.128), channel_id=1, source_target_pairs={{0,2},{1,3},{2,0},{3,1},{4,6},{5,7},{6,4},{7,5},{8,10},{9,11},{10,... | collective-permute-start | bytes 442376 | tf_op jit(solution)/shard_map/ppermute | solution.py:391
  94.2 8.2 %collective-permute-start.21 = (bf16[144,768]{1,0:T(8,128)(2,1)S(1)}, bf16[144,768]{1,0:T(8,128)(2,1)S(1)}, u32[]{:S(2)}, u32[]{:S(2)}) collective-permute-start(bf16[144,768]{1,0:T(8,128)(2,1)S(1)} %get-tuple-element.139), channel_id=1, source_target_pairs={{0,2},{1,3},{2,0},{3,1},{4,6},{5,7},{6,4},{7,5},{8,10},{9,11},{10,... | collective-permute-start | bytes 663560 | tf_op jit(solution)/shard_map/ppermute | solution.py:391
  94.8 7.6 %collective-permute-start.22 = (bf16[256,128]{1,0:T(8,128)(2,1)S(1)}, bf16[256,128]{1,0:T(8,128)(2,1)S(1)}, u32[]{:S(2)}, u32[]{:S(2)}) collective-permute-start(bf16[256,128]{1,0:T(8,128)(2,1)S(1)} %get-tuple-element.140.here), channel_id=1, source_target_pairs={{0,16},{1,17},{2,18},{3,19},{4,20},{5,21},{6,22},{7,23},{8,24},{9,... | collective-permute-start | bytes 196616 | tf_op jit(solution)/shard_map/ppermute | solution.py:391
  104.2 13.5 %collective-permute-start.26 = (f32[512,768]{1,0:T(8,128)S(1)}, f32[512,768]{1,0:T(8,128)S(1)}, u32[]{:S(2)}, u32[]{:S(2)}) collective-permute-start(f32[512,768]{1,0:T(8,128)S(1)} %get-tuple-element.156), channel_id=1, source_target_pairs={{0,1},{1,0},{2,3},{3,2},{4,5},{5,4},{6,7},{7,6},{8,9},{9,8},{10,11... | collective-permute-start | bytes 4718600 | tf_op jit(solution)/shard_map/ppermute | solution.py:391
  104.7 13.0 %collective-permute-start.25 = (f32[512,512]{1,0:T(8,128)S(1)}, f32[512,512]{1,0:T(8,128)S(1)}, u32[]{:S(2)}, u32[]{:S(2)}) collective-permute-start(f32[512,512]{1,0:T(8,128)S(1)} %get-tuple-element.155), channel_id=1, source_target_pairs={{0,1},{1,0},{2,3},{3,2},{4,5},{5,4},{6,7},{7,6},{8,9},{9,8},{10,11... | collective-permute-start | bytes 3145736 | tf_op jit(solution)/shard_map/ppermute | solution.py:391
  104.8 8.5 %collective-permute-start.24 = (bf16[2,256,128]{2,1,0:T(8,128)(2,1)S(1)}, bf16[2,256,128]{2,1,0:T(8,128)(2,1)S(1)}, u32[]{:S(2)}, u32[]{:S(2)}) collective-permute-start(bf16[2,256,128]{2,1,0:T(8,128)(2,1)S(1)} %pad_maximum_fusion.2), channel_id=1, source_target_pairs={{0,8},{1,9},{2,10},{3,11},{4,12},{5,13},{6,14},{7,15},{8,0},{9,1},... | collective-permute-start | bytes 393224 | tf_op jit(solution)/shard_map/ppermute | solution.py:391
  (12 other events, 64.2 us)
